TPU v7x, 32 devices: a whole 2x2x4 slice. The times are simulated.
32 devices in a mesh: dp: 4 (over z), fsdp: 8 (over y, x, core).
Axes of the slice: x: 2, y: 2, z: 4, core: 2. Of those that a mesh axis runs over, the one named last changes fastest.
Arguments:
- pixels: float32 [24576, 768], P(('dp', 'fsdp')), may hold values from 0 to 2
- masked: int32 [24576], P(('dp', 'fsdp')), may hold values from 0 to 1, as said below
- valid: int32 [24576], P(('dp', 'fsdp')), may hold values from 0 to 1, as said below
- scene_ids: int32 [24576], P(('dp', 'fsdp')), may hold values from 0 to 63, as said below
- gsd_index: int32 [64], P(('dp', 'fsdp')), may hold values from 0 to 7
- coords: int32 [24576, 2], P(('dp', 'fsdp')), may hold values from 0 to 31
- embed: float32 [768, 1024], P('fsdp'), may hold values from -0.21875 to 0.21875
- wide_enc: float32 [1024, 8704], P('fsdp'), may hold values from -0.1875 to 0.1875
- enc_down: float32 [4096, 1024], P('fsdp'), may hold values from -0.09375 to 0.09375
- wide_dec: float32 [512, 5056], P('fsdp'), may hold values from -0.25 to 0.25
- dec_down: float32 [2048, 512], P('fsdp'), may hold values from -0.125 to 0.125
- vectors: float32 [5120], replicated, may hold values from 0.5 to 1.5
- embed_mom: float32 [768, 1024], P('fsdp'), may hold values from -0.01171875 to 0.01171875
- wide_enc_mom: float32 [1024, 8704], P('fsdp'), may hold values from -0.01171875 to 0.01171875
- enc_down_mom: float32 [4096, 1024], P('fsdp'), may hold values from -0.01171875 to 0.01171875
- wide_dec_mom: float32 [512, 5056], P('fsdp'), may hold values from -0.01171875 to 0.01171875
- dec_down_mom: float32 [2048, 512], P('fsdp'), may hold values from -0.01171875 to 0.01171875
- vector_mom: float32 [5120], replicated, may hold values from -0.0390625 to 0.0390625
- embed_avg: float32 [768, 1024], P('fsdp'), may hold values from -0.21875 to 0.21875
- wide_enc_avg: float32 [1024, 8704], P('fsdp'), may hold values from -0.1875 to 0.1875
- enc_down_avg: float32 [4096, 1024], P('fsdp'), may hold values from -0.09375 to 0.09375
- wide_dec_avg: float32 [512, 5056], P('fsdp'), may hold values from -0.25 to 0.25
- dec_down_avg: float32 [2048, 512], P('fsdp'), may hold values from -0.125 to 0.125
- vector_avg: float32 [5120], replicated, may hold values from 0.5 to 1.5
Outputs:
- embed_mom_new: float32 [768, 1024], P('fsdp')
- embed_new: float32 [768, 1024], P('fsdp')
- embed_avg_new: float32 [768, 1024], P('fsdp')
- embed_copy: bfloat16 [768, 1024], P('fsdp')
- wide_enc_mom_new: float32 [1024, 8704], P('fsdp')
- wide_enc_new: float32 [1024, 8704], P('fsdp')
- wide_enc_avg_new: float32 [1024, 8704], P('fsdp')
- wide_enc_copy: bfloat16 [1024, 8704], P('fsdp')
- enc_down_mom_new: float32 [4096, 1024], P('fsdp')
- enc_down_new: float32 [4096, 1024], P('fsdp')
- enc_down_avg_new: float32 [4096, 1024], P('fsdp')
- enc_down_copy: bfloat16 [4096, 1024], P('fsdp')
- wide_dec_mom_new: float32 [512, 5056], P('fsdp')
- wide_dec_new: float32 [512, 5056], P('fsdp')
- wide_dec_avg_new: float32 [512, 5056], P('fsdp')
- wide_dec_copy: bfloat16 [512, 5056], P('fsdp')
- dec_down_mom_new: float32 [2048, 512], P('fsdp')
- dec_down_new: float32 [2048, 512], P('fsdp')
- dec_down_avg_new: float32 [2048, 512], P('fsdp')
- dec_down_copy: bfloat16 [2048, 512], P('fsdp')
- vector_mom_new: float32 [5120], replicated
- vectors_new: float32 [5120], replicated
- vector_avg_new: float32 [5120], replicated
- loss_sum: float32 [], replicated
- count: float32 [], replicated
Inputs may be any that keep to these rules, and one draw needn't show every extreme that they name: In each block the valid slots are its first 4 k, k from 1 to 192; the last block holds 768 valid slots. Invalid slots are masked; in each block exactly a quarter of the valid slots are unmasked, at most 192. `scene_ids`: block b holds scene 2 b in its first slots and scene 2 b + 1 from a split on, possibly none.
All inputs are finite; a program needn't handle non-finite values.
Results may differ from a plain program's by a relative error of at most 0.0044.
The roundings to bfloat16 on the way count: a program that leaves them out, or rounds other values in their place, can miss the bound.
Values may be sent and summed in bfloat16 or wider, within the bound.
A program may use at most 320 MiB of HBM per device.

v0:
```python
from functools import partial

import jax
import jax.numpy as jnp
from jax import lax
from jax.sharding import PartitionSpec as P

D = 1024
HEADS = 16
FF = 4096
DD = 512
DHEADS = 16
DFF = 2048
PATCH = 16
BANDS = 3
TOK_DEV = 768
PD = 768
LOWD = 192
VIS = 192


EPS = 1e-06
MOMENTUM = 0.9
DECAY = 0.0001
AVERAGE = 0.9
STEP_UNIT = 0.003
NEGATIVE = -1e30


def matmul(left, right):
    return jnp.dot(left, right, preferred_element_type=jnp.float32)


def left_t(left, right):
    return lax.dot_general(
        left, right, (((0,), (0,)), ((), ())), preferred_element_type=jnp.float32
    )


def right_t(left, right):
    return lax.dot_general(
        left, right, (((1,), (1,)), ((), ())), preferred_element_type=jnp.float32
    )


def layer_norm(h, gain):
    mean = jnp.mean(h, -1, keepdims=True)
    cent = h - mean
    var = jnp.mean(cent * cent, -1, keepdims=True)
    return cent * lax.rsqrt(var + EPS) * gain


def norm_back(h, gain, grad):
    result, pull = jax.vjp(layer_norm, h, gain)
    return pull(grad)


def positions(coord, scale, width):
    quarter = width // 4
    omega = 10000.0 ** (-jnp.arange(quarter, dtype=jnp.float32) / quarter)
    angle_x = coord[:, 0:1].astype(jnp.float32) * scale[:, None] * omega[None, :]
    angle_y = coord[:, 1:2].astype(jnp.float32) * scale[:, None] * omega[None, :]
    return jnp.concatenate(
        [jnp.sin(angle_x), jnp.cos(angle_x), jnp.sin(angle_y), jnp.cos(angle_y)], -1
    )


def row_loss(pred, normed):
    rows = normed.shape[0]
    coarse = jnp.mean(normed.reshape(rows, BANDS, PATCH // 2, 2, PATCH // 2, 2), axis=(3, 5))
    upper = jnp.repeat(jnp.repeat(coarse, 2, axis=2), 2, axis=3).reshape(rows, PD)
    err_high = pred[:, :PD] - (normed - upper)
    err_low = pred[:, PD:] - coarse.reshape(rows, LOWD)
    return jnp.mean(jnp.sqrt(err_high * err_high + 1.0) - 1.0, -1) + jnp.mean(err_low * err_low, -1)


def split_heads(qkv, heads):
    rows, width = (qkv.shape[0], qkv.shape[1] // 3)
    parts = qkv.reshape(rows, 3, heads, width // heads).transpose(1, 2, 0, 3)
    return (parts[0], parts[1], parts[2])


def head_probs(query, keys, allow):
    scores = right_t(query, keys) * query.shape[1] ** (-0.5)
    scores = jnp.where(allow, scores, NEGATIVE)
    probs = jnp.exp(scores - jnp.max(scores, -1, keepdims=True))
    return probs / jnp.sum(probs, -1, keepdims=True)


def attend(qkv, allow, heads):
    query, keys, values = split_heads(qkv, heads)

    def one_head(item):
        probs = head_probs(item[0], item[1], allow)
        return matmul(probs.astype(jnp.bfloat16), item[2])

    mixed = lax.map(one_head, (query, keys, values))
    return mixed.transpose(1, 0, 2).reshape(qkv.shape[0], qkv.shape[1] // 3).astype(jnp.bfloat16)


def attend_back(qkv, dmixed, allow, heads):
    rows = qkv.shape[0]
    query, keys, values = split_heads(qkv, heads)
    dout = dmixed.astype(jnp.bfloat16).reshape(rows, heads, -1).transpose(1, 0, 2)
    factor = query.shape[2] ** (-0.5)

    def one_head(item):
        hq, hk, hv, hd = item
        probs = head_probs(hq, hk, allow)
        dvalues = left_t(probs.astype(jnp.bfloat16), hd)
        dprobs = right_t(hd, hv)
        dscores = (probs * (dprobs - jnp.sum(dprobs * probs, -1, keepdims=True))).astype(
            jnp.bfloat16
        )
        dquery = matmul(dscores, hk) * factor
        dkeys = left_t(dscores, hq) * factor
        return jnp.stack([dquery, dkeys, dvalues])

    grads = lax.map(one_head, (query, keys, values, dout))
    return grads.transpose(2, 1, 0, 3).reshape(rows, qkv.shape[1])


def block_parts(h, weights, gains, allow, heads):
    wqkv, wout, wup, wdown = weights
    normed_a = layer_norm(h, gains[0]).astype(jnp.bfloat16)
    qkv = matmul(normed_a, wqkv).astype(jnp.bfloat16)
    mixed = attend(qkv, allow, heads)
    return (normed_a, qkv, mixed)


def block_forward(h, weights, gains, allow, heads):
    normed_a, qkv, mixed = block_parts(h, weights, gains, allow, heads)
    middle = h + matmul(mixed, weights[1])
    normed_b = layer_norm(middle, gains[1]).astype(jnp.bfloat16)
    hidden = jax.nn.gelu(matmul(normed_b, weights[2]), approximate=False).astype(jnp.bfloat16)
    return (middle + matmul(hidden, weights[3]), middle)


def block_backward(h, middle, grad, weights, gains, allow, heads):
    wqkv, wout, wup, wdown = weights
    normed_a, qkv, mixed = block_parts(h, weights, gains, allow, heads)
    normed_b = layer_norm(middle, gains[1]).astype(jnp.bfloat16)
    before = matmul(normed_b, wup)
    after, gelu_pull = jax.vjp(partial(jax.nn.gelu, approximate=False), before)
    hidden = after.astype(jnp.bfloat16)
    dbranch = grad.astype(jnp.bfloat16)
    dbefore = gelu_pull(right_t(dbranch, wdown))[0].astype(jnp.bfloat16)
    dmiddle, dgain_two = norm_back(middle, gains[1], right_t(dbefore, wup))
    dmiddle = dmiddle + grad
    dattn = dmiddle.astype(jnp.bfloat16)
    dqkv = attend_back(qkv, right_t(dattn, wout), allow, heads).astype(jnp.bfloat16)
    dh, dgain_one = norm_back(h, gains[0], right_t(dqkv, wqkv))
    pairs = ((normed_a, dqkv), (mixed, dattn), (normed_b, dbefore), (hidden, dbranch))
    return (dh + dmiddle, pairs, (dgain_one, dgain_two))


def reduce_rows(left, right):
    return lax.psum_scatter(
        left_t(
            lax.slice_in_dim(
                left, 0, lax.axis_size("fsdp") * (left.shape[1] // lax.axis_size("fsdp")), axis=1
            ),
            right,
        ),
        "fsdp",
        scatter_dimension=0,
        tiled=True,
    )


def enc_split(wide, down):
    return (
        (wide[:, : 3 * D], wide[:, 3 * D : 4 * D], wide[:, 4 * D : 4 * D + FF], down),
        wide[:, 4 * D + FF :],
    )


def dec_split(wide, down):
    return (
        (wide[:, : 3 * DD], wide[:, 3 * DD : 4 * DD], wide[:, 4 * DD : 4 * DD + DFF], down),
        wide[:, 4 * DD + DFF :],
    )


def advance(weight, mom, avg, grad, rate):
    grad = grad + DECAY * weight
    buf = MOMENTUM * mom + grad
    new = weight - rate * (grad + MOMENTUM * buf)
    return (buf, new, AVERAGE * avg + (1.0 - AVERAGE) * new)


def body(
    pixels,
    masked,
    valid,
    scene_ids,
    gsd_index,
    coords,
    embed,
    wide_enc,
    enc_down,
    wide_dec,
    dec_down,
    vectors,
    embed_mom,
    wide_enc_mom,
    enc_down_mom,
    wide_dec_mom,
    dec_down_mom,
    vector_mom,
    embed_avg,
    wide_enc_avg,
    enc_down_avg,
    wide_dec_avg,
    dec_down_avg,
    vector_avg,
):
    slots = pixels.shape[0]
    rows_ok = valid.astype(jnp.float32)
    flags = rows_ok * masked.astype(jnp.float32)
    bands = pixels.reshape(slots, BANDS, PATCH * PATCH)
    weighted = bands * rows_ok[:, None, None]
    band_sum = jnp.sum(weighted, axis=(0, 2))
    counts = jnp.stack([jnp.sum(rows_ok), jnp.sum(flags)])
    band_sq = jnp.sum(weighted * bands, axis=(0, 2))
    band_sum, band_sq, counts = lax.psum((band_sum, band_sq, counts), ("dp", "fsdp"))
    n_pix = counts[0] * (PATCH * PATCH)
    mean = band_sum / n_pix
    var = band_sq / n_pix - mean * mean
    cent = bands - mean[None, :, None]
    normed = (cent * lax.rsqrt(var + EPS)[None, :, None]).reshape(slots, PD)
    count = counts[1]
    level = jnp.where(scene_ids % 2 == 0, gsd_index[0], gsd_index[1]).astype(jnp.float32)
    scale = jnp.exp2(0.5 * level - 1.0)
    index = jnp.arange(slots, dtype=jnp.int32)
    seen_rows = (valid > 0) & (masked == 0)
    order = jnp.argsort(jnp.where(seen_rows, index, index + slots))[:VIS]
    kept = jnp.arange(VIS, dtype=jnp.int32) < jnp.sum(seen_rows.astype(jnp.int32))
    keptf = kept.astype(jnp.float32)[:, None]
    scene_seen = scene_ids[order]
    allow_enc = kept[None, :] & (scene_seen[:, None] == scene_seen[None, :]) | jnp.eye(
        VIS, dtype=bool
    )
    allow_dec = (valid[None, :] > 0) & (scene_ids[:, None] == scene_ids[None, :]) | jnp.eye(
        slots, dtype=bool
    )
    gains_enc = (vectors[:D], vectors[D : 2 * D])
    gain_enc_out = vectors[2 * D : 3 * D]
    base = 3 * D
    gains_dec = (vectors[base : base + DD], vectors[base + DD : base + 2 * DD])
    gain_dec_out = vectors[base + 2 * DD : base + 3 * DD]
    token = vectors[base + 3 * DD :]
    low_enc = (
        embed.astype(jnp.bfloat16),
        wide_enc.astype(jnp.bfloat16),
        enc_down.astype(jnp.bfloat16),
    )
    low_dec = (wide_dec.astype(jnp.bfloat16), dec_down.astype(jnp.bfloat16))
    w_embed, w_enc, w_enc_down = (
        lax.all_gather(low_enc[0], "fsdp", axis=0, tiled=True),
        lax.all_gather(low_enc[1], "fsdp", axis=0, tiled=True),
        lax.all_gather(low_enc[2], "fsdp", axis=0, tiled=True),
    )
    enc_weights, w_link = enc_split(w_enc, w_enc_down)
    inputs = normed.astype(jnp.bfloat16)[order]
    h_start = matmul(inputs, w_embed) + positions(coords[order], scale[order], D)
    h_end, h_middle = block_forward(h_start, enc_weights, gains_enc, allow_enc, HEADS)
    encoded = layer_norm(h_end, gain_enc_out).astype(jnp.bfloat16)
    seen_out = matmul(encoded, w_link)
    y_start = (
        token
        + positions(coords, scale, DD)
        + jnp.zeros((slots, DD), jnp.float32).at[order].add((seen_out - token) * keptf)
    )
    w_dec, w_dec_down = (
        lax.all_gather(low_dec[0], "fsdp", axis=0, tiled=True),
        lax.all_gather(low_dec[1], "fsdp", axis=0, tiled=True),
    )
    dec_weights, w_head = dec_split(w_dec, w_dec_down)
    y_end, y_middle = block_forward(y_start, dec_weights, gains_dec, allow_dec, DHEADS)
    decoded = layer_norm(y_end, gain_dec_out).astype(jnp.bfloat16)
    pred = matmul(decoded, w_head)
    losses, loss_pull = jax.vjp(lambda values: row_loss(values, normed), pred)
    local_loss = jnp.sum(flags * losses)
    dpred = loss_pull(flags / count)[0].astype(jnp.bfloat16)
    w_dec, w_dec_down = (
        lax.all_gather(low_dec[0], "fsdp", axis=0, tiled=True),
        lax.all_gather(low_dec[1], "fsdp", axis=0, tiled=True),
    )
    dec_weights, w_head = dec_split(w_dec, w_dec_down)
    head_grad = reduce_rows(decoded, dpred)
    dy_end, dgain_dec_out = norm_back(y_end, gain_dec_out, right_t(dpred, w_head))
    dy_start, dec_pairs, dgains_dec = block_backward(
        y_start, y_middle, dy_end, dec_weights, gains_dec, allow_dec, DHEADS
    )
    dec_grads = [reduce_rows(pair[0], pair[1]) for pair in dec_pairs]
    picked = dy_start[order] * keptf
    dtoken = jnp.sum(dy_start, 0) - jnp.sum(picked, 0)
    dseen = picked.astype(jnp.bfloat16)
    w_embed, w_enc, w_enc_down = (
        lax.all_gather(low_enc[0], "fsdp", axis=0, tiled=True),
        lax.all_gather(low_enc[1], "fsdp", axis=0, tiled=True),
        lax.all_gather(low_enc[2], "fsdp", axis=0, tiled=True),
    )
    enc_weights, w_link = enc_split(w_enc, w_enc_down)
    link_grad = reduce_rows(encoded, dseen)
    dh_end, dgain_enc_out = norm_back(h_end, gain_enc_out, right_t(dseen, w_link))
    dh_start, enc_pairs, dgains_enc = block_backward(
        h_start, h_middle, dh_end, enc_weights, gains_enc, allow_enc, HEADS
    )
    enc_grads = [reduce_rows(pair[0], pair[1]) for pair in enc_pairs]
    embed_grad = reduce_rows(inputs, dh_start.astype(jnp.bfloat16))
    wide_enc_grad = jnp.concatenate([enc_grads[0], enc_grads[1], enc_grads[2], link_grad], 1)
    wide_dec_grad = jnp.concatenate([dec_grads[0], dec_grads[1], dec_grads[2], head_grad], 1)
    vector_grad = jnp.concatenate(
        [
            dgains_enc[0],
            dgains_enc[1],
            dgain_enc_out,
            dgains_dec[0],
            dgains_dec[1],
            dgain_dec_out,
            dtoken,
        ]
    )
    vector_grad, loss_sum = lax.psum((vector_grad, local_loss), ("dp", "fsdp"))
    rate = STEP_UNIT * (PD * TOK_DEV * lax.axis_size("dp") * lax.axis_size("fsdp")) ** 0.5
    weights = (embed, wide_enc, enc_down, wide_dec, dec_down)
    moms = (embed_mom, wide_enc_mom, enc_down_mom, wide_dec_mom, dec_down_mom)
    avgs = (embed_avg, wide_enc_avg, enc_down_avg, wide_dec_avg, dec_down_avg)
    outs = []
    shard_grads = lax.psum(
        (embed_grad, wide_enc_grad, enc_grads[3], wide_dec_grad, dec_grads[3]), "dp"
    )
    for number in range(5):
        buf, new, avg = advance(
            weights[number], moms[number], avgs[number], shard_grads[number], rate
        )
        outs += [buf, new, avg, new.astype(jnp.bfloat16)]
    buf, new, avg = advance(vectors, vector_mom, vector_avg, vector_grad, rate)
    return (
        outs[0],
        outs[1],
        outs[2],
        outs[3],
        outs[4],
        outs[5],
        outs[6],
        outs[7],
        outs[8],
        outs[9],
        outs[10],
        outs[11],
        outs[12],
        outs[13],
        outs[14],
        outs[15],
        outs[16],
        outs[17],
        outs[18],
        outs[19],
        buf,
        new,
        avg,
        loss_sum,
        count,
    )


def solution(mesh):
    placed = (
        P(("dp", "fsdp"), None),
        P(("dp", "fsdp")),
        P(("dp", "fsdp")),
        P(("dp", "fsdp")),
        P(("dp", "fsdp")),
        P(("dp", "fsdp"), None),
        P("fsdp", None),
        P("fsdp", None),
        P("fsdp", None),
        P("fsdp", None),
        P("fsdp", None),
        P(),
        P("fsdp", None),
        P("fsdp", None),
        P("fsdp", None),
        P("fsdp", None),
        P("fsdp", None),
        P(),
        P("fsdp", None),
        P("fsdp", None),
        P("fsdp", None),
        P("fsdp", None),
        P("fsdp", None),
        P(),
    )
    return jax.shard_map(
        body,
        mesh=mesh,
        in_specs=placed,
        out_specs=(
            P("fsdp", None),
            P("fsdp", None),
            P("fsdp", None),
            P("fsdp", None),
            P("fsdp", None),
            P("fsdp", None),
            P("fsdp", None),
            P("fsdp", None),
            P("fsdp", None),
            P("fsdp", None),
            P("fsdp", None),
            P("fsdp", None),
            P("fsdp", None),
            P("fsdp", None),
            P("fsdp", None),
            P("fsdp", None),
            P("fsdp", None),
            P("fsdp", None),
            P("fsdp", None),
            P("fsdp", None),
            P(),
            P(),
            P(),
            P(),
            P(),
        ),
        check_vma=False,
    )
```

profile of v0, /device:TPU:0, one launch (start us, length us, event | category | flops | bytes accessed | tf_op | source)
XLA Modules:
  0.0 1523.2 jit_solution(3085294072656772149)
XLA Ops:
  42.6 42.2 %all-reduce.3 = (f32[3]{0:T(128)S(1)}, f32[2]{0:T(128)S(1)}, f32[3]{0:T(128)S(1)}) all-reduce(f32[3]{0:T(128)S(1)} %reduce_sum.445, f32[2]{0:T(128)S(1)} %pad_maximum_fusion.2, f32[3]{0:T(128)S(1)} %reduce_sum.453), channel_id=1, replica_groups=mesh['dp'=4,'fsdp'=8] {'dp','fsdp'}, use_global_device_ids=true, to_apply=%region_2.0 | all-reduce | flops 8 | bytes 64 | tf_op jit(solution)/shard_map/psum | solution.py:226
  113.2 23.3 %all-gather.8.cloned.1.call-done = bf16[1024,8704]{1,0:T(8,128)(2,1)} async-done(((bf16[128,8704]{1,0:T(8,128)(2,1)}), bf16[1024,8704]{1,0:T(8,128)(2,1)}) %all-gather.8.cloned.1.call-update) | async-done | bytes 17825808 | tf_op jit(solution)/shard_map/all_gather | solution.py:302
  152.6 43.8 %while.52 = (s32[]{:T(128)}, bf16[16,192,64]{1,2,0:T(8,128)(2,1)}, bf16[16,192,64]{2,1,0:T(8,128)(2,1)}, bf16[16,192,64]{2,1,0:T(8,128)(2,1)}, bf16[16,192,64]{2...) while((s32[]{:T(128)}, bf16[16,192,64]{1,2,0:T(8,128)(2,1)}, ...), condition=%wide.region_16.17_spmd.clone, body=%wide.region_13.16_spmd.clone.sunk | while | flops 9879170 | bytes 663901 | solution.py:97
  199.1 13.2 multiply_convert_fusion.3
  223.8 13.0 all-gather.12.cloned.1.call-done
  257.6 57.9 %while.53 = (s32[]{:T(128)}, bf16[16,768,32]{1,2,0:T(8,128)(2,1)S(1)}, bf16[16,768,32]{2,1,0:T(8,128)(2,1)}, bf16[16,768,32]{2,1,0:T(8,128)(2,1)}, bf16[16,768,3...) while((s32[]{:T(128)}, ...), condition=%wide.region_27.28_spmd.clone, body=%wide.region_24.27_spmd.clone.sunk | while | flops 82573824 | bytes 7794781 | solution.py:97
  318.6 18.6 %multiply_convert_fusion.2 = (bf16[768,2048]{1,0:T(8,128)(2,1)}, f32[768,2048]{1,0:T(8,128)}, f32[768,2048]{1,0:T(8,128)}) fusion(bf16[512,5056]{1,0:T(8,128)(2,1)} %all-gather.12.cloned.1.call-done, f32[768,512]{0,1:T(8,128)S(1)} %get-tuple-element.515, f32[512]{0:T(512)S(1)} %copy-done.113, f32[768]{0:T(1024)S(1)} %fusion.163, ...), kind=kOutput, calls=%fused_computation.127 | convolution fusion | flops 1714421760 | bytes 19406848 | tf_op jit(solution)/shard_map/dot_general | solution.py:31
  376.8 148.1 %while.54 = (s32[]{:T(128)}, bf16[16,3,768,32]{2,3,0,1:T(8,128)(2,1)}, bf16[16,768,32]{2,1,0:T(8,128)(2,1)}, bf16[16,768,32]{2,1,0:T(8,128)(2,1)}, bf16[16,768,3...) while((s32[]{:T(128)}, ...), condition=%wide.region_41.42_spmd.clone, body=%wide.region_37.41_spmd.clone.sunk | while | flops 201668352 | bytes 21917812 | solution.py:119
  554.5 9.1 add_convert_fusion.1
  563.7 7.6 multiply_reduce_fusion.14
  582.1 80.6 %while.55 = (s32[]{:T(128)}, bf16[16,3,192,64]{2,3,1,0:T(8,128)(2,1)}, bf16[16,192,64]{2,1,0:T(8,128)(2,1)}, bf16[16,192,64]{2,1,0:T(8,128)(2,1)}, bf16[16,192,6...) while((s32[]{:T(128)}, ...), condition=%wide.region_52.53_spmd.clone, body=%wide.region_48.52_spmd.clone.sunk | while | flops 24636864 | bytes 1922933 | solution.py:119
  665.6 6.6 fusion.177
  672.4 9.7 fusion.178
  700.4 8.5 fusion.172
  711.6 20.9 %reduce-scatter.16.cloned.1.call-done = f32[128,1024]{1,0:T(8,128)} async-done(((f32[1024,1024]{1,0:T(8,128)}), f32[128,1024]{1,0:T(8,128)}) %reduce-scatter.16.cloned.1.call-update) | async-done | bytes 524304 | tf_op jit(solution)/shard_map/reduce_scatter | solution.py:158
  732.5 96.2 %reduce-scatter.14.cloned.1.call-done = f32[128,3072]{1,0:T(8,128)} async-done(((f32[1024,3072]{1,0:T(8,128)}), f32[128,3072]{1,0:T(8,128)}) %reduce-scatter.14.cloned.1.call-update) | async-done | bytes 1572880 | tf_op jit(solution)/shard_map/reduce_scatter | solution.py:158
  828.7 120.0 %reduce-scatter.18.cloned.1.call-done = f32[128,4096]{1,0:T(8,128)} async-done(((f32[1024,4096]{1,0:T(8,128)}), f32[128,4096]{1,0:T(8,128)}) %reduce-scatter.18.cloned.1.call-update) | async-done | bytes 2097168 | tf_op jit(solution)/shard_map/reduce_scatter | solution.py:158
  953.4 45.1 %reduce-scatter.12.cloned.1.call-done = f32[96,1024]{1,0:T(8,128)} async-done(((f32[768,1024]{1,0:T(8,128)}), f32[96,1024]{1,0:T(8,128)}) %reduce-scatter.12.cloned.1.call-update) | async-done | bytes 393232 | tf_op jit(solution)/shard_map/reduce_scatter | solution.py:158
  998.5 55.1 %reduce-scatter.32.cloned.1.call-done = f32[256,512]{1,0:T(8,128)} async-done(((f32[2048,512]{1,0:T(8,128)}), f32[256,512]{1,0:T(8,128)}) %reduce-scatter.32.cloned.1.call-update) | async-done | bytes 524304 | tf_op jit(solution)/shard_map/reduce_scatter | solution.py:158
  1053.6 119.9 %reduce-scatter.22.cloned.1.call-done = f32[512,1024]{1,0:T(8,128)} async-done(((f32[4096,1024]{1,0:T(8,128)}), f32[512,1024]{1,0:T(8,128)}) %reduce-scatter.22.cloned.1.call-update) | async-done | bytes 2097168 | tf_op jit(solution)/shard_map/reduce_scatter | solution.py:158
  1174.4 43.4 %all-reduce.2 = (f32[5120]{0:T(1024)S(1)}, f32[]{:T(128)}) all-reduce(f32[5120]{0:T(1024)S(1)} %constant_dynamic-update-slice_fusion, f32[]{:T(128)} %get-tuple-element.491), channel_id=1, replica_groups=mesh['dp'=4,'fsdp'=8] {'dp','fsdp'}, use_global_device_ids=true, to_apply=%region_79.80 | all-reduce | flops 5121 | bytes 40968 | tf_op jit(solution)/shard_map/psum | solution.py:326
  1218.4 266.7 %all-reduce.7.cloned.1.call-done = (f32[96,1024]{1,0:T(8,128)}, f32[128,8704]{1,0:T(8,128)}, f32[512,1024]{1,0:T(8,128)}, f32[64,5056]{1,0:T(8,128)}, f32[256,512]{1,0:T(8,128)}) async-done(((f32[96,1024]{1,0:T(8,128)}, f32[128,8704]{1,0:T(8,128)}, f32[512,1024]{1,0:T(8,128)}, f32[64,5056]{1,0:T(8,128)}, f32[256,512]{1,0:T(8,128)}), (f32[96,1024]{1,0:T(8,128)}, f32[128,8704]{1,0:T(8,128)}, ...) | async-done | bytes 8765456 | tf_op jit(solution)/shard_map/psum | solution.py:332
  1488.0 9.2 fusion.183
  1497.2 6.7 multiply_add_fusion
  (840 shorter events, 570.9 us)
Async XLA Ops:
  7.2 103.6 %all-gather.6.cloned.1.call-start = ((), (), s32[]{:S(2)}) async-start(), calls=%async_computation.11 | async-start | bytes 1769472 | tf_op jit(solution)/shard_map/all_gather | solution.py:260
  9.0 127.5 %all-gather.8.cloned.1.call-start = ((), (), s32[]{:S(2)}) async-start(), calls=%async_computation.12 | async-start | bytes 20054016 | tf_op jit(solution)/shard_map/all_gather | solution.py:302
  12.9 199.4 %all-gather.10.cloned.1.call-start = ((), (), s32[]{:S(2)}) async-start(), calls=%async_computation.13 | async-start | bytes 9437184 | tf_op jit(solution)/shard_map/all_gather | solution.py:262
  15.6 221.2 %all-gather.12.cloned.1.call-start = ((), (), s32[]{:S(2)}) async-start(), calls=%async_computation.14 | async-start | bytes 5898240 | tf_op jit(solution)/shard_map/all_gather | solution.py:287
  16.6 320.6 %all-gather.14.cloned.1.call-start = ((), (), s32[]{:S(2)}) async-start(), calls=%async_computation.15 | async-start | bytes 2359296 | tf_op jit(solution)/shard_map/all_gather | solution.py:277
  17.5 691.5 %reduce-scatter.26.cloned.1.call-start = ((), (), s32[]{:S(2)}) async-start(), calls=%async_computation.23 | async-start | bytes 1179648 | tf_op jit(solution)/shard_map/reduce_scatter | solution.py:158
  33.0 166.1 %copy-start.58 = (f32[1024]{0:T(1024)}, f32[1024]{0:T(1024)S(1)}, u32[]{:S(2)}) copy-start(f32[1024]{0:T(1024)S(1)} %get-tuple-element.485) | copy-start | bytes 12292
  365.5 343.5 %reduce-scatter.30.cloned.1.call-start = ((), (), s32[]{:S(2)}) async-start(), calls=%async_computation.25 | async-start | bytes 2359296 | tf_op jit(solution)/shard_map/reduce_scatter | solution.py:158
  376.7 332.3 %reduce-scatter.24.cloned.1.call-start = ((), (), s32[]{:S(2)}) async-start(), calls=%async_computation.22 | async-start | bytes 3538944 | tf_op jit(solution)/shard_map/reduce_scatter | solution.py:158
  376.8 148.2 %copy-start.65 = (f32[768]{0:T(1024)S(1)}, f32[768]{0:T(1024)}, u32[]{:S(2)}) copy-start(f32[768]{0:T(1024)} %copy-done.64) | copy-start | bytes 9220
  376.8 148.2 %copy-start.71 = (f32[768]{0:T(1024)S(1)}, f32[768]{0:T(1024)}, u32[]{:S(2)}) copy-start(f32[768]{0:T(1024)} %copy-done.70) | copy-start | bytes 9220
  376.8 148.2 %copy-start.89 = (f32[512]{0:T(512)S(1)}, f32[512]{0:T(512)}, u32[]{:S(2)}) copy-start(f32[512]{0:T(512)} %get-tuple-element.482) | copy-start | bytes 6148
  529.7 179.3 %reduce-scatter.28.cloned.1.call-start = ((), (), s32[]{:S(2)}) async-start(), calls=%async_computation.24 | async-start | bytes 4718592 | tf_op jit(solution)/shard_map/reduce_scatter | solution.py:158
  536.9 174.6 %reduce-scatter.20.cloned.1.call-start = ((), (), s32[]{:S(2)}) async-start(), calls=%async_computation.20 | async-start | bytes 2359296 | tf_op jit(solution)/shard_map/reduce_scatter | solution.py:158
  554.3 178.2 %reduce-scatter.16.cloned.1.call-start = ((), (), s32[]{:S(2)}) async-start(), calls=%async_computation.18 | async-start | bytes 4718592 | tf_op jit(solution)/shard_map/reduce_scatter | solution.py:158
  581.5 247.2 %reduce-scatter.14.cloned.1.call-start = ((), (), s32[]{:S(2)}) async-start(), calls=%async_computation.17 | async-start | bytes 14155776 | tf_op jit(solution)/shard_map/reduce_scatter | solution.py:158
  672.2 276.5 %reduce-scatter.18.cloned.1.call-start = ((), (), s32[]{:S(2)}) async-start(), calls=%async_computation.19 | async-start | bytes 18874368 | tf_op jit(solution)/shard_map/reduce_scatter | solution.py:158
  682.2 316.4 %reduce-scatter.12.cloned.1.call-start = ((), (), s32[]{:S(2)}) async-start(), calls=%async_computation.16 | async-start | bytes 3538944 | tf_op jit(solution)/shard_map/reduce_scatter | solution.py:158
  692.7 361.0 %reduce-scatter.32.cloned.1.call-start = ((), (), s32[]{:S(2)}) async-start(), calls=%async_computation.26 | async-start | bytes 4718592 | tf_op jit(solution)/shard_map/reduce_scatter | solution.py:158
  698.8 474.7 %reduce-scatter.22.cloned.1.call-start = ((), (), s32[]{:S(2)}) async-start(), calls=%async_computation.21 | async-start | bytes 18874368 | tf_op jit(solution)/shard_map/reduce_scatter | solution.py:158
  708.9 776.2 %all-reduce.7.cloned.1.call-start = ((), (), s32[]{:S(2)}) async-start(), calls=%async_computation.27 | async-start | bytes 17563648 | tf_op jit(solution)/shard_map/psum | solution.py:332
  1173.6 311.6 %copy-start.45 = (f32[96,1024]{1,0:T(8,128)S(1)}, f32[96,1024]{1,0:T(8,128)}, u32[]{:S(2)}) copy-start(f32[96,1024]{1,0:T(8,128)} %param.38) | copy-start | bytes 1179652
  1173.6 311.6 %copy-start.57 = (f32[96,1024]{1,0:T(8,128)S(1)}, f32[96,1024]{1,0:T(8,128)}, u32[]{:S(2)}) copy-start(f32[96,1024]{1,0:T(8,128)} %param.44) | copy-start | bytes 1179652
  1173.6 313.5 %copy-start.56 = (f32[96,1024]{1,0:T(8,128)S(1)}, f32[96,1024]{1,0:T(8,128)}, u32[]{:S(2)}) copy-start(f32[96,1024]{1,0:T(8,128)} %param.50) | copy-start | bytes 1179652
  (134 other events, 1017.5 us)
Sparse Core Ops, SparseCore 0:
  10.5 28.8 all-gather.5
  41.8 94.6 all-gather.7
  139.0 54.3 all-gather.9
  195.7 41.1 all-gather.11
  239.2 27.9 all-gather.13
  365.6 36.2 reduce-scatter.25
  405.8 41.1 reduce-scatter.29
  529.9 46.5 reduce-scatter.23
  580.4 51.4 reduce-scatter.27
  635.9 41.2 reduce-scatter.19
  681.1 51.2 reduce-scatter.15
  736.2 92.4 reduce-scatter.13
  832.7 115.9 reduce-scatter.17
  952.3 46.2 reduce-scatter.11
  1002.3 51.2 reduce-scatter.31
  1057.5 115.9 reduce-scatter.21
  1177.9 307.1 all-reduce.6
where the time goes:
time: 1540 us; the launch traced here: 1520 us
  waiting for transfers between devices  761 us (49%)
  matrix products  449 us (29%)
  other arithmetic  130 us (8%)
  blocking collectives  85.6 us (6%)
  local copies, waits for them, and re-layouts  78.3 us (5%)
  between operations  16.7 us (1%)
    reduce_scatter x11, waiting for transfers between devices, reduce_rows(): lax.psum_scatter(left_t(lax.slice_in_dim(left, 0, lax.axis_size('fsdp') *...  457 us
    psum x1, waiting for transfers between devices, body(): lax.psum((embed_grad, wide_enc_grad, enc_grads[3], wide_dec_grad, dec_gra...  267 us
    dot_general x106, matrix products, right_t(): lax.dot_general(left, right, (((1,), (1,)), ((), ())), preferred_element_...  180 us
    dot_general x75, matrix products, matmul(): return jnp.dot(left, right, preferred_element_type=jnp.float32)  149 us
    dot_general x75, matrix products, left_t(): lax.dot_general(left, right, (((0,), (0,)), ((), ())), preferred_element_...  120 us
    psum x1, blocking collectives, body(): vector_grad, loss_sum = lax.psum((vector_grad, local_loss), ('dp', 'fsdp'))  43.4 us
    psum x1, blocking collectives, body(): lax.psum((band_sum, band_sq, counts), ('dp', 'fsdp'))  42.2 us
    unnamed x296, local copies, waits for them, and re-layouts  37 us
  transfers between devices with their start and end apart: 17, of which 9 were waited for; matrix products, arithmetic and copies ran while one was open for 38% of the time, Pallas kernels for 0%

commit v1 on v0

v1 whole, which is shorter than its diff:
```python
from functools import partial

import jax
import jax.numpy as jnp
from jax import lax
from jax.experimental import pallas as pl
from jax.experimental.pallas import tpu as pltpu
from jax.sharding import PartitionSpec as P

D = 1024
HEADS = 16
FF = 4096
DD = 512
DHEADS = 16
DFF = 2048
PATCH = 16
BANDS = 3
TOK_DEV = 768
PD = 768
LOWD = 192
VIS = 192
HID = TOK_DEV - VIS

EPS = 1e-06
MOMENTUM = 0.9
DECAY = 0.0001
AVERAGE = 0.9
STEP_UNIT = 0.003
NEGATIVE = -1e30
LANES = 128
BF = jnp.bfloat16
F32 = jnp.float32


def matmul(left, right):
    return jnp.dot(left, right, preferred_element_type=jnp.float32)


def left_t(left, right):
    return lax.dot_general(
        left, right, (((0,), (0,)), ((), ())), preferred_element_type=jnp.float32
    )


def right_t(left, right):
    return lax.dot_general(
        left, right, (((1,), (1,)), ((), ())), preferred_element_type=jnp.float32
    )


def layer_norm(h, gain):
    mean = jnp.mean(h, -1, keepdims=True)
    cent = h - mean
    var = jnp.mean(cent * cent, -1, keepdims=True)
    return cent * lax.rsqrt(var + EPS) * gain


def norm_back(h, gain, grad):
    result, pull = jax.vjp(layer_norm, h, gain)
    return pull(grad)


def positions(coord, scale, width):
    quarter = width // 4
    omega = 10000.0 ** (-jnp.arange(quarter, dtype=jnp.float32) / quarter)
    angle_x = coord[:, 0:1] * scale[:, None] * omega[None, :]
    angle_y = coord[:, 1:2] * scale[:, None] * omega[None, :]
    return jnp.concatenate(
        [jnp.sin(angle_x), jnp.cos(angle_x), jnp.sin(angle_y), jnp.cos(angle_y)], -1
    )


def row_loss(pred, normed):
    rows = normed.shape[0]
    coarse = jnp.mean(normed.reshape(rows, BANDS, PATCH // 2, 2, PATCH // 2, 2), axis=(3, 5))
    upper = jnp.repeat(jnp.repeat(coarse, 2, axis=2), 2, axis=3).reshape(rows, PD)
    err_high = pred[:, :PD] - (normed - upper)
    err_low = pred[:, PD:] - coarse.reshape(rows, LOWD)
    return jnp.mean(jnp.sqrt(err_high * err_high + 1.0) - 1.0, -1) + jnp.mean(err_low * err_low, -1)


def attend_kernel(size, qt_ref, k_ref, vt_ref, bias_ref, ot_ref, lse_ref):
    per = LANES // size
    row_head = lax.broadcasted_iota(jnp.int32, qt_ref.shape, 0) // size
    factor = size ** (-0.5)
    for j in range(per):
        query = jnp.where(row_head == j, qt_ref[...].astype(F32), 0.0).astype(BF)
        scores = matmul(k_ref[...], query) * factor + bias_ref[...]
        top = jnp.max(scores, 0, keepdims=True)
        probs = jnp.exp(scores - top)
        total = jnp.sum(probs, 0, keepdims=True)
        probs = (probs * (1.0 / total)).astype(BF)
        rows = slice(j * size, (j + 1) * size)
        ot_ref[rows, :] = matmul(vt_ref[rows, :], probs).astype(BF)
        lse_ref[0, j : j + 1, :] = top + jnp.log(total)


def attend(qt, keys, vt, bias, size):
    width, queries = qt.shape
    rows = keys.shape[0]
    groups, per = width // LANES, LANES // size
    return pl.pallas_call(
        partial(attend_kernel, size),
        grid=(groups,),
        out_shape=(
            jax.ShapeDtypeStruct((width, queries), BF),
            jax.ShapeDtypeStruct((groups, per, queries), F32),
        ),
        in_specs=[
            pl.BlockSpec((LANES, queries), lambda g: (g, 0)),
            pl.BlockSpec((rows, LANES), lambda g: (0, g)),
            pl.BlockSpec((LANES, rows), lambda g: (g, 0)),
            pl.BlockSpec((rows, queries), lambda g: (0, 0)),
        ],
        out_specs=(
            pl.BlockSpec((LANES, queries), lambda g: (g, 0)),
            pl.BlockSpec((1, per, queries), lambda g: (g, 0, 0)),
        ),
        compiler_params=pltpu.CompilerParams(vmem_limit_bytes=40 * 2**20),
        cost_estimate=pl.CostEstimate(
            flops=4 * rows * queries * width * per,
            bytes_accessed=4 * rows * queries,
            transcendentals=rows * queries * width // size,
        ),
    )(qt, keys, vt, bias)


def attend_back_kernel(
    size,
    qt_ref,
    q_ref,
    k_ref,
    kt_ref,
    v_ref,
    do_ref,
    dot_ref,
    bias_ref,
    lse_ref,
    dqt_ref,
    dk_ref,
    dv_ref,
):
    per = LANES // size
    row_head = lax.broadcasted_iota(jnp.int32, qt_ref.shape, 0) // size
    lane_head = lax.broadcasted_iota(jnp.int32, dk_ref.shape, 1) // size
    factor = size ** (-0.5)
    dkeys = jnp.zeros(dk_ref.shape, F32)
    dvalues = jnp.zeros(dv_ref.shape, F32)
    for j in range(per):
        query = jnp.where(row_head == j, qt_ref[...].astype(F32), 0.0).astype(BF)
        dout = jnp.where(row_head == j, dot_ref[...].astype(F32), 0.0).astype(BF)
        scores = matmul(k_ref[...], query) * factor + bias_ref[...]
        probs = jnp.exp(scores - lse_ref[0, j : j + 1, :])
        dvalues = jnp.where(lane_head == j, matmul(probs.astype(BF), do_ref[...]), dvalues)
        dprobs = matmul(v_ref[...], dout)
        delta = jnp.sum(dprobs * probs, 0, keepdims=True)
        dscores = (probs * (dprobs - delta)).astype(BF)
        dkeys = jnp.where(lane_head == j, matmul(dscores, q_ref[...]), dkeys)
        rows = slice(j * size, (j + 1) * size)
        dqt_ref[rows, :] = (matmul(kt_ref[rows, :], dscores) * factor).astype(BF)
    dk_ref[...] = (dkeys * factor).astype(BF)
    dv_ref[...] = dvalues.astype(BF)


def attend_back(query, keys, values, dmixed, bias, lse, size):
    queries, width = query.shape
    rows = keys.shape[0]
    groups, per = width // LANES, LANES // size
    tall = lambda n: pl.BlockSpec((n, LANES), lambda g: (0, g))
    flat = lambda n: pl.BlockSpec((LANES, n), lambda g: (g, 0))
    return pl.pallas_call(
        partial(attend_back_kernel, size),
        grid=(groups,),
        out_shape=(
            jax.ShapeDtypeStruct((width, queries), BF),
            jax.ShapeDtypeStruct((rows, width), BF),
            jax.ShapeDtypeStruct((rows, width), BF),
        ),
        in_specs=[
            flat(queries),
            tall(queries),
            tall(rows),
            flat(rows),
            tall(rows),
            tall(queries),
            flat(queries),
            pl.BlockSpec((rows, queries), lambda g: (0, 0)),
            pl.BlockSpec((1, per, queries), lambda g: (g, 0, 0)),
        ],
        out_specs=(flat(queries), tall(rows), tall(rows)),
        compiler_params=pltpu.CompilerParams(vmem_limit_bytes=48 * 2**20),
        cost_estimate=pl.CostEstimate(
            flops=10 * rows * queries * width * per,
            bytes_accessed=4 * rows * queries,
            transcendentals=rows * queries * width // size,
        ),
    )(query.T, query, keys, keys.T, values, dmixed, dmixed.T, bias, lse)


def block_forward(h, weights, gains, bias, heads, skip):
    wqkv, wout, wup, wdown = weights
    width = h.shape[1]
    normed_a = layer_norm(h, gains[0]).astype(BF)
    query = matmul(normed_a[skip:], wqkv[:, :width]).astype(BF)
    keys = matmul(normed_a, wqkv[:, width : 2 * width]).astype(BF)
    values = matmul(normed_a, wqkv[:, 2 * width :]).astype(BF)
    mixed_t, lse = attend(query.T, keys, values.T, bias, width // heads)
    middle = h[skip:] + left_t(mixed_t, wout)
    normed_b = layer_norm(middle, gains[1]).astype(BF)
    before = matmul(normed_b, wup)
    hidden = jax.nn.gelu(before, approximate=False).astype(BF)
    end = middle + matmul(hidden, wdown)
    return end, (h, normed_a, query, keys, values, mixed_t, lse, middle, normed_b, before, hidden)


def block_backward(saved, grad, weights, gains, bias, heads, skip):
    wqkv, wout, wup, wdown = weights
    h, normed_a, query, keys, values, mixed_t, lse, middle, normed_b, before, hidden = saved
    width = h.shape[1]
    dbranch = grad.astype(BF)
    after, gelu_pull = jax.vjp(partial(jax.nn.gelu, approximate=False), before)
    dbefore = gelu_pull(right_t(dbranch, wdown))[0].astype(BF)
    dmiddle, dgain_two = norm_back(middle, gains[1], right_t(dbefore, wup))
    dmiddle = dmiddle + grad
    dattn = dmiddle.astype(BF)
    dmixed = right_t(dattn, wout).astype(BF)
    dqt, dkeys, dvalues = attend_back(query, keys, values, dmixed, bias, lse, width // heads)
    dquery = dqt.T
    if skip:
        dquery = jnp.pad(dquery, ((skip, 0), (0, 0)))
        dmiddle = jnp.pad(dmiddle, ((skip, 0), (0, 0)))
    dqkv = jnp.concatenate([dquery, dkeys, dvalues], 1)
    dh, dgain_one = norm_back(h, gains[0], right_t(dqkv, wqkv))
    wgrads = (
        left_t(normed_a, dqkv),
        matmul(mixed_t, dattn),
        left_t(normed_b, dbefore),
        left_t(hidden, dbranch),
    )
    return (dh + dmiddle, wgrads, (dgain_one, dgain_two))


def reduce_rows(grad):
    return lax.psum_scatter(grad.astype(BF), "fsdp", scatter_dimension=0, tiled=True)


def enc_split(wide, down):
    return (
        (wide[:, : 3 * D], wide[:, 3 * D : 4 * D], wide[:, 4 * D : 4 * D + FF], down),
        wide[:, 4 * D + FF :],
    )


def dec_split(wide, down):
    return (
        (wide[:, : 3 * DD], wide[:, 3 * DD : 4 * DD], wide[:, 4 * DD : 4 * DD + DFF], down),
        wide[:, 4 * DD + DFF :],
    )


def advance(weight, mom, avg, grad, rate):
    grad = grad + DECAY * weight
    buf = MOMENTUM * mom + grad
    new = weight - rate * (grad + MOMENTUM * buf)
    return (buf, new, AVERAGE * avg + (1.0 - AVERAGE) * new)


def arrange(valid, masked, scene_ids):
    slots = valid.shape[0]
    live = valid > 0
    kinds = jnp.stack([live & (masked == 0), live & (masked > 0), ~live], 1)
    index = jnp.arange(slots, dtype=jnp.int32)
    ranks = matmul((index[None, :] < index[:, None]).astype(BF), kinds.astype(BF)).astype(jnp.int32)
    n_seen, n_hid = [jnp.sum(kinds[:, i].astype(jnp.int32)) for i in range(2)]
    empty = ranks[:, 2]
    to_empty = jnp.where(empty < VIS - n_seen, n_seen + empty, n_seen + n_hid + empty)
    place = jnp.where(
        kinds[:, 0], ranks[:, 0], jnp.where(kinds[:, 1], VIS + ranks[:, 1], to_empty)
    )
    return (place[None, :] == index[:, None]).astype(BF), n_seen, n_hid


def exact_pick(pick, array):
    high = lax.reduce_precision(array, 8, 7)
    rest = array - high
    mid = lax.reduce_precision(rest, 8, 7)
    low = rest - mid
    return (
        matmul(pick, high.astype(BF)) + matmul(pick, mid.astype(BF)) + matmul(pick, low.astype(BF))
    )


def body(
    pixels,
    masked,
    valid,
    scene_ids,
    gsd_index,
    coords,
    embed,
    wide_enc,
    enc_down,
    wide_dec,
    dec_down,
    vectors,
    embed_mom,
    wide_enc_mom,
    enc_down_mom,
    wide_dec_mom,
    dec_down_mom,
    vector_mom,
    embed_avg,
    wide_enc_avg,
    enc_down_avg,
    wide_dec_avg,
    dec_down_avg,
    vector_avg,
):
    slots = pixels.shape[0]
    w_embed, w_enc, w_enc_down, w_dec, w_dec_down = [
        lax.all_gather(w.astype(BF), "fsdp", axis=0, tiled=True)
        for w in (embed, wide_enc, enc_down, wide_dec, dec_down)
    ]
    enc_weights, w_link = enc_split(w_enc, w_enc_down)
    dec_weights, w_head = dec_split(w_dec, w_dec_down)
    rows_ok = valid.astype(jnp.float32)
    flags = rows_ok * masked.astype(jnp.float32)
    bands = pixels.reshape(slots, BANDS, PATCH * PATCH)
    weighted = bands * rows_ok[:, None, None]
    band_sum = jnp.sum(weighted, axis=(0, 2))
    counts = jnp.stack([jnp.sum(rows_ok), jnp.sum(flags)])
    band_sq = jnp.sum(weighted * bands, axis=(0, 2))
    stats = lax.psum(jnp.concatenate([band_sum, band_sq, counts]), ("dp", "fsdp"))
    band_sum, band_sq, counts = stats[:3], stats[3:6], stats[6:]
    n_pix = counts[0] * (PATCH * PATCH)
    mean = band_sum / n_pix
    var = band_sq / n_pix - mean * mean
    count = counts[1]

    pick, n_seen, n_hid = arrange(valid, masked, scene_ids)
    picked_pixels = exact_pick(pick, pixels)
    small = matmul(
        pick, jnp.concatenate([(scene_ids % 2)[:, None], coords], 1).astype(BF)
    )
    odd, coord = small[:, 0], small[:, 1:]
    cent = picked_pixels.reshape(slots, BANDS, PATCH * PATCH) - mean[None, :, None]
    normed = (cent * lax.rsqrt(var + EPS)[None, :, None]).reshape(slots, PD)
    level = jnp.where(odd == 0, gsd_index[0], gsd_index[1]).astype(jnp.float32)
    scale = jnp.exp2(0.5 * level - 1.0)
    index = jnp.arange(slots, dtype=jnp.int32)
    kept = index[:VIS] < n_seen
    hidden_ok = index[:HID] < n_hid
    live = jnp.concatenate([kept, hidden_ok])
    keptf = kept.astype(jnp.float32)[:, None]
    allow = live[:, None] & (odd[:, None] == odd[None, :]) | (index[:, None] == index[None, :])
    bias = jnp.where(allow, 0.0, NEGATIVE)
    bias_enc, bias_dec = bias[:VIS, :VIS], bias[:, VIS:]

    gains_enc = (vectors[:D], vectors[D : 2 * D])
    gain_enc_out = vectors[2 * D : 3 * D]
    base = 3 * D
    gains_dec = (vectors[base : base + DD], vectors[base + DD : base + 2 * DD])
    gain_dec_out = vectors[base + 2 * DD : base + 3 * DD]
    token = vectors[base + 3 * DD :]

    inputs = normed[:VIS].astype(BF)
    h_start = matmul(inputs, w_embed) + positions(coord[:VIS], scale[:VIS], D)
    h_end, enc_saved = block_forward(h_start, enc_weights, gains_enc, bias_enc, HEADS, 0)
    encoded = layer_norm(h_end, gain_enc_out).astype(BF)
    seen_out = matmul(encoded, w_link)
    y_start = positions(coord, scale, DD) + jnp.concatenate(
        [jnp.where(kept[:, None], seen_out, token), jnp.broadcast_to(token, (HID, DD))]
    )
    y_end, dec_saved = block_forward(y_start, dec_weights, gains_dec, bias_dec, DHEADS, VIS)
    decoded = layer_norm(y_end, gain_dec_out).astype(BF)
    pred = matmul(decoded, w_head)
    flag = hidden_ok.astype(jnp.float32)
    losses, loss_pull = jax.vjp(lambda values: row_loss(values, normed[VIS:]), pred)
    local_loss = jnp.sum(flag * losses)
    dpred = loss_pull(flag / count)[0].astype(BF)
    head_grad = left_t(decoded, dpred)
    dy_end, dgain_dec_out = norm_back(y_end, gain_dec_out, right_t(dpred, w_head))
    dy_start, dec_grads, dgains_dec = block_backward(
        dec_saved, dy_end, dec_weights, gains_dec, bias_dec, DHEADS, VIS
    )
    picked = dy_start[:VIS] * keptf
    dtoken = jnp.sum(dy_start, 0) - jnp.sum(picked, 0)
    dseen = picked.astype(BF)
    link_grad = left_t(encoded, dseen)
    dh_end, dgain_enc_out = norm_back(h_end, gain_enc_out, right_t(dseen, w_link))
    dh_start, enc_grads, dgains_enc = block_backward(
        enc_saved, dh_end, enc_weights, gains_enc, bias_enc, HEADS, 0
    )
    embed_grad = left_t(inputs, dh_start.astype(BF))

    dec_parts = [
        reduce_rows(jnp.concatenate([dec_grads[0], dec_grads[1], dec_grads[2], head_grad], 1)),
        reduce_rows(dec_grads[3]),
    ]
    enc_parts = [
        reduce_rows(embed_grad),
        reduce_rows(jnp.concatenate([enc_grads[0], enc_grads[1], enc_grads[2], link_grad], 1)),
        reduce_rows(enc_grads[3]),
    ]
    dec_parts = lax.psum(tuple(dec_parts), "dp")
    enc_parts = lax.psum(tuple(enc_parts), "dp")
    shard_grads = [g.astype(F32) for g in (*enc_parts, *dec_parts)]
    vector_grad = jnp.concatenate(
        [
            dgains_enc[0],
            dgains_enc[1],
            dgain_enc_out,
            dgains_dec[0],
            dgains_dec[1],
            dgain_dec_out,
            dtoken,
        ]
    )
    vector_grad, loss_sum = lax.psum((vector_grad, local_loss), ("dp", "fsdp"))
    rate = STEP_UNIT * (PD * TOK_DEV * lax.axis_size("dp") * lax.axis_size("fsdp")) ** 0.5
    weights = (embed, wide_enc, enc_down, wide_dec, dec_down)
    moms = (embed_mom, wide_enc_mom, enc_down_mom, wide_dec_mom, dec_down_mom)
    avgs = (embed_avg, wide_enc_avg, enc_down_avg, wide_dec_avg, dec_down_avg)
    outs = []
    for number in range(5):
        buf, new, avg = advance(
            weights[number], moms[number], avgs[number], shard_grads[number], rate
        )
        outs += [buf, new, avg, new.astype(jnp.bfloat16)]
    return (*outs, *advance(vectors, vector_mom, vector_avg, vector_grad, rate), loss_sum, count)


def solution(mesh):
    both, rows = P(("dp", "fsdp")), P("fsdp", None)
    placed = (P(("dp", "fsdp"), None), both, both, both, both, P(("dp", "fsdp"), None))
    states = (rows,) * 5 + (P(),)
    return jax.shard_map(
        body,
        mesh=mesh,
        in_specs=placed + states * 3,
        out_specs=(rows,) * 20 + (P(),) * 5,
        check_vma=False,
    )
```

time: 1540 us -> 947 us (0.61)
  matrix products: 449 us -> 141 us
  waiting for transfers between devices: 761 us -> 498 us
  other arithmetic: 130 us -> 76 us
  Pallas kernels: 0 us -> 52.9 us
    reduce_scatter x11 -> x5, waiting for transfers between devices: 457 us -> 294 us  [reduce_rows(): lax.psum_scatter(grad.astype(BF), 'fsdp', scatter_dimension=0, tiled=True)]
    psum x1, waiting for transfers between devices: 267 us -> 119 us  [body(): enc_parts = lax.psum(tuple(enc_parts), 'dp')]
    dot_general x106 -> x10, matrix products: 180 us -> 39.8 us  [right_t(): lax.dot_general(left, right, (((1,), (1,)), ((), ())), preferred_element_...]
    dot_general x75 -> x11, matrix products: 120 us -> 33.6 us  [left_t(): lax.dot_general(left, right, (((0,), (0,)), ((), ())), preferred_element_...]
    dot_general x75 -> x20, matrix products: 149 us -> 67.5 us  [matmul(): return jnp.dot(left, right, preferred_element_type=jnp.float32)]
    pallas_call x0 -> x4, Pallas kernels: none -> 52.9 us  [the longest x2 32.5 us: attend_back(): pl.pallas_call(partial(attend_back_kernel, size), grid=(groups,), out_sha...]
    all_gather x5, waiting for transfers between devices: 36.3 us -> 85.5 us  [body(): lax.all_gather(w.astype(BF), 'fsdp', axis=0, tiled=True)]
    dynamic_update_slice x32 -> x0, other arithmetic: 21.3 us -> none  [attend_back(): grads = lax.map(one_head, (query, keys, values, dout))]
  transfers between devices with their start and end apart: 17 -> 11, of which waited for: 9 -> 8; matrix products, arithmetic and copies ran while one was open for 38% -> 17% of each run, Pallas kernels for 0% -> 2%
where the time goes in v1:
time: 947 us; the launch traced here: 941 us
  waiting for transfers between devices  498 us (53%)
  matrix products  141 us (15%)
  blocking collectives  88.1 us (9%)
  other arithmetic  76 us (8%)
  local copies, waits for them, and re-layouts  64.5 us (7%)
  Pallas kernels  52.9 us (6%)
  between operations  19.5 us (2%)
    reduce_scatter x5, waiting for transfers between devices, reduce_rows(): lax.psum_scatter(grad.astype(BF), 'fsdp', scatter_dimension=0, tiled=True)  294 us
    psum x1, waiting for transfers between devices, body(): enc_parts = lax.psum(tuple(enc_parts), 'dp')  119 us
    all_gather x5, waiting for transfers between devices, body(): lax.all_gather(w.astype(BF), 'fsdp', axis=0, tiled=True)  85.5 us
    dot_general x20, matrix products, matmul(): return jnp.dot(left, right, preferred_element_type=jnp.float32)  67.5 us
    psum x1, blocking collectives, body(): vector_grad, loss_sum = lax.psum((vector_grad, local_loss), ('dp', 'fsdp'))  45.7 us
    psum x1, blocking collectives, body(): lax.psum(jnp.concatenate([band_sum, band_sq, counts]), ('dp', 'fsdp'))  42.4 us
    dot_general x10, matrix products, right_t(): lax.dot_general(left, right, (((1,), (1,)), ((), ())), preferred_element_...  39.8 us
    dot_general x11, matrix products, left_t(): lax.dot_general(left, right, (((0,), (0,)), ((), ())), preferred_element_...  33.6 us
  transfers between devices with their start and end apart: 11, of which 8 were waited for; matrix products, arithmetic and copies ran while one was open for 17% of the time, Pallas kernels for 2%

profile of v1, /device:TPU:0, one launch (start us, length us, event | category | flops | bytes accessed | tf_op | source)
XLA Modules:
  0.0 940.9 jit_solution(15307707580941854650)
XLA Ops:
  31.9 42.4 %psum.56 = f32[8]{0:T(128)S(1)} all-reduce(f32[8]{0:T(128)S(1)} %pad_maximum_fusion.5), channel_id=1, replica_groups=mesh['dp'=4,'fsdp'=8] {'dp','fsdp'}, use_global_device_ids=true, to_apply=%region_8.9 | all-reduce | flops 8 | bytes 64 | tf_op jit(solution)/shard_map/psum | solution.py:333
  111.7 24.7 %all-gather.8.cloned.1.call-done = bf16[1024,8704]{1,0:T(8,128)(2,1)} async-done(((bf16[128,8704]{1,0:T(8,128)(2,1)}), bf16[1024,8704]{1,0:T(8,128)(2,1)}) %all-gather.8.cloned.1.call-update) | async-done | bytes 17825808 | tf_op jit(solution)/shard_map/all_gather | solution.py:321
  144.3 5.6 shard_map.423
  152.9 13.0 %multiply_convert_fusion.1 = (bf16[192,4096]{1,0:T(8,128)(2,1)}, f32[192,4096]{1,0:T(8,128)}, f32[192,4096]{1,0:T(8,128)}) fusion(bf16[1024,8704]{1,0:T(8,128)(2,1)} %all-gather.8.cloned.1.call-done, f32[192,1024]{1,0:T(8,128)S(1)} %get-tuple-element.156, f32[1024]{0:T(1024)S(1)} %get-tuple-element.132, f32[192]{0:T(256)S(1)} %fusion.117, ...), kind=kOutput, calls=%fused_computation.43 | convolution fusion | flops 1662517248 | bytes 17044992 | tf_op jit(solution)/shard_map/dot_general | solution.py:36
  166.0 27.3 %all-gather.10.cloned.1.call-done = bf16[4096,1024]{1,0:T(8,128)(2,1)} async-done(((bf16[512,1024]{1,0:T(8,128)(2,1)}), bf16[4096,1024]{1,0:T(8,128)(2,1)}) %all-gather.10.cloned.1.call-update) | async-done | bytes 8388624 | tf_op jit(solution)/shard_map/all_gather | solution.py:321
  193.3 5.8 fusion.162
  203.4 33.4 %all-gather.12.cloned.1.call-done = bf16[512,5056]{1,0:T(8,128)(2,1)} async-done(((bf16[64,5056]{1,0:T(8,128)(2,1)}), bf16[512,5056]{1,0:T(8,128)(2,1)}) %all-gather.12.cloned.1.call-update) | async-done | bytes 5177360 | tf_op jit(solution)/shard_map/all_gather | solution.py:321
  252.5 14.8 %shard_map.424 = (bf16[512,576]{1,0:T(8,128)(2,1)S(1)}, f32[4,4,576]{2,1,0:T(4,128)S(1)}) custom-call(bf16[512,576]{1,0:T(8,128)(2,1)S(1)} %copy-done.7, bf16[768,512]{1,0:T(8,128)(2,1)S(1)} %copy.134.k_ref, bf16[512,768]{1,0:T(8,128)(2,1)S(1)} %copy-done.6, f32[768,576]{1,0:T(8,128)S(1)} %copy-done), custom_call_target="tpu_custom_call" | custom-call | flops 3623878656 | bytes 1769472 | tf_op jit(solution)/shard_map/pallas_call | solution.py:102
  270.0 14.5 %multiply_convert_fusion = (bf16[576,2048]{1,0:T(8,128)(2,1)}, f32[576,2048]{1,0:T(8,128)}, f32[576,2048]{1,0:T(8,128)}) fusion(bf16[512,5056]{1,0:T(8,128)(2,1)} %all-gather.12.cloned.1.call-done, f32[576,512]{1,0:T(8,128)S(1)} %get-tuple-element.161, f32[512]{0:T(512)S(1)} %copy-done.136, f32[576]{0:T(1024)S(1)} %fusion.105, ...), kind=kOutput, calls=%fused_computation.16 | convolution fusion | flops 1285816320 | bytes 15079936 | tf_op jit(solution)/shard_map/dot_general | solution.py:36
  311.2 25.9 %shard_map.425 = (bf16[512,576]{1,0:T(8,128)(2,1)S(1)}, bf16[768,512]{1,0:T(8,128)(2,1)S(1)}, bf16[768,512]{1,0:T(8,128)(2,1)S(1)}) custom-call(bf16[512,576]{1,0:T(8,128)(2,1)S(1)} %copy-done.8, bf16[576,512]{1,0:T(8,128)(2,1)S(1)} %copy-done.12, bf16[768,512]{1,0:T(8,128)(2,1)S(1)} %copy-done.5, bf16[512,768]{1,0:T(8,128)(2,1)} %bitcast.72, ...), custom_call_target="tpu_custom_call" | custom-call | flops 9059696640 | bytes 1769472 | tf_op jit(solution)/shard_map/pallas_call | solution.py:171
  351.7 7.5 add_convert_fusion.1
  359.2 7.6 multiply_reduce_fusion.11
  374.7 6.6 shard_map.426
  384.9 6.3 multiply_reduce_fusion.12
  394.3 5.3 convolution_convert_fusion.4
  417.3 5.8 convolution_convert_fusion
  436.7 6.9 pad_maximum_fusion
  443.8 34.1 %reduce-scatter.14.cloned.1.call-done = bf16[256,512]{1,0:T(8,128)(2,1)} async-done(((bf16[2048,512]{1,0:T(8,128)(2,1)}), bf16[256,512]{1,0:T(8,128)(2,1)}) %reduce-scatter.14.cloned.1.call-update) | async-done | bytes 262160 | tf_op jit(solution)/shard_map/reduce_scatter | solution.py:244
  477.9 60.4 %reduce-scatter.12.cloned.1.call-done = bf16[64,5056]{1,0:T(8,128)(2,1)} async-done(((bf16[512,5056]{1,0:T(8,128)(2,1)}), bf16[64,5056]{1,0:T(8,128)(2,1)}) %reduce-scatter.12.cloned.1.call-update) | async-done | bytes 647184 | tf_op jit(solution)/shard_map/reduce_scatter | solution.py:244
  538.3 74.8 %reduce-scatter.10.cloned.1.call-done = bf16[512,1024]{1,0:T(8,128)(2,1)} async-done(((bf16[4096,1024]{1,0:T(8,128)(2,1)}), bf16[512,1024]{1,0:T(8,128)(2,1)}) %reduce-scatter.10.cloned.1.call-update) | async-done | bytes 1048592 | tf_op jit(solution)/shard_map/reduce_scatter | solution.py:244
  613.0 124.9 %reduce-scatter.8.cloned.1.call-done = bf16[128,8704]{1,0:T(8,128)(2,1)} async-done(((bf16[1024,8704]{1,0:T(8,128)(2,1)}), bf16[128,8704]{1,0:T(8,128)(2,1)}) %reduce-scatter.8.cloned.1.call-update) | async-done | bytes 2228240 | tf_op jit(solution)/shard_map/reduce_scatter | solution.py:244
  739.9 45.7 %all-reduce.4 = (f32[5120]{0:T(1024)S(1)}, f32[]{:T(128)}) all-reduce(f32[5120]{0:T(1024)S(1)} %constant_dynamic-update-slice_fusion, f32[]{:T(128)} %select_reduce_fusion), channel_id=1, replica_groups=mesh['dp'=4,'fsdp'=8] {'dp','fsdp'}, use_global_device_ids=true, to_apply=%region_52.53 | all-reduce | flops 5121 | bytes 40968 | tf_op jit(solution)/shard_map/psum | solution.py:419
  786.2 118.5 %all-reduce.8.cloned.1.call-done = (bf16[96,1024]{1,0:T(8,128)(2,1)}, bf16[128,8704]{1,0:T(8,128)(2,1)}, bf16[512,1024]{1,0:T(8,128)(2,1)}, bf16[64,5056]{1,0:T(8,128)(2,1)}, bf16[256,512]{1,0:T(8,128)(2,1)}) async-done(((bf16[96,1024]{1,0:T(8,128)(2,1)}, bf16[128,8704]{1,0:T(8,128)(2,1)}, bf16[512,1024]{1,0:T(8,128)(2,1)}, bf16[64,5056]{1,0:T(8,128)(2,1)}, bf16[256,512]{1,0:T(8,128)(2,1)}), ...) | async-done | bytes 4382736 | tf_op jit(solution)/shard_map/psum | solution.py:406
  908.9 8.0 fusion.142
  (513 shorter events, 201.5 us)
Async XLA Ops:
  7.2 101.3 %all-gather.6.cloned.1.call-start = ((), (), s32[]{:S(2)}) async-start(), calls=%async_computation.5 | async-start | bytes 1769472 | tf_op jit(solution)/shard_map/all_gather | solution.py:321
  9.0 127.4 %all-gather.8.cloned.1.call-start = ((), (), s32[]{:S(2)}) async-start(), calls=%async_computation.6 | async-start | bytes 20054016 | tf_op jit(solution)/shard_map/all_gather | solution.py:321
  12.9 180.4 %all-gather.10.cloned.1.call-start = ((), (), s32[]{:S(2)}) async-start(), calls=%async_computation.7 | async-start | bytes 9437184 | tf_op jit(solution)/shard_map/all_gather | solution.py:321
  15.6 221.1 %all-gather.12.cloned.1.call-start = ((), (), s32[]{:S(2)}) async-start(), calls=%async_computation.8 | async-start | bytes 5898240 | tf_op jit(solution)/shard_map/all_gather | solution.py:321
  18.1 266.4 %all-gather.14.cloned.1.call-start = ((), (), s32[]{:S(2)}) async-start(), calls=%async_computation.9 | async-start | bytes 2359296 | tf_op jit(solution)/shard_map/all_gather | solution.py:321
  18.9 424.9 %reduce-scatter.6.cloned.1.call-start = ((), (), s32[]{:S(2)}) async-start(), calls=%async_computation.10 | async-start | bytes 1769472 | tf_op jit(solution)/shard_map/reduce_scatter | solution.py:244
  29.9 172.5 %copy-start.103 = (f32[512]{0:T(512)}, f32[512]{0:T(512)S(1)}, u32[]{:S(2)}) copy-start(f32[512]{0:T(512)S(1)} %get-tuple-element.129) | copy-start | bytes 6148
  394.2 83.7 %reduce-scatter.14.cloned.1.call-start = ((), (), s32[]{:S(2)}) async-start(), calls=%async_computation.14 | async-start | bytes 2359296 | tf_op jit(solution)/shard_map/reduce_scatter | solution.py:244
  399.6 138.7 %reduce-scatter.12.cloned.1.call-start = ((), (), s32[]{:S(2)}) async-start(), calls=%async_computation.13 | async-start | bytes 5898240 | tf_op jit(solution)/shard_map/reduce_scatter | solution.py:244
  415.7 197.3 %reduce-scatter.10.cloned.1.call-start = ((), (), s32[]{:S(2)}) async-start(), calls=%async_computation.12 | async-start | bytes 9437184 | tf_op jit(solution)/shard_map/reduce_scatter | solution.py:244
  423.1 314.8 %reduce-scatter.8.cloned.1.call-start = ((), (), s32[]{:S(2)}) async-start(), calls=%async_computation.11 | async-start | bytes 20054016 | tf_op jit(solution)/shard_map/reduce_scatter | solution.py:244
  443.6 294.4 %copy-start.141 = (f32[1024]{0:T(1024)S(1)}, f32[1024]{0:T(1024)}, u32[]{:S(2)}) copy-start(f32[1024]{0:T(1024)} %get-tuple-element.57) | copy-start | bytes 12292
  443.6 294.4 %copy-start.140 = (f32[1024]{0:T(1024)S(1)}, f32[1024]{0:T(1024)}, u32[]{:S(2)}) copy-start(f32[1024]{0:T(1024)} %get-tuple-element.55) | copy-start | bytes 12292
  443.6 294.4 %copy-start.139 = (f32[1024]{0:T(1024)S(1)}, f32[1024]{0:T(1024)}, u32[]{:S(2)}) copy-start(f32[1024]{0:T(1024)} %get-tuple-element.53) | copy-start | bytes 12292
  443.6 294.4 %copy-start.144 = (f32[512]{0:T(512)S(1)}, f32[512]{0:T(512)}, u32[]{:S(2)}) copy-start(f32[512]{0:T(512)} %get-tuple-element.45) | copy-start | bytes 6148
  443.6 294.5 %copy-start.143 = (f32[512]{0:T(512)S(1)}, f32[512]{0:T(512)}, u32[]{:S(2)}) copy-start(f32[512]{0:T(512)} %get-tuple-element.49) | copy-start | bytes 6148
  443.7 294.5 %copy-start.142 = (f32[512]{0:T(512)S(1)}, f32[512]{0:T(512)}, u32[]{:S(2)}) copy-start(f32[512]{0:T(512)} %get-tuple-element.47) | copy-start | bytes 6148
  443.7 294.5 %copy-start.113 = (f32[576]{0:T(1024)S(1)}, f32[576]{0:T(1024)}, u32[]{:S(2)}) copy-start(f32[576]{0:T(1024)} %get-tuple-element.125) | copy-start | bytes 6916
  443.7 294.5 %copy-start.114 = (f32[576]{0:T(1024)S(1)}, f32[576]{0:T(1024)}, u32[]{:S(2)}) copy-start(f32[576]{0:T(1024)} %get-tuple-element.123) | copy-start | bytes 6916
  443.7 294.5 %copy-start.118 = (pred[576]{0:T(1024)(128)(4,1)S(1)}, pred[576]{0:T(1024)(128)(4,1)}, u32[]{:S(2)}) copy-start(pred[576]{0:T(1024)(128)(4,1)} %copy-done.117) | copy-start | bytes 1732
  443.7 461.0 %all-reduce.8.cloned.1.call-start = ((), (), s32[]{:S(2)}) async-start(), calls=%async_computation.15 | async-start | bytes 8781824 | tf_op jit(solution)/shard_map/psum | solution.py:406
  738.0 47.6 %copy-start.101 = (f32[5120]{0:T(1024)S(1)}, f32[5120]{0:T(1024)}, u32[]{:S(2)}) copy-start(f32[5120]{0:T(1024)} %param.41) | copy-start | bytes 61444
  738.0 166.8 %copy-start.70 = (f32[96,1024]{1,0:T(8,128)S(1)}, f32[96,1024]{1,0:T(8,128)}, u32[]{:S(2)}) copy-start(f32[96,1024]{1,0:T(8,128)} %param.30) | copy-start | bytes 1179652
  738.0 178.9 %slice-start = ((s8[4456448]{0:T(1024)(128)(4,1)}), s8[262144]{0:T(1024)(128)(4,1)S(1)}, s32[]{:S(2)}) async-start(s8[4456448]{0:T(1024)(128)(4,1)} %bitcast.62), calls=%async_computation.16 | async-start | bytes 524288
  (145 other events, 1055.8 us)
Sparse Core Ops, SparseCore 0:
  10.5 28.3 all-gather.5
  41.4 94.9 all-gather.7
  138.9 54.3 all-gather.9
  195.6 41.1 all-gather.11
  239.1 27.8 all-gather.13
  394.3 38.4 reduce-scatter.5
  436.7 41.1 reduce-scatter.13
  481.6 56.5 reduce-scatter.11
  541.7 71.2 reduce-scatter.9
  617.0 120.9 reduce-scatter.7
  741.0 163.7 all-reduce.7

commit v2 on v1

--- a/solution.py
+++ b/solution.py
@@ -197,6 +197,370 @@
     )(query.T, query, keys, keys.T, values, dmixed, dmixed.T, bias, lse)
 
 
+MESH = pl.DeviceIdType.MESH
+UNIT = 1024
+HALF = UNIT // 2
+ROWS = 128
+
+
+def put(source, target, send, recv, device):
+    return pltpu.make_async_remote_copy(
+        src_ref=source,
+        dst_ref=target,
+        send_sem=send,
+        recv_sem=recv,
+        device_id=device,
+        device_id_type=MESH,
+    )
+
+
+def sum_kernel(units, vec_ref, *refs):
+    n_left = max(u[0] for u in units) + 1
+    n_right = max(u[2] for u in units) + 1
+    lefts, rights = refs[:n_left], refs[n_left : n_left + n_right]
+    out_ref, vec_out = refs[n_left + n_right : n_left + n_right + 2]
+    (
+        xo,
+        xp,
+        yo,
+        yp,
+        a_out,
+        a_in,
+        b_out,
+        b_in,
+        sums,
+        z_out,
+        z_one,
+        z_two,
+        v_in,
+        v_out,
+        load_sem,
+        swap_send,
+        swap_recv,
+        a_send,
+        a_recv,
+        b_send,
+        b_recv,
+        z_send,
+        z_recv,
+        v_send,
+        v_recv,
+    ) = refs[n_left + n_right + 2 :]
+    count = len(units)
+    z, f = lax.axis_index("dp"), lax.axis_index("fsdp")
+    core, place = f % 2, f // 2
+    x, y = place % 2, place // 2
+    partner = (z, f + 1 - 2 * core)
+    x_side = (z, f + 2 - 4 * x)
+    y_side = (z, f + 4 - 8 * y)
+    at_x, at_y, at_far = place + 1 - 2 * x, place + 2 - 4 * y, 3 - place
+    low = z < 2
+    outer = (z == 0) | (z == 3)
+    inner = (z == 1) | (z == 2)
+    inward = (jnp.where(low, 1, 2), f)
+    across = (3 - z, f)
+    outward = (jnp.where(low, 0, 3), f)
+
+    barrier = pltpu.get_barrier_semaphore()
+    for device in (partner, x_side, y_side):
+        pl.semaphore_signal(barrier, inc=1, device_id=device, device_id_type=MESH)
+
+    @pl.when(outer)
+    def _():
+        pl.semaphore_signal(barrier, inc=1, device_id=inward, device_id_type=MESH)
+        pl.semaphore_wait(barrier, 4)
+
+    @pl.when(inner)
+    def _():
+        pl.semaphore_signal(barrier, inc=1, device_id=across, device_id_type=MESH)
+        pl.semaphore_signal(barrier, inc=1, device_id=outward, device_id_type=MESH)
+        pl.semaphore_wait(barrier, 5)
+
+    for number, (left, sub, right, column) in enumerate(units):
+        rows, cols = pl.ds(sub * ROWS, ROWS), pl.ds(column, UNIT)
+        whole = pl.ds(0, rights[right].shape[0])
+        put(
+            lefts[left].at[:, 1 - core, rows],
+            xp.at[number],
+            swap_send.at[number, 0],
+            swap_recv.at[number, 0],
+            partner,
+        ).start()
+        put(
+            rights[right].at[whole, cols],
+            yp.at[number],
+            swap_send.at[number, 1],
+            swap_recv.at[number, 1],
+            partner,
+        ).start()
+        pltpu.make_async_copy(
+            lefts[left].at[:, core, rows], xo.at[number], load_sem.at[number, 0]
+        ).start()
+        pltpu.make_async_copy(
+            rights[right].at[whole, cols], yo.at[number], load_sem.at[number, 1]
+        ).start()
+
+    first, second = pl.ds(0, HALF), pl.ds(HALF, HALF)
+
+    def swap(u, side, source, target):
+        return put(source, target, swap_send.at[u, side], swap_recv.at[u, side], partner)
+
+    def part(u, owner, columns):
+        return matmul(xo[u, owner], yo[u, :, columns]) + matmul(xp[u, owner], yp[u, :, columns])
+
+    def copy_a(u, side):
+        slot = u % a_out.shape[0]
+        return put(
+            a_out.at[slot, side],
+            a_in.at[u, side],
+            a_send.at[slot, side],
+            a_recv.at[u, side],
+            (x_side, y_side)[side],
+        )
+
+    def copy_b(u, side):
+        slot = u % b_out.shape[0]
+        return put(
+            b_out.at[slot, side],
+            b_in.at[u, side],
+            b_send.at[slot, side],
+            b_recv.at[u, side],
+            (y_side, x_side)[side],
+        )
+
+    def copy_in(u):
+        return put(z_out.at[u], z_one.at[u], z_send.at[u, 0], z_recv.at[u, 0], inward)
+
+    def copy_across(u):
+        return put(z_out.at[u], z_two.at[u], z_send.at[u, 0], z_recv.at[u, 1], across)
+
+    def copy_out(u):
+        return put(out_ref.at[u], z_one.at[u], z_send.at[u, 1], z_recv.at[u, 0], outward)
+
+    def copy_v(step, device):
+        return put(v_out.at[step], v_in.at[step], v_send.at[step], v_recv.at[step], device)
+
+    def step(i, _):
+        def stage(lag, also=None):
+            u = i - lag
+            ok = (u >= 0) & (u < count)
+            if also is not None:
+                ok = ok & also
+            return u, pl.when(ok)
+
+        u0, when = stage(0)
+
+        @when
+        def _():
+            u = u0
+            pltpu.make_async_copy(xo.at[u], xo.at[u], load_sem.at[u, 0]).wait()
+            pltpu.make_async_copy(yo.at[u], yo.at[u], load_sem.at[u, 1]).wait()
+            swap(u, 0, xo.at[u], xp.at[u]).wait()
+            swap(u, 1, yo.at[u], yp.at[u]).wait()
+
+            @pl.when(u >= a_out.shape[0])
+            def _():
+                for side in range(2):
+                    copy_a(u - a_out.shape[0], side).wait_send()
+
+            slot = u % a_out.shape[0]
+            a_out[slot, 0, 0] = part(u, at_x, first).astype(BF)
+            a_out[slot, 0, 1] = part(u, at_far, first).astype(BF)
+            copy_a(u, 0).start()
+            a_out[slot, 1, 0] = part(u, at_y, second).astype(BF)
+            a_out[slot, 1, 1] = part(u, at_far, second).astype(BF)
+            copy_a(u, 1).start()
+
+        u1, when = stage(1)
+
+        @when
+        def _():
+            u = u1
+            slot = u % b_out.shape[0]
+
+            @pl.when(u >= b_out.shape[0])
+            def _():
+                for side in range(2):
+                    copy_b(u - b_out.shape[0], side).wait_send()
+
+            copy_a(u, 0).wait_recv()
+            b_out[slot, 0] = (part(u, at_y, first) + a_in[u, 0, 1].astype(F32)).astype(BF)
+            copy_b(u, 0).start()
+            copy_a(u, 1).wait_recv()
+            b_out[slot, 1] = (part(u, at_x, second) + a_in[u, 1, 1].astype(F32)).astype(BF)
+            copy_b(u, 1).start()
+
+        u2, when = stage(2)
+
+        @when
+        def _():
+            u = u2
+            copy_b(u, 0).wait_recv()
+            copy_b(u, 1).wait_recv()
+            for side, columns in enumerate((first, second)):
+                total = part(u, place, columns) + a_in[u, side, 0].astype(F32)
+                sums[u % 2, :, columns] = total + b_in[u, side].astype(F32)
+
+            @pl.when(outer)
+            def _():
+                z_out[u] = sums[u % 2].astype(BF)
+                copy_in(u).start()
+
+        u3, when = stage(3, inner)
+
+        @when
+        def _():
+            u = u3
+            copy_in(u).wait_recv()
+            z_out[u] = (sums[u % 2] + z_one[u].astype(F32)).astype(BF)
+            copy_across(u).start()
+
+        u4, when = stage(4, inner)
+
+        @when
+        def _():
+            u = u4
+            copy_across(u).wait_recv()
+            out_ref[u] = (z_out[u].astype(F32) + z_two[u].astype(F32)).astype(BF)
+            copy_out(u).start()
+
+        u5, when = stage(6, outer)
+
+        @when
+        def _():
+            u = u5
+            copy_out(u).wait_recv()
+            out_ref[u] = z_one[u]
+
+        for number, device in enumerate((partner, x_side, y_side)):
+
+            @pl.when(i == number)
+            def _():
+                if number == 0:
+                    v_out[0] = vec_ref[...]
+                else:
+                    copy_v(number - 1, (partner, x_side, y_side)[number - 1]).wait_recv()
+                    v_out[number] = v_out[number - 1] + v_in[number - 1]
+                copy_v(number, device).start()
+
+        @pl.when(i == 3)
+        def _():
+            copy_v(2, y_side).wait_recv()
+            v_out[3] = v_out[2] + v_in[2]
+
+            @pl.when(outer)
+            def _():
+                copy_v(3, inward).start()
+
+        @pl.when((i == 4) & inner)
+        def _():
+            copy_v(3, inward).wait_recv()
+            v_out[4] = v_out[3] + v_in[3]
+            copy_v(4, across).start()
+
+        @pl.when((i == 5) & inner)
+        def _():
+            copy_v(4, across).wait_recv()
+            v_out[5] = v_out[4] + v_in[4]
+            copy_v(5, outward).start()
+            vec_out[...] = v_out[5]
+
+        @pl.when((i == 7) & outer)
+        def _():
+            copy_v(5, outward).wait_recv()
+            vec_out[...] = v_in[5]
+
+        return 0
+
+    lax.fori_loop(0, count + 6, step, 0)
+
+    for u in range(count - a_out.shape[0], count):
+        for side in range(2):
+            copy_a(u, side).wait_send()
+    for u in range(count - b_out.shape[0], count):
+        for side in range(2):
+            copy_b(u, side).wait_send()
+    for number, device in enumerate((partner, x_side, y_side)):
+        copy_v(number, device).wait_send()
+
+    @pl.when(outer)
+    def _():
+        copy_v(3, inward).wait_send()
+
+        def drain(u, _):
+            copy_in(u).wait_send()
+            return 0
+
+        lax.fori_loop(0, count, drain, 0)
+
+    @pl.when(inner)
+    def _():
+        copy_v(4, across).wait_send()
+        copy_v(5, outward).wait_send()
+
+        def drain(u, _):
+            copy_across(u).wait_send()
+            copy_out(u).wait_send()
+            return 0
+
+        lax.fori_loop(0, count, drain, 0)
+
+
+def sum_products(units, lefts, rights, vec):
+    count, depth = len(units), rights[0].shape[0]
+    lefts = [a.reshape(4, 2, a.shape[0] // 8, depth) for a in lefts]
+    slots = 3
+    dma = pltpu.SemaphoreType.DMA
+    return pl.pallas_call(
+        partial(sum_kernel, units),
+        out_shape=(
+            jax.ShapeDtypeStruct((count, ROWS, UNIT), BF),
+            jax.ShapeDtypeStruct(vec.shape, F32),
+        ),
+        in_specs=[pl.BlockSpec(memory_space=pltpu.VMEM)]
+        + [pl.BlockSpec(memory_space=pl.ANY)] * (len(lefts) + len(rights)),
+        out_specs=(
+            pl.BlockSpec(memory_space=pltpu.VMEM),
+            pl.BlockSpec(memory_space=pltpu.VMEM),
+        ),
+        scratch_shapes=[
+            pltpu.VMEM((count, 4, ROWS, depth), BF),
+            pltpu.VMEM((count, 4, ROWS, depth), BF),
+            pltpu.VMEM((count, depth, UNIT), BF),
+            pltpu.VMEM((count, depth, UNIT), BF),
+            pltpu.VMEM((slots, 2, 2, ROWS, HALF), BF),
+            pltpu.VMEM((count, 2, 2, ROWS, HALF), BF),
+            pltpu.VMEM((slots, 2, ROWS, HALF), BF),
+            pltpu.VMEM((count, 2, ROWS, HALF), BF),
+            pltpu.VMEM((2, ROWS, UNIT), F32),
+            pltpu.VMEM((count, ROWS, UNIT), BF),
+            pltpu.VMEM((count, ROWS, UNIT), BF),
+            pltpu.VMEM((count, ROWS, UNIT), BF),
+            pltpu.VMEM((6, *vec.shape), F32),
+            pltpu.VMEM((6, *vec.shape), F32),
+            dma((count, 2)),
+            dma((count, 2)),
+            dma((count, 2)),
+            dma((slots, 2)),
+            dma((count, 2)),
+            dma((slots, 2)),
+            dma((count, 2)),
+            dma((count, 2)),
+            dma((count, 2)),
+            dma((6,)),
+            dma((6,)),
+        ],
+        compiler_params=pltpu.CompilerParams(
+            collective_id=0, has_side_effects=True, vmem_limit_bytes=58 * 2**20
+        ),
+        cost_estimate=pl.CostEstimate(
+            flops=8 * 2 * count * ROWS * UNIT * depth,
+            bytes_accessed=300 * 2**20,
+            transcendentals=0,
+        ),
+    )(vec, *lefts, *rights)
+
+
 def block_forward(h, weights, gains, bias, heads, skip):
     wqkv, wout, wup, wdown = weights
     width = h.shape[1]
@@ -231,17 +595,35 @@
         dmiddle = jnp.pad(dmiddle, ((skip, 0), (0, 0)))
     dqkv = jnp.concatenate([dquery, dkeys, dvalues], 1)
     dh, dgain_one = norm_back(h, gains[0], right_t(dqkv, wqkv))
-    wgrads = (
-        left_t(normed_a, dqkv),
-        matmul(mixed_t, dattn),
-        left_t(normed_b, dbefore),
-        left_t(hidden, dbranch),
-    )
-    return (dh + dmiddle, wgrads, (dgain_one, dgain_two))
+    factors = ((normed_a.T, dqkv), (mixed_t, dattn), (normed_b.T, dbefore), (hidden.T, dbranch))
+    return (dh + dmiddle, factors, (dgain_one, dgain_two))
 
 
 def reduce_rows(grad):
     return lax.psum_scatter(grad.astype(BF), "fsdp", scatter_dimension=0, tiled=True)
+
+
+def sum_encoder(factors, encoded, dseen, inputs, dh_low, vector_grad, local_loss):
+    lefts = [pair[0] for pair in factors] + [encoded.T]
+    owners = lax.axis_size("fsdp")
+    first = inputs.T.reshape(owners, PD // owners, VIS)
+    lefts.append(jnp.pad(first, ((0, 0), (0, ROWS - PD // owners), (0, 0))).reshape(-1, VIS))
+    rights = [pair[1] for pair in factors] + [jnp.pad(dseen, ((0, 0), (0, UNIT - DD))), dh_low]
+    units = [(2, 0, 2, UNIT * n) for n in range(FF // UNIT)]
+    units += [(3, n, 3, 0) for n in range(FF // owners // ROWS)]
+    units += [(0, 0, 0, UNIT * n) for n in range(3 * D // UNIT)]
+    units += [(1, 0, 1, 0), (4, 0, 4, 0), (5, 0, 5, 0)]
+    length = vector_grad.shape[0]
+    rows = -(-(length + 1) // (8 * LANES)) * 8
+    vec = jnp.concatenate(
+        [vector_grad, local_loss[None], jnp.zeros((rows * LANES - length - 1,), F32)]
+    )
+    grads, vec = sum_products(tuple(units), lefts, rights, vec.reshape(rows, LANES))
+    vec = vec.reshape(-1)
+    up, down, qkv = grads[:4], grads[4:8], grads[8:11]
+    wide = jnp.concatenate([*qkv, grads[11], *up, grads[12][:, :DD]], 1)
+    parts = (grads[13][: PD // owners], wide, down.reshape(-1, D))
+    return parts, vec[:length], vec[length]
 
 
 def enc_split(wide, down):
@@ -378,33 +760,24 @@
     losses, loss_pull = jax.vjp(lambda values: row_loss(values, normed[VIS:]), pred)
     local_loss = jnp.sum(flag * losses)
     dpred = loss_pull(flag / count)[0].astype(BF)
-    head_grad = left_t(decoded, dpred)
     dy_end, dgain_dec_out = norm_back(y_end, gain_dec_out, right_t(dpred, w_head))
-    dy_start, dec_grads, dgains_dec = block_backward(
+    dy_start, dec_factors, dgains_dec = block_backward(
         dec_saved, dy_end, dec_weights, gains_dec, bias_dec, DHEADS, VIS
     )
+    dec_grads = [matmul(*pair).astype(BF) for pair in dec_factors]
+    head_grad = left_t(decoded, dpred).astype(BF)
+    wide_dec_grad = jnp.concatenate([dec_grads[0], dec_grads[1], dec_grads[2], head_grad], 1)
+    dec_parts = (wide_dec_grad, dec_grads[3])
+    dy_start, dec_parts = lax.optimization_barrier((dy_start, dec_parts))
+    dec_parts = lax.psum(tuple(reduce_rows(g) for g in dec_parts), "dp")
     picked = dy_start[:VIS] * keptf
     dtoken = jnp.sum(dy_start, 0) - jnp.sum(picked, 0)
     dseen = picked.astype(BF)
-    link_grad = left_t(encoded, dseen)
     dh_end, dgain_enc_out = norm_back(h_end, gain_enc_out, right_t(dseen, w_link))
-    dh_start, enc_grads, dgains_enc = block_backward(
+    dh_start, enc_factors, dgains_enc = block_backward(
         enc_saved, dh_end, enc_weights, gains_enc, bias_enc, HEADS, 0
     )
-    embed_grad = left_t(inputs, dh_start.astype(BF))
-
-    dec_parts = [
-        reduce_rows(jnp.concatenate([dec_grads[0], dec_grads[1], dec_grads[2], head_grad], 1)),
-        reduce_rows(dec_grads[3]),
-    ]
-    enc_parts = [
-        reduce_rows(embed_grad),
-        reduce_rows(jnp.concatenate([enc_grads[0], enc_grads[1], enc_grads[2], link_grad], 1)),
-        reduce_rows(enc_grads[3]),
-    ]
-    dec_parts = lax.psum(tuple(dec_parts), "dp")
-    enc_parts = lax.psum(tuple(enc_parts), "dp")
-    shard_grads = [g.astype(F32) for g in (*enc_parts, *dec_parts)]
+    dh_low = dh_start.astype(BF)
     vector_grad = jnp.concatenate(
         [
             dgains_enc[0],
@@ -416,7 +789,25 @@
             dtoken,
         ]
     )
-    vector_grad, loss_sum = lax.psum((vector_grad, local_loss), ("dp", "fsdp"))
+    if (lax.axis_size("dp"), lax.axis_size("fsdp")) == (4, 8):
+        enc_parts, vector_grad, loss_sum = sum_encoder(
+            enc_factors, encoded, dseen, inputs, dh_low, vector_grad, local_loss
+        )
+    else:
+        enc_grads = [matmul(*pair).astype(BF) for pair in enc_factors]
+        link_grad = left_t(encoded, dseen).astype(BF)
+        enc_parts = lax.psum(
+            (
+                reduce_rows(left_t(inputs, dh_low)),
+                reduce_rows(
+                    jnp.concatenate([enc_grads[0], enc_grads[1], enc_grads[2], link_grad], 1)
+                ),
+                reduce_rows(enc_grads[3]),
+            ),
+            "dp",
+        )
+        vector_grad, loss_sum = lax.psum((vector_grad, local_loss), ("dp", "fsdp"))
+    shard_grads = [g.astype(F32) for g in (*enc_parts, *dec_parts)]
     rate = STEP_UNIT * (PD * TOK_DEV * lax.axis_size("dp") * lax.axis_size("fsdp")) ** 0.5
     weights = (embed, wide_enc, enc_down, wide_dec, dec_down)
     moms = (embed_mom, wide_enc_mom, enc_down_mom, wide_dec_mom, dec_down_mom)

time: 947 us -> 708 us (0.75)
  waiting for transfers between devices: 498 us -> 108 us
  Pallas kernels: 52.9 us -> 227 us
  blocking collectives: 88.1 us -> 42.5 us
  local copies, waits for them, and re-layouts: 64.5 us -> 80.9 us
    reduce_scatter x5 -> x2, waiting for transfers between devices: 294 us -> 0.01 us  [reduce_rows(): lax.psum_scatter(grad.astype(BF), 'fsdp', scatter_dimension=0, tiled=True)]
    pallas_call x0 -> x1, Pallas kernels: none -> 175 us  [sum_products(): pl.pallas_call(partial(sum_kernel, units), out_shape=(jax.ShapeDtypeStruc...]
    psum x1, waiting for transfers between devices: 119 us -> 36.9 us  [body(): dec_parts = lax.psum(tuple((reduce_rows(g) for g in dec_parts)), 'dp')]
    psum x1 -> x0, blocking collectives: 45.7 us -> none  [body(): vector_grad, loss_sum = lax.psum((vector_grad, local_loss), ('dp', 'fsdp'))]
    dot_general x11 -> x3, matrix products: 33.6 us -> 6.15 us  [left_t(): lax.dot_general(left, right, (((0,), (0,)), ((), ())), preferred_element_...]
    dot_general x20 -> x22, matrix products: 67.5 us -> 85.9 us  [matmul(): return jnp.dot(left, right, preferred_element_type=jnp.float32)]
    all_gather x5, waiting for transfers between devices: 85.5 us -> 70.7 us  [body(): lax.all_gather(w.astype(BF), 'fsdp', axis=0, tiled=True)]
    unnamed x322 -> x226, local copies, waits for them, and re-layouts: 32.8 us -> 32.2 us
  transfers between devices with their start and end apart: 11 -> 8, of which waited for: 8 -> 4; matrix products, arithmetic and copies ran while one was open for 17% -> 28% of each run, Pallas kernels for 2% -> 29%
where the time goes in v2:
time: 708 us; the launch traced here: 702 us
  Pallas kernels  227 us (32%)
  matrix products  139 us (20%)
  waiting for transfers between devices  108 us (15%)
  other arithmetic  83.2 us (12%)
  local copies, waits for them, and re-layouts  80.9 us (11%)
  blocking collectives  42.5 us (6%)
  between operations  20.4 us (3%)
    pallas_call x1, Pallas kernels, sum_products(): pl.pallas_call(partial(sum_kernel, units), out_shape=(jax.ShapeDtypeStruc...  175 us
    dot_general x22, matrix products, matmul(): return jnp.dot(left, right, preferred_element_type=jnp.float32)  85.9 us
    all_gather x5, waiting for transfers between devices, body(): lax.all_gather(w.astype(BF), 'fsdp', axis=0, tiled=True)  70.7 us
    dot_general x10, matrix products, right_t(): lax.dot_general(left, right, (((1,), (1,)), ((), ())), preferred_element_...  47.4 us
    psum x1, blocking collectives, body(): lax.psum(jnp.concatenate([band_sum, band_sq, counts]), ('dp', 'fsdp'))  42.5 us
    psum x1, waiting for transfers between devices, body(): dec_parts = lax.psum(tuple((reduce_rows(g) for g in dec_parts)), 'dp')  36.9 us
    pallas_call x2, Pallas kernels, attend_back(): pl.pallas_call(partial(attend_back_kernel, size), grid=(groups,), out_sha...  32.2 us
    unnamed x226, local copies, waits for them, and re-layouts  32.2 us
  transfers between devices with their start and end apart: 8, of which 4 were waited for; matrix products, arithmetic and copies ran while one was open for 28% of the time, Pallas kernels for 29%

profile of v2, /device:TPU:0, one launch (start us, length us, event | category | flops | bytes accessed | tf_op | source)
XLA Modules:
  0.0 701.6 jit_solution(14272819890932299786)
XLA Ops:
  9.0 4.0 convert_element_type.222
  33.8 42.5 %psum.21 = f32[8]{0:T(128)S(1)} all-reduce(f32[8]{0:T(128)S(1)} %pad_maximum_fusion.2), channel_id=1, replica_groups=mesh['dp'=4,'fsdp'=8] {'dp','fsdp'}, use_global_device_ids=true, to_apply=%region_8.9 | all-reduce | flops 8 | bytes 64 | tf_op jit(solution)/shard_map/psum | solution.py:715
  109.8 4.6 multiply_sine_fusion.1
  118.5 18.0 %all-gather.8.cloned.1.call-done = bf16[1024,8704]{1,0:T(8,128)(2,1)} async-done(((bf16[128,8704]{1,0:T(8,128)(2,1)}), bf16[1024,8704]{1,0:T(8,128)(2,1)}) %all-gather.8.cloned.1.call-update) | async-done | bytes 17825808 | tf_op jit(solution)/shard_map/all_gather | solution.py:703
  146.3 5.6 shard_map.423
  155.3 12.3 %fusion.17 = (bf16[4096,192]{0,1:T(8,128)(2,1)}, f32[192,4096]{1,0:T(8,128)}) fusion(bf16[1024,8704]{1,0:T(8,128)(2,1)} %all-gather.8.cloned.1.call-done, f32[192,1024]{1,0:T(8,128)S(1)} %get-tuple-element.161, f32[1024]{0:T(1024)S(1)} %get-tuple-element.137, f32[192]{0:T(256)S(1)} %fusion.134, f32[192]{0:T(256)S(1)} %broadcast_multiply_fusion.5), kind=kOutput, calls=%fused_computation.41 | convolution fusion | flops 1662517248 | bytes 13899264 | tf_op jit(solution)/shard_map/dot_general | solution.py:36
  167.6 25.7 %all-gather.10.cloned.1.call-done = bf16[4096,1024]{1,0:T(8,128)(2,1)} async-done(((bf16[512,1024]{1,0:T(8,128)(2,1)}), bf16[4096,1024]{1,0:T(8,128)(2,1)}) %all-gather.10.cloned.1.call-update) | async-done | bytes 8388624 | tf_op jit(solution)/shard_map/all_gather | solution.py:703
  193.4 11.4 %fusion.177 = (f32[192]{0:T(256)S(1)}, f32[192,1024]{1,0:T(8,128)S(1)}) fusion(f32[192,1024]{1,0:T(8,128)} %copy-done.46, bf16[4096,1024]{1,0:T(8,128)(2,1)} %all-gather.10.cloned.1.call-done, f32[192,4096]{1,0:T(8,128)} %get-tuple-element.176), kind=kOutput, calls=%fused_computation.353 | convolution fusion | flops 1662123776 | bytes 13107968 | tf_op jit(solution)/shard_map/dot_general | solution.py:36
  209.9 26.9 %all-gather.12.cloned.1.call-done = bf16[512,5056]{1,0:T(8,128)(2,1)} async-done(((bf16[64,5056]{1,0:T(8,128)(2,1)}), bf16[512,5056]{1,0:T(8,128)(2,1)}) %all-gather.12.cloned.1.call-update) | async-done | bytes 5177360 | tf_op jit(solution)/shard_map/all_gather | solution.py:703
  253.2 14.8 %shard_map.424 = (bf16[512,576]{1,0:T(8,128)(2,1)S(1)}, f32[4,4,576]{2,1,0:T(4,128)S(1)}) custom-call(bf16[512,576]{1,0:T(8,128)(2,1)S(1)} %copy-done.9, bf16[768,512]{1,0:T(8,128)(2,1)S(1)} %copy-done.6, bf16[512,768]{1,0:T(8,128)(2,1)S(1)} %copy-done.8, f32[768,576]{1,0:T(8,128)S(1)} %slice.275.bias_ref), custom_call_target="tpu_custom_call" | custom-call | flops 3623878656 | bytes 1769472 | tf_op jit(solution)/shard_map/pallas_call | solution.py:102
  269.9 14.7 %multiply_convert_fusion = (bf16[576,2048]{1,0:T(8,128)(2,1)}, f32[576,2048]{1,0:T(8,128)}, f32[576,2048]{1,0:T(8,128)}) fusion(bf16[512,5056]{1,0:T(8,128)(2,1)} %all-gather.12.cloned.1.call-done, f32[576,512]{1,0:T(8,128)S(1)} %get-tuple-element.165, f32[512]{0:T(512)S(1)} %get-tuple-element.133, f32[576]{0:T(1024)S(1)} %fusion.122, ...), kind=kOutput, calls=%fused_computation.13 | convolution fusion | flops 1285816320 | bytes 15079936 | tf_op jit(solution)/shard_map/dot_general | solution.py:36
  302.3 7.1 %add_convert_fusion = bf16[576,2048]{1,0:T(8,128)(2,1)S(1)} fusion(f32[576,2048]{1,0:T(8,128)} %get-tuple-element.114, f32[576,2048]{1,0:T(8,128)} %get-tuple-element.166, bf16[2048,512]{1,0:T(8,128)(2,1)} %all-gather.14.cloned.1.call-done, f32[576,512]{1,0:T(8,128)} %copy-done.44, f32[576]{0:T(1024)S(1)} %negate_multiply_fusion.4), kind=kOutput, calls=%fused_computation.12 | convolution fusion | flops 1225064448 | bytes 15075584 | tf_op jit(solution)/shard_map/dot_general | solution.py:46
  322.2 25.5 %shard_map.425 = (bf16[512,576]{1,0:T(8,128)(2,1)S(1)}, bf16[768,512]{1,0:T(8,128)(2,1)S(1)}, bf16[768,512]{1,0:T(8,128)(2,1)S(1)}) custom-call(bf16[512,576]{1,0:T(8,128)(2,1)S(1)} %copy-done.10, bf16[576,512]{1,0:T(8,128)(2,1)S(1)} %copy-done.13, bf16[768,512]{1,0:T(8,128)(2,1)S(1)} %copy-done.7, bf16[512,768]{1,0:T(8,128)(2,1)} %bitcast.186, ...), custom_call_target="tpu_custom_call" | custom-call | flops 9059696640 | bytes 1769472 | tf_op jit(solution)/shard_map/pallas_call | solution.py:171
  351.7 4.3 convolution_convert_fusion
  375.5 12.1 %add_convert_fusion.1.refs_8_ = bf16[192,4096]{1,0:T(8,128)(2,1)S(1)} fusion(f32[192,4096]{1,0:T(8,128)S(1)} %copy-done.106, bf16[192,1024]{1,0:T(8,128)(2,1)S(1)} %add_convert_fusion.5.refs_9_, bf16[4096,1024]{1,0:T(8,128)(2,1)} %all-gather.10.cloned.1.call-done), kind=kOutput, calls=%fused_computation.59 | convolution fusion | flops 1667235840 | bytes 13500416 | tf_op jit(solution)/shard_map/dot_general | solution.py:46
  387.6 7.8 %multiply_reduce_fusion.12 = (f32[1024]{0:T(1024)S(1)}, f32[192]{0:T(256)S(1)}, f32[192,1024]{1,0:T(8,128)}) fusion(f32[192,1024]{1,0:T(8,128)S(1)} %copy-done.47, f32[192]{0:T(256)S(1)} %copy-done.101, f32[192]{0:T(256)S(1)} %copy-done.93, f32[1024]{0:T(1024)S(1)} %copy-done.86, bf16[192,4096]{1,0:T(8,128)(2,1)S(1)} %add_convert_fusion.1.refs_8_, ...), kind=kOutput, calls=%fused_computation.180 | convolution fusion | flops 1611987712 | bytes 11544832 | tf_op jit(solution)/shard_map/dot_general | solution.py:46
  405.5 6.7 shard_map.426
  418.0 3.8 copy.163
  423.5 5.4 multiply_reduce_fusion.10
  432.7 174.6 %shard_map.427 = (bf16[14,128,1024]{2,1,0:T(8,128)(2,1)}, f32[48,128]{1,0:T(8,128)}) custom-call(f32[48,128]{1,0:T(8,128)} %bitcast.194, bf16[4,2,128,192]{3,2,1,0:T(8,128)(2,1)} %bitcast.190, bf16[4,2,128,192]{3,2,1,0:T(8,128)(2,1)} %bitcast.174, bf16[4,2,128,192]{3,2,1,0:T(8,128)(2,1)} %bitcast.191, bf16[4,2,512,192]{3,2,1,0:T(8,128)(2,1)} %bitcast.181, ...), custom_call_target="tpu_custom_call" | custom-call | flops 5637144576 | bytes 314572800 | tf_op jit(solution)/shard_map/pallas_call | solution.py:514
  626.0 7.1 %fusion.158 = (bf16[128,8704]{1,0:T(8,128)(2,1)}, f32[128,8704]{1,0:T(8,128)S(1)}, f32[128,8704]{1,0:T(8,128)}) fusion(f32[128,8704]{1,0:T(8,128)S(1)} %bitcast.176, bf16[128,8704]{1,0:T(8,128)(2,1)} %slice_dynamic-update-slice_fusion, f32[128,8704]{1,0:T(8,128)} %param.37), kind=kLoop, calls=%fused_computation.337 | loop fusion | flops 11141120 | bytes 22282240 | tf_op jit(solution)/shard_map/convert_element_type | solution.py:820
  635.2 5.1 multiply_add_fusion
  642.8 5.1 fusion.156
  649.9 36.9 %all-reduce.9.cloned.1.call-done = (bf16[64,5056]{1,0:T(8,128)(2,1)}, bf16[256,512]{1,0:T(8,128)(2,1)}) async-done(((bf16[64,5056]{1,0:T(8,128)(2,1)}, bf16[256,512]{1,0:T(8,128)(2,1)}), (bf16[64,5056]{1,0:T(8,128)(2,1)}, bf16[256,512]{1,0:T(8,128)(2,1)})) %all-reduce.9.cloned.1.call-update) | async-done | bytes 909328 | tf_op jit(solution)/shard_map/psum | solution.py:772
  (413 shorter events, 199.2 us)
Async XLA Ops:
  7.2 107.2 %all-gather.6.cloned.1.call-start = ((), (), s32[]{:S(2)}) async-start(), calls=%async_computation.2 | async-start | bytes 1769472 | tf_op jit(solution)/shard_map/all_gather | solution.py:703
  9.0 127.5 %all-gather.8.cloned.1.call-start = ((), (), s32[]{:S(2)}) async-start(), calls=%async_computation.3 | async-start | bytes 20054016 | tf_op jit(solution)/shard_map/all_gather | solution.py:703
  13.1 180.3 %all-gather.10.cloned.1.call-start = ((), (), s32[]{:S(2)}) async-start(), calls=%async_computation.4 | async-start | bytes 9437184 | tf_op jit(solution)/shard_map/all_gather | solution.py:703
  14.3 222.6 %all-gather.12.cloned.1.call-start = ((), (), s32[]{:S(2)}) async-start(), calls=%async_computation.5 | async-start | bytes 5898240 | tf_op jit(solution)/shard_map/all_gather | solution.py:703
  16.7 268.0 %all-gather.14.cloned.1.call-start = ((), (), s32[]{:S(2)}) async-start(), calls=%async_computation.6 | async-start | bytes 2359296 | tf_op jit(solution)/shard_map/all_gather | solution.py:703
  17.5 622.8 %reduce-scatter.5.cloned.1.call-start = ((), (), s32[]{:S(2)}) async-start(), calls=%async_computation.8 | async-start | bytes 2359296 | tf_op jit(solution)/shard_map/reduce_scatter | solution.py:603
  28.0 115.7 %copy-start.77 = (f32[1024]{0:T(1024)}, f32[1024]{0:T(1024)S(1)}, u32[]{:S(2)}) copy-start(f32[1024]{0:T(1024)S(1)} %get-tuple-element.138) | copy-start | bytes 12292
  28.0 126.7 %copy-start.85 = (f32[1024]{0:T(1024)}, f32[1024]{0:T(1024)S(1)}, u32[]{:S(2)}) copy-start(f32[1024]{0:T(1024)S(1)} %get-tuple-element.137) | copy-start | bytes 12292
  80.7 169.1 %copy-start.2 = (f32[768,576]{1,0:T(8,128)}, f32[768,576]{1,0:T(8,128)S(1)}, u32[]{:S(2)}) copy-start(f32[768,576]{1,0:T(8,128)S(1)} %slice.275.bias_ref) | copy-start | bytes 5308420
  116.5 27.2 %copy-start.83 = (f32[192]{0:T(256)}, f32[192]{0:T(256)S(1)}, u32[]{:S(2)}) copy-start(f32[192]{0:T(256)S(1)} %broadcast_multiply_fusion.6) | copy-start | bytes 2308
  116.7 22.5 %copy-start.94 = (f32[192]{0:T(256)}, f32[192]{0:T(256)S(1)}, u32[]{:S(2)}) copy-start(f32[192]{0:T(256)S(1)} %multiply_reduce_fusion.18) | copy-start | bytes 2308
  116.7 26.9 %copy-start.90 = (f32[192]{0:T(256)}, f32[192]{0:T(256)S(1)}, u32[]{:S(2)}) copy-start(f32[192]{0:T(256)S(1)} %fusion.133) | copy-start | bytes 2308
  154.4 13.2 %copy-start.92 = (f32[192]{0:T(256)}, f32[192]{0:T(256)S(1)}, u32[]{:S(2)}) copy-start(f32[192]{0:T(256)S(1)} %broadcast_multiply_fusion.5) | copy-start | bytes 2308
  154.6 13.0 %copy-start.96 = (f32[192]{0:T(256)}, f32[192]{0:T(256)S(1)}, u32[]{:S(2)}) copy-start(f32[192]{0:T(256)S(1)} %multiply_reduce_fusion.17) | copy-start | bytes 2308
  253.2 14.8 %copy-start.25 = (f32[768,512]{1,0:T(8,128)S(1)}, f32[768,512]{1,0:T(8,128)}, u32[]{:S(2)}) copy-start(f32[768,512]{1,0:T(8,128)} %copy-done.24) | copy-start | bytes 4718596
  375.3 25.3 %copy-start.30 = (f32[192,1024]{1,0:T(8,128)}, f32[192,1024]{1,0:T(8,128)S(1)}, u32[]{:S(2)}) copy-start(f32[192,1024]{1,0:T(8,128)S(1)} %get-tuple-element.102) | copy-start | bytes 2359300
  395.5 244.9 %reduce-scatter.3.cloned.1.call-start = ((), (), s32[]{:S(2)}) async-start(), calls=%async_computation.7 | async-start | bytes 5898240 | tf_op jit(solution)/shard_map/reduce_scatter | solution.py:603
  431.3 255.5 %all-reduce.9.cloned.1.call-start = ((), (), s32[]{:S(2)}) async-start(), calls=%async_computation.9 | async-start | bytes 1835008 | tf_op jit(solution)/shard_map/psum | solution.py:772
  432.7 193.2 %slice-start = ((s8[4456448]{0:T(1024)(128)(4,1)}), s8[4194304]{0:T(1024)(128)(4,1)S(1)}, s32[]{:S(2)}) async-start(s8[4456448]{0:T(1024)(128)(4,1)} %bitcast.175), calls=%async_computation.10 | async-start | bytes 8388608
  432.7 193.2 %slice-start.1 = ((s8[4456448]{0:T(1024)(128)(4,1)}), s8[262144]{0:T(1024)(128)(4,1)S(1)}, s32[]{:S(2)}) async-start(s8[4456448]{0:T(1024)(128)(4,1)} %bitcast.175), calls=%async_computation.11 | async-start | bytes 524288
  607.4 15.1 %copy-start.61 = (f32[96,1024]{1,0:T(8,128)S(1)}, f32[96,1024]{1,0:T(8,128)}, u32[]{:S(2)}) copy-start(f32[96,1024]{1,0:T(8,128)} %param.30) | copy-start | bytes 1179652
  607.4 15.1 %copy-start.73 = (f32[96,1024]{1,0:T(8,128)S(1)}, f32[96,1024]{1,0:T(8,128)}, u32[]{:S(2)}) copy-start(f32[96,1024]{1,0:T(8,128)} %param.36) | copy-start | bytes 1179652
  609.1 16.0 %copy-start.70 = (f32[96,1024]{1,0:T(8,128)S(1)}, f32[96,1024]{1,0:T(8,128)}, u32[]{:S(2)}) copy-start(f32[96,1024]{1,0:T(8,128)} %param.42) | copy-start | bytes 1179652
  647.9 38.9 %copy-start.42 = (f32[64,5056]{1,0:T(8,128)S(1)}, f32[64,5056]{1,0:T(8,128)}, u32[]{:S(2)}) copy-start(f32[64,5056]{1,0:T(8,128)} %param.33) | copy-start | bytes 3883012
  (93 other events, 405.0 us)
Sparse Core Ops, SparseCore 0:
  10.5 28.3 all-gather.5
  41.4 95.0 all-gather.7
  138.9 54.3 all-gather.9
  195.7 41.1 all-gather.11
  239.1 27.8 all-gather.13
  395.6 41.1 reduce-scatter.4
  440.6 78.4 reduce-scatter.2
  640.5 46.2 all-reduce.8

commit v3 on v2

--- a/solution.py
+++ b/solution.py
@@ -198,9 +198,11 @@
 
 
 MESH = pl.DeviceIdType.MESH
-UNIT = 1024
+UNIT = 512
 HALF = UNIT // 2
 ROWS = 128
+HALF_ROWS = ROWS // 2
+LAGS = (2, 4, 6, 8, 11)
 
 
 def put(source, target, send, recv, device):
@@ -214,11 +216,12 @@
     )
 
 
-def sum_kernel(units, vec_ref, *refs):
-    n_left = max(u[0] for u in units) + 1
-    n_right = max(u[2] for u in units) + 1
+def sum_kernel(blocks, units, spots, vec_ref, dec_ref, *refs):
+    n_left = max(b[0] for b in blocks) + 1
+    n_right = max(u[1] for u in units) + 1
     lefts, rights = refs[:n_left], refs[n_left : n_left + n_right]
-    out_ref, vec_out = refs[n_left + n_right : n_left + n_right + 2]
+    outs = refs[n_left + n_right : n_left + n_right + 3]
+    dec_out, vec_out = refs[n_left + n_right + 3 : n_left + n_right + 5]
     (
         xo,
         xp,
@@ -234,9 +237,8 @@
         z_two,
         v_in,
         v_out,
-        load_sem,
-        swap_send,
-        swap_recv,
+        left_sem,
+        right_sem,
         a_send,
         a_recv,
         b_send,
@@ -245,8 +247,10 @@
         z_recv,
         v_send,
         v_recv,
-    ) = refs[n_left + n_right + 2 :]
+        store_sem,
+    ) = refs[n_left + n_right + 5 :]
     count = len(units)
+    extra = z_one.shape[0] - count
     z, f = lax.axis_index("dp"), lax.axis_index("fsdp")
     core, place = f % 2, f // 2
     x, y = place % 2, place // 2
@@ -276,37 +280,34 @@
         pl.semaphore_signal(barrier, inc=1, device_id=outward, device_id_type=MESH)
         pl.semaphore_wait(barrier, 5)
 
-    for number, (left, sub, right, column) in enumerate(units):
-        rows, cols = pl.ds(sub * ROWS, ROWS), pl.ds(column, UNIT)
-        whole = pl.ds(0, rights[right].shape[0])
-        put(
-            lefts[left].at[:, 1 - core, rows],
-            xp.at[number],
-            swap_send.at[number, 0],
-            swap_recv.at[number, 0],
-            partner,
-        ).start()
-        put(
-            rights[right].at[whole, cols],
-            yp.at[number],
-            swap_send.at[number, 1],
-            swap_recv.at[number, 1],
-            partner,
-        ).start()
-        pltpu.make_async_copy(
-            lefts[left].at[:, core, rows], xo.at[number], load_sem.at[number, 0]
-        ).start()
-        pltpu.make_async_copy(
-            rights[right].at[whole, cols], yo.at[number], load_sem.at[number, 1]
-        ).start()
+    def swap_left(source, b):
+        return put(source, xp.at[b], left_sem.at[b, 1], left_sem.at[b, 2], partner)
+
+    def swap_right(source, u):
+        return put(source, yp.at[u], right_sem.at[u, 1], right_sem.at[u, 2], partner)
+
+    for number, (block, right, column) in enumerate(units):
+        if number == 0 or block != units[number - 1][0]:
+            left, sub = blocks[block]
+            rows = pl.ds(sub * ROWS, ROWS)
+            swap_left(lefts[left].at[:, 1 - core, rows], block).start()
+            pltpu.make_async_copy(
+                lefts[left].at[:, core, rows], xo.at[block], left_sem.at[block, 0]
+            ).start()
+        piece = rights[right].at[:, pl.ds(column, UNIT)]
+        swap_right(piece, number).start()
+        pltpu.make_async_copy(piece, yo.at[number], right_sem.at[number, 0]).start()
+
+    starts = [n for n in range(1, count) if units[n][0] != units[n - 1][0]]
+
+    def block_of(u):
+        return sum([jnp.where(u >= n, 1, 0) for n in starts], jnp.int32(0))
 
     first, second = pl.ds(0, HALF), pl.ds(HALF, HALF)
 
-    def swap(u, side, source, target):
-        return put(source, target, swap_send.at[u, side], swap_recv.at[u, side], partner)
-
     def part(u, owner, columns):
-        return matmul(xo[u, owner], yo[u, :, columns]) + matmul(xp[u, owner], yp[u, :, columns])
+        b = block_of(u)
+        return matmul(xo[b, owner], yo[u, :, columns]) + matmul(xp[b, owner], yp[u, :, columns])
 
     def copy_a(u, side):
         slot = u % a_out.shape[0]
@@ -335,10 +336,33 @@
         return put(z_out.at[u], z_two.at[u], z_send.at[u, 0], z_recv.at[u, 1], across)
 
     def copy_out(u):
-        return put(out_ref.at[u], z_one.at[u], z_send.at[u, 1], z_recv.at[u, 0], outward)
+        return put(z_one.at[u], z_one.at[u], z_send.at[u, 1], z_recv.at[u, 0], outward)
 
     def copy_v(step, device):
         return put(v_out.at[step], v_in.at[step], v_send.at[step], v_recv.at[step], device)
+
+    def ready(n):
+        halves = [
+            dec_ref[:, pl.ds(pl.multiple_of((2 * n + part) * UNIT, UNIT), UNIT)] for part in range(2)
+        ]
+        return jnp.concatenate(halves, 0).astype(F32)
+
+    def send_in(u, value):
+        z_out[u] = value.astype(BF)
+        copy_in(u).start()
+
+    def add_in(u, value):
+        copy_in(u).wait_recv()
+        z_out[u] = (value + z_one[u].astype(F32)).astype(BF)
+        copy_across(u).start()
+
+    def add_across(u):
+        copy_across(u).wait_recv()
+        z_one[u] = (z_out[u].astype(F32) + z_two[u].astype(F32)).astype(BF)
+        copy_out(u).start()
+
+    def take(u):
+        copy_out(u).wait_recv()
 
     def step(i, _):
         def stage(lag, also=None):
@@ -353,10 +377,15 @@
         @when
         def _():
             u = u0
-            pltpu.make_async_copy(xo.at[u], xo.at[u], load_sem.at[u, 0]).wait()
-            pltpu.make_async_copy(yo.at[u], yo.at[u], load_sem.at[u, 1]).wait()
-            swap(u, 0, xo.at[u], xp.at[u]).wait()
-            swap(u, 1, yo.at[u], yp.at[u]).wait()
+            b = block_of(u)
+
+            @pl.when((u == 0) | (b != block_of(u - 1)))
+            def _():
+                pltpu.make_async_copy(xo.at[b], xo.at[b], left_sem.at[b, 0]).wait()
+                swap_left(xo.at[b], b).wait()
+
+            pltpu.make_async_copy(yo.at[u], yo.at[u], right_sem.at[u, 0]).wait()
+            swap_right(yo.at[u], u).wait()
 
             @pl.when(u >= a_out.shape[0])
             def _():
@@ -371,7 +400,7 @@
             a_out[slot, 1, 1] = part(u, at_far, second).astype(BF)
             copy_a(u, 1).start()
 
-        u1, when = stage(1)
+        u1, when = stage(LAGS[0])
 
         @when
         def _():
@@ -390,7 +419,7 @@
             b_out[slot, 1] = (part(u, at_x, second) + a_in[u, 1, 1].astype(F32)).astype(BF)
             copy_b(u, 1).start()
 
-        u2, when = stage(2)
+        u2, when = stage(LAGS[1])
 
         @when
         def _():
@@ -399,38 +428,47 @@
             copy_b(u, 1).wait_recv()
             for side, columns in enumerate((first, second)):
                 total = part(u, place, columns) + a_in[u, side, 0].astype(F32)
-                sums[u % 2, :, columns] = total + b_in[u, side].astype(F32)
+                sums[u % 4, :, columns] = total + b_in[u, side].astype(F32)
 
             @pl.when(outer)
             def _():
-                z_out[u] = sums[u % 2].astype(BF)
-                copy_in(u).start()
-
-        u3, when = stage(3, inner)
+                send_in(u + extra, sums[u % 4])
+
+        u3, when = stage(LAGS[2], inner)
 
         @when
         def _():
-            u = u3
-            copy_in(u).wait_recv()
-            z_out[u] = (sums[u % 2] + z_one[u].astype(F32)).astype(BF)
-            copy_across(u).start()
-
-        u4, when = stage(4, inner)
+            add_in(u3 + extra, sums[u3 % 4])
+
+        u4, when = stage(LAGS[3], inner)
 
         @when
         def _():
-            u = u4
-            copy_across(u).wait_recv()
-            out_ref[u] = (z_out[u].astype(F32) + z_two[u].astype(F32)).astype(BF)
-            copy_out(u).start()
-
-        u5, when = stage(6, outer)
+            add_across(u4 + extra)
+
+        u5, when = stage(LAGS[4], outer)
 
         @when
         def _():
-            u = u5
-            copy_out(u).wait_recv()
-            out_ref[u] = z_one[u]
+            take(u5 + extra)
+
+        @pl.when((i < extra) & outer)
+        def _():
+            send_in(i, ready(i))
+
+        one, two, three = [lag - LAGS[1] for lag in LAGS[2:]]
+
+        @pl.when((i >= one) & (i < extra + one) & inner)
+        def _():
+            add_in(i - one, ready(i - one))
+
+        @pl.when((i >= two) & (i < extra + two) & inner)
+        def _():
+            add_across(i - two)
+
+        @pl.when((i >= three) & (i < extra + three) & outer)
+        def _():
+            take(i - three)
 
         for number, device in enumerate((partner, x_side, y_side)):
 
@@ -472,8 +510,27 @@
 
         return 0
 
-    lax.fori_loop(0, count + 6, step, 0)
-
+    lax.fori_loop(0, count + LAGS[4], step, 0)
+
+    stores = []
+    for number, (out, row, rows, column, columns) in enumerate(spots):
+        stores.append(
+            pltpu.make_async_copy(
+                z_one.at[extra + number, pl.ds(0, rows), pl.ds(0, columns)],
+                outs[out].at[pl.ds(row, rows), pl.ds(column, columns)],
+                store_sem.at[number],
+            )
+        )
+    for number in range(2 * extra):
+        stores.append(
+            pltpu.make_async_copy(
+                z_one.at[number // 2, pl.ds(number % 2 * HALF_ROWS, HALF_ROWS)],
+                dec_out.at[:, pl.ds(number * UNIT, UNIT)],
+                store_sem.at[count + number],
+            )
+        )
+    for store in stores:
+        store.start()
     for u in range(count - a_out.shape[0], count):
         for side in range(2):
             copy_a(u, side).wait_send()
@@ -483,6 +540,9 @@
     for number, device in enumerate((partner, x_side, y_side)):
         copy_v(number, device).wait_send()
 
+    for store in stores:
+        store.wait()
+
     @pl.when(outer)
     def _():
         copy_v(3, inward).wait_send()
@@ -491,7 +551,7 @@
             copy_in(u).wait_send()
             return 0
 
-        lax.fori_loop(0, count, drain, 0)
+        lax.fori_loop(0, count + extra, drain, 0)
 
     @pl.when(inner)
     def _():
@@ -503,52 +563,50 @@
             copy_out(u).wait_send()
             return 0
 
-        lax.fori_loop(0, count, drain, 0)
-
-
-def sum_products(units, lefts, rights, vec):
+        lax.fori_loop(0, count + extra, drain, 0)
+
+
+def sum_products(blocks, units, spots, shapes, lefts, rights, dec, vec):
     count, depth = len(units), rights[0].shape[0]
+    extra = dec.shape[1] // (2 * UNIT)
+    full = count + extra
     lefts = [a.reshape(4, 2, a.shape[0] // 8, depth) for a in lefts]
     slots = 3
     dma = pltpu.SemaphoreType.DMA
     return pl.pallas_call(
-        partial(sum_kernel, units),
-        out_shape=(
-            jax.ShapeDtypeStruct((count, ROWS, UNIT), BF),
-            jax.ShapeDtypeStruct(vec.shape, F32),
-        ),
-        in_specs=[pl.BlockSpec(memory_space=pltpu.VMEM)]
+        partial(sum_kernel, blocks, units, spots),
+        out_shape=tuple(jax.ShapeDtypeStruct(shape, BF) for shape in (*shapes, dec.shape))
+        + (jax.ShapeDtypeStruct(vec.shape, F32),),
+        in_specs=[pl.BlockSpec(memory_space=pltpu.VMEM)] * 2
         + [pl.BlockSpec(memory_space=pl.ANY)] * (len(lefts) + len(rights)),
-        out_specs=(
-            pl.BlockSpec(memory_space=pltpu.VMEM),
-            pl.BlockSpec(memory_space=pltpu.VMEM),
-        ),
+        out_specs=(pl.BlockSpec(memory_space=pl.ANY),) * (len(shapes) + 1)
+        + (pl.BlockSpec(memory_space=pltpu.VMEM),),
         scratch_shapes=[
-            pltpu.VMEM((count, 4, ROWS, depth), BF),
-            pltpu.VMEM((count, 4, ROWS, depth), BF),
+            pltpu.VMEM((len(blocks), 4, ROWS, depth), BF),
+            pltpu.VMEM((len(blocks), 4, ROWS, depth), BF),
             pltpu.VMEM((count, depth, UNIT), BF),
             pltpu.VMEM((count, depth, UNIT), BF),
             pltpu.VMEM((slots, 2, 2, ROWS, HALF), BF),
             pltpu.VMEM((count, 2, 2, ROWS, HALF), BF),
             pltpu.VMEM((slots, 2, ROWS, HALF), BF),
             pltpu.VMEM((count, 2, ROWS, HALF), BF),
-            pltpu.VMEM((2, ROWS, UNIT), F32),
-            pltpu.VMEM((count, ROWS, UNIT), BF),
-            pltpu.VMEM((count, ROWS, UNIT), BF),
-            pltpu.VMEM((count, ROWS, UNIT), BF),
+            pltpu.VMEM((4, ROWS, UNIT), F32),
+            pltpu.VMEM((full, ROWS, UNIT), BF),
+            pltpu.VMEM((full, ROWS, UNIT), BF),
+            pltpu.VMEM((full, ROWS, UNIT), BF),
             pltpu.VMEM((6, *vec.shape), F32),
             pltpu.VMEM((6, *vec.shape), F32),
-            dma((count, 2)),
-            dma((count, 2)),
-            dma((count, 2)),
+            dma((len(blocks), 3)),
+            dma((count, 3)),
             dma((slots, 2)),
             dma((count, 2)),
             dma((slots, 2)),
             dma((count, 2)),
-            dma((count, 2)),
-            dma((count, 2)),
+            dma((full, 2)),
+            dma((full, 2)),
             dma((6,)),
             dma((6,)),
+            dma((count + 2 * extra,)),
         ],
         compiler_params=pltpu.CompilerParams(
             collective_id=0, has_side_effects=True, vmem_limit_bytes=58 * 2**20
@@ -558,7 +616,7 @@
             bytes_accessed=300 * 2**20,
             transcendentals=0,
         ),
-    )(vec, *lefts, *rights)
+    )(vec, dec, *lefts, *rights)
 
 
 def block_forward(h, weights, gains, bias, heads, skip):
@@ -603,27 +661,41 @@
     return lax.psum_scatter(grad.astype(BF), "fsdp", scatter_dimension=0, tiled=True)
 
 
-def sum_encoder(factors, encoded, dseen, inputs, dh_low, vector_grad, local_loss):
+def sum_gradients(factors, encoded, dseen, inputs, dh_low, dec, vector_grad, local_loss):
     lefts = [pair[0] for pair in factors] + [encoded.T]
     owners = lax.axis_size("fsdp")
-    first = inputs.T.reshape(owners, PD // owners, VIS)
-    lefts.append(jnp.pad(first, ((0, 0), (0, ROWS - PD // owners), (0, 0))).reshape(-1, VIS))
-    rights = [pair[1] for pair in factors] + [jnp.pad(dseen, ((0, 0), (0, UNIT - DD))), dh_low]
-    units = [(2, 0, 2, UNIT * n) for n in range(FF // UNIT)]
-    units += [(3, n, 3, 0) for n in range(FF // owners // ROWS)]
-    units += [(0, 0, 0, UNIT * n) for n in range(3 * D // UNIT)]
-    units += [(1, 0, 1, 0), (4, 0, 4, 0), (5, 0, 5, 0)]
+    own = PD // owners
+    first = inputs.T.reshape(owners, own, VIS)
+    lefts.append(jnp.pad(first, ((0, 0), (0, ROWS - own), (0, 0))).reshape(-1, VIS))
+    rights = [pair[1] for pair in factors] + [dseen, dh_low]
+    blocks, units, spots = [], [], []
+
+    def add(left, sub, right, out, row, rows, column, columns):
+        blocks.append((left, sub))
+        for n in range(0, columns, UNIT):
+            units.append((len(blocks) - 1, right, n))
+            spots.append((out, row, rows, column + n, UNIT))
+
+    add(4, 0, 4, 1, 0, ROWS, 4 * D + FF, DD)
+    for n in range(FF // owners // ROWS):
+        add(3, n, 3, 2, n * ROWS, ROWS, 0, D)
+    add(2, 0, 2, 1, 0, ROWS, 4 * D, FF)
+    add(1, 0, 1, 1, 0, ROWS, 3 * D, D)
+    add(0, 0, 0, 1, 0, ROWS, 0, 3 * D)
+    add(5, 0, 5, 0, 0, own, 0, D)
+    shapes = ((own, D), (ROWS, 4 * D + FF + DD), (FF // owners, D))
     length = vector_grad.shape[0]
     rows = -(-(length + 1) // (8 * LANES)) * 8
     vec = jnp.concatenate(
         [vector_grad, local_loss[None], jnp.zeros((rows * LANES - length - 1,), F32)]
     )
-    grads, vec = sum_products(tuple(units), lefts, rights, vec.reshape(rows, LANES))
+    used = dec.shape[1]
+    dec = jnp.pad(dec, ((0, 0), (0, -used % (2 * UNIT))))
+    *parts, dec, vec = sum_products(
+        tuple(blocks), tuple(units), tuple(spots), shapes, lefts, rights, dec, vec.reshape(rows, LANES)
+    )
     vec = vec.reshape(-1)
-    up, down, qkv = grads[:4], grads[4:8], grads[8:11]
-    wide = jnp.concatenate([*qkv, grads[11], *up, grads[12][:, :DD]], 1)
-    parts = (grads[13][: PD // owners], wide, down.reshape(-1, D))
-    return parts, vec[:length], vec[length]
+    return parts, dec[:, :used], vec[:length], vec[length]
 
 
 def enc_split(wide, down):
@@ -764,12 +836,15 @@
     dy_start, dec_factors, dgains_dec = block_backward(
         dec_saved, dy_end, dec_weights, gains_dec, bias_dec, DHEADS, VIS
     )
+    owners = lax.axis_size("fsdp")
     dec_grads = [matmul(*pair).astype(BF) for pair in dec_factors]
-    head_grad = left_t(decoded, dpred).astype(BF)
-    wide_dec_grad = jnp.concatenate([dec_grads[0], dec_grads[1], dec_grads[2], head_grad], 1)
-    dec_parts = (wide_dec_grad, dec_grads[3])
-    dy_start, dec_parts = lax.optimization_barrier((dy_start, dec_parts))
-    dec_parts = lax.psum(tuple(reduce_rows(g) for g in dec_parts), "dp")
+    down_grad = dec_grads[3].reshape(owners, -1, DD // owners, DD)
+    down_grad = down_grad.transpose(0, 2, 1, 3).reshape(DD, DFF)
+    dec_grads = jnp.concatenate(
+        [*dec_grads[:3], left_t(decoded, dpred).astype(BF), down_grad], 1
+    )
+    dy_start, dec_grads = lax.optimization_barrier((dy_start, dec_grads))
+    dec_sum = reduce_rows(dec_grads)
     picked = dy_start[:VIS] * keptf
     dtoken = jnp.sum(dy_start, 0) - jnp.sum(picked, 0)
     dseen = picked.astype(BF)
@@ -790,8 +865,8 @@
         ]
     )
     if (lax.axis_size("dp"), lax.axis_size("fsdp")) == (4, 8):
-        enc_parts, vector_grad, loss_sum = sum_encoder(
-            enc_factors, encoded, dseen, inputs, dh_low, vector_grad, local_loss
+        enc_parts, dec_sum, vector_grad, loss_sum = sum_gradients(
+            enc_factors, encoded, dseen, inputs, dh_low, dec_sum, vector_grad, local_loss
         )
     else:
         enc_grads = [matmul(*pair).astype(BF) for pair in enc_factors]
@@ -807,6 +882,11 @@
             "dp",
         )
         vector_grad, loss_sum = lax.psum((vector_grad, local_loss), ("dp", "fsdp"))
+        dec_sum = lax.psum(dec_sum, "dp")
+    rows = dec_sum.shape[0]
+    wide = wide_dec.shape[1]
+    down = dec_sum[:, wide:].reshape(rows, -1, DD).transpose(1, 0, 2).reshape(-1, DD)
+    dec_parts = (dec_sum[:, :wide], down)
     shard_grads = [g.astype(F32) for g in (*enc_parts, *dec_parts)]
     rate = STEP_UNIT * (PD * TOK_DEV * lax.axis_size("dp") * lax.axis_size("fsdp")) ** 0.5
     weights = (embed, wide_enc, enc_down, wide_dec, dec_down)

time: 708 us -> 633 us (0.89)
  waiting for transfers between devices: 108 us -> 79.7 us
  Pallas kernels: 227 us -> 200 us
  matrix products: 139 us -> 127 us
    psum x1 -> x0, waiting for transfers between devices: 36.9 us -> none  [body(): dec_parts = lax.psum(tuple((reduce_rows(g) for g in dec_parts)), 'dp')]
    pallas_call x1, Pallas kernels: 175 us -> 148 us  [sum_products(): pl.pallas_call(partial(sum_kernel, blocks, units, spots), out_shape=tuple...]
    unnamed x226 -> x249, local copies, waits for them, and re-layouts: 32.2 us -> 19.4 us
    dot_general x10, matrix products: 47.4 us -> 35.1 us  [right_t(): lax.dot_general(left, right, (((1,), (1,)), ((), ())), preferred_element_...]
    concatenate x2, local copies, waits for them, and re-layouts: 1.99 us -> 13.7 us  [the longest x1 12.4 us: body(): jnp.concatenate([*dec_grads[:3], left_t(decoded, dpred).astype(BF), down_...]
  transfers between devices with their start and end apart: 8 -> 6, of which waited for: 4 -> 4; matrix products, arithmetic and copies ran while one was open for 28% -> 28% of each run, Pallas kernels for 29% -> 4%
where the time goes in v3:
time: 633 us; the launch traced here: 627 us
  Pallas kernels  200 us (32%)
  matrix products  127 us (20%)
  local copies, waits for them, and re-layouts  80.1 us (13%)
  waiting for transfers between devices  79.7 us (13%)
  other arithmetic  76.7 us (12%)
  blocking collectives  42.4 us (7%)
  between operations  20.3 us (3%)
    pallas_call x1, Pallas kernels, sum_products(): pl.pallas_call(partial(sum_kernel, blocks, units, spots), out_shape=tuple...  148 us
    dot_general x22, matrix products, matmul(): return jnp.dot(left, right, preferred_element_type=jnp.float32)  85.8 us
    all_gather x5, waiting for transfers between devices, body(): lax.all_gather(w.astype(BF), 'fsdp', axis=0, tiled=True)  72.5 us
    psum x1, blocking collectives, body(): lax.psum(jnp.concatenate([band_sum, band_sq, counts]), ('dp', 'fsdp'))  42.4 us
    dot_general x10, matrix products, right_t(): lax.dot_general(left, right, (((1,), (1,)), ((), ())), preferred_element_...  35.1 us
    pallas_call x2, Pallas kernels, attend_back(): pl.pallas_call(partial(attend_back_kernel, size), grid=(groups,), out_sha...  32.3 us
    pallas_call x2, Pallas kernels, attend(): pl.pallas_call(partial(attend_kernel, size), grid=(groups,), out_shape=(j...  20.4 us
    unnamed x249, local copies, waits for them, and re-layouts  19.4 us
  transfers between devices with their start and end apart: 6, of which 4 were waited for; matrix products, arithmetic and copies ran while one was open for 28% of the time, Pallas kernels for 4%

profile of v3, /device:TPU:0, one launch (start us, length us, event | category | flops | bytes accessed | tf_op | source)
XLA Modules:
  0.0 627.1 jit_solution(7579448471249208002)
XLA Ops:
  9.0 4.0 convert_element_type.225
  33.8 42.4 %psum.7 = f32[8]{0:T(128)S(1)} all-reduce(f32[8]{0:T(128)S(1)} %pad_maximum_fusion.1), channel_id=1, replica_groups=mesh['dp'=4,'fsdp'=8] {'dp','fsdp'}, use_global_device_ids=true, to_apply=%region_8.9 | all-reduce | flops 8 | bytes 64 | tf_op jit(solution)/shard_map/psum | solution.py:787
  100.0 3.5 reshape.313
  108.8 4.4 multiply_sine_fusion.1
  116.4 20.0 %all-gather.8.cloned.1.call-done = bf16[1024,8704]{1,0:T(8,128)(2,1)} async-done(((bf16[128,8704]{1,0:T(8,128)(2,1)}), bf16[1024,8704]{1,0:T(8,128)(2,1)}) %all-gather.8.cloned.1.call-update) | async-done | bytes 17825808 | tf_op jit(solution)/shard_map/all_gather | solution.py:775
  146.2 5.6 shard_map.423
  155.2 12.3 %fusion.17 = (bf16[4096,192]{0,1:T(8,128)(2,1)}, f32[192,4096]{1,0:T(8,128)}) fusion(bf16[1024,8704]{1,0:T(8,128)(2,1)} %all-gather.8.cloned.1.call-done, f32[192,1024]{1,0:T(8,128)S(1)} %get-tuple-element.163, f32[1024]{0:T(1024)S(1)} %get-tuple-element.139, f32[192]{0:T(256)S(1)} %fusion.133, f32[192]{0:T(256)S(1)} %broadcast_multiply_fusion.5), kind=kOutput, calls=%fused_computation.40 | convolution fusion | flops 1662517248 | bytes 13899264 | tf_op jit(solution)/shard_map/dot_general | solution.py:36
  167.6 25.8 %all-gather.10.cloned.1.call-done = bf16[4096,1024]{1,0:T(8,128)(2,1)} async-done(((bf16[512,1024]{1,0:T(8,128)(2,1)}), bf16[4096,1024]{1,0:T(8,128)(2,1)}) %all-gather.10.cloned.1.call-update) | async-done | bytes 8388624 | tf_op jit(solution)/shard_map/all_gather | solution.py:775
  193.3 11.6 %fusion.175 = (f32[192]{0:T(256)S(1)}, f32[192,1024]{1,0:T(8,128)S(1)}) fusion(f32[192,1024]{1,0:T(8,128)} %copy-done.48, bf16[4096,1024]{1,0:T(8,128)(2,1)} %all-gather.10.cloned.1.call-done, f32[192,4096]{1,0:T(8,128)} %get-tuple-element.178), kind=kOutput, calls=%fused_computation.343 | convolution fusion | flops 1662123776 | bytes 13107968 | tf_op jit(solution)/shard_map/dot_general | solution.py:36
  210.1 26.7 %all-gather.12.cloned.1.call-done = bf16[512,5056]{1,0:T(8,128)(2,1)} async-done(((bf16[64,5056]{1,0:T(8,128)(2,1)}), bf16[512,5056]{1,0:T(8,128)(2,1)}) %all-gather.12.cloned.1.call-update) | async-done | bytes 5177360 | tf_op jit(solution)/shard_map/all_gather | solution.py:775
  253.2 14.8 %shard_map.424 = (bf16[512,576]{1,0:T(8,128)(2,1)S(1)}, f32[4,4,576]{2,1,0:T(4,128)S(1)}) custom-call(bf16[512,576]{1,0:T(8,128)(2,1)S(1)} %copy-done.9, bf16[768,512]{1,0:T(8,128)(2,1)S(1)} %copy-done.6, bf16[512,768]{1,0:T(8,128)(2,1)S(1)} %copy-done.8, f32[768,576]{1,0:T(8,128)S(1)} %slice.254.bias_ref), custom_call_target="tpu_custom_call" | custom-call | flops 3623878656 | bytes 1769472 | tf_op jit(solution)/shard_map/pallas_call | solution.py:102
  270.0 14.5 %multiply_convert_fusion = (bf16[576,2048]{1,0:T(8,128)(2,1)}, f32[576,2048]{1,0:T(8,128)}, f32[576,2048]{1,0:T(8,128)}) fusion(bf16[512,5056]{1,0:T(8,128)(2,1)} %all-gather.12.cloned.1.call-done, f32[576,512]{1,0:T(8,128)S(1)} %get-tuple-element.167, f32[512]{0:T(512)S(1)} %get-tuple-element.135, f32[576]{0:T(1024)S(1)} %fusion.121, ...), kind=kOutput, calls=%fused_computation.12 | convolution fusion | flops 1285816320 | bytes 15079936 | tf_op jit(solution)/shard_map/dot_general | solution.py:36
  284.5 3.8 fusion.177
  313.0 25.9 %shard_map.425 = (bf16[512,576]{1,0:T(8,128)(2,1)S(1)}, bf16[768,512]{1,0:T(8,128)(2,1)S(1)}, bf16[768,512]{1,0:T(8,128)(2,1)S(1)}) custom-call(bf16[512,576]{1,0:T(8,128)(2,1)S(1)} %copy-done.10, bf16[576,512]{1,0:T(8,128)(2,1)S(1)} %copy-done.13, bf16[768,512]{1,0:T(8,128)(2,1)S(1)} %copy-done.7, bf16[512,768]{1,0:T(8,128)(2,1)} %bitcast.174, ...), custom_call_target="tpu_custom_call" | custom-call | flops 9059696640 | bytes 1769472 | tf_op jit(solution)/shard_map/pallas_call | solution.py:171
  342.9 4.3 convolution_convert_fusion
  359.2 12.4 %concatenate.38 = bf16[512,7104]{1,0:T(8,128)(2,1)} concatenate(bf16[512,1536]{1,0:T(8,128)(2,1)} %convolution_convert_fusion, bf16[512,512]{1,0:T(8,128)(2,1)} %convolution_convert_fusion.8, bf16[512,2048]{1,0:T(8,128)(2,1)} %convolution_convert_fusion.2, bf16[512,960]{1,0:T(8,128)(2,1)S(1)} %copy.157, bf16[512,2048]{1,0:T(8,128)(2,1)} %bitcast.161), dimensions={1} | concatenate | bytes 14548992 | tf_op jit(solution)/shard_map/concatenate | solution.py:843
  381.2 13.0 %add_convert_fusion.1.refs_8_ = bf16[192,4096]{1,0:T(8,128)(2,1)S(1)} fusion(f32[192,4096]{1,0:T(8,128)S(1)} %copy-done.112, bf16[192,1024]{1,0:T(8,128)(2,1)S(1)} %add_convert_fusion.5.refs_9_, bf16[4096,1024]{1,0:T(8,128)(2,1)} %all-gather.10.cloned.1.call-done), kind=kOutput, calls=%fused_computation.58 | convolution fusion | flops 1667235840 | bytes 13500416 | tf_op jit(solution)/shard_map/dot_general | solution.py:46
  401.3 6.4 %shard_map.426 = (bf16[1024,192]{1,0:T(8,128)(2,1)S(1)}, bf16[192,1024]{1,0:T(8,128)(2,1)S(1)}, bf16[192,1024]{1,0:T(8,128)(2,1)S(1)}) custom-call(bf16[1024,192]{1,0:T(8,128)(2,1)S(1)} %copy.159.qt_ref, bf16[192,1024]{1,0:T(8,128)(2,1)S(1)} %copy-done.4, bf16[192,1024]{1,0:T(8,128)(2,1)S(1)} %copy-done.1, bf16[1024,192]{1,0:T(8,128)(2,1)S(1)} %bitcast.152, ...), custom_call_target="tpu_custom_call" | custom-call | flops 754974720 | bytes 147456 | tf_op jit(solution)/shard_map/pallas_call | solution.py:171
  414.1 3.8 copy.172
  419.6 6.2 multiply_reduce_fusion.10
  431.7 7.1 %reduce-scatter.2.cloned.1.call-done = bf16[64,7104]{1,0:T(8,128)(2,1)} async-done(((bf16[512,7104]{1,0:T(8,128)(2,1)}), bf16[64,7104]{1,0:T(8,128)(2,1)}) %reduce-scatter.2.cloned.1.call-update) | async-done | bytes 909328 | tf_op jit(solution)/shard_map/reduce_scatter | solution.py:661
  440.9 147.7 %shard_map.427 = (bf16[96,1024]{1,0:T(8,128)(2,1)}, bf16[128,8704]{1,0:T(8,128)(2,1)}, bf16[512,1024]{1,0:T(8,128)(2,1)}, bf16[64,7168]{1,0:T(8,128)(2,1)}, f32[48,128]{1,0:T(8,128)}) custom-call(f32[48,128]{1,0:T(8,128)} %bitcast.182, bf16[64,7168]{1,0:T(8,128)(2,1)} %pad.26.dec_ref, bf16[4,2,128,192]{3,2,1,0:T(8,128)(2,1)} %bitcast.178, ...), custom_call_target="tpu_custom_call" | custom-call | flops 5435817984 | bytes 314572800 | tf_op jit(solution)/shard_map/pallas_call | solution.py:576
  596.7 7.9 %fusion.156 = (bf16[128,8704]{1,0:T(8,128)(2,1)}, f32[128,8704]{1,0:T(8,128)S(1)}, f32[128,8704]{1,0:T(8,128)}) fusion(f32[128,8704]{1,0:T(8,128)} %param.31, bf16[128,8704]{1,0:T(8,128)(2,1)S(1)} %copy-done.54, f32[128,8704]{1,0:T(8,128)} %param.37), kind=kLoop, calls=%fused_computation.327 | loop fusion | flops 11141120 | bytes 22282240 | tf_op jit(solution)/shard_map/convert_element_type | solution.py:900
  604.6 6.7 %multiply_add_fusion = f32[128,8704]{1,0:T(8,128)} fusion(f32[128,8704]{1,0:T(8,128)S(1)} %get-tuple-element.94, f32[128,8704]{1,0:T(8,128)} %param.43), kind=kLoop, calls=%fused_computation.27 | loop fusion | flops 3342336 | bytes 13369344 | tf_op jit(solution)/shard_map/add | solution.py:719
  (433 shorter events, 175.9 us)
Async XLA Ops:
  7.2 106.1 %all-gather.6.cloned.1.call-start = ((), (), s32[]{:S(2)}) async-start(), calls=%async_computation.1 | async-start | bytes 1769472 | tf_op jit(solution)/shard_map/all_gather | solution.py:775
  9.0 127.5 %all-gather.8.cloned.1.call-start = ((), (), s32[]{:S(2)}) async-start(), calls=%async_computation.2 | async-start | bytes 20054016 | tf_op jit(solution)/shard_map/all_gather | solution.py:775
  13.1 180.3 %all-gather.10.cloned.1.call-start = ((), (), s32[]{:S(2)}) async-start(), calls=%async_computation.3 | async-start | bytes 9437184 | tf_op jit(solution)/shard_map/all_gather | solution.py:775
  14.3 222.5 %all-gather.12.cloned.1.call-start = ((), (), s32[]{:S(2)}) async-start(), calls=%async_computation.4 | async-start | bytes 5898240 | tf_op jit(solution)/shard_map/all_gather | solution.py:775
  16.7 267.8 %all-gather.14.cloned.1.call-start = ((), (), s32[]{:S(2)}) async-start(), calls=%async_computation.5 | async-start | bytes 2359296 | tf_op jit(solution)/shard_map/all_gather | solution.py:775
  17.5 421.2 %reduce-scatter.2.cloned.1.call-start = ((), (), s32[]{:S(2)}) async-start(), calls=%async_computation.6 | async-start | bytes 8257536 | tf_op jit(solution)/shard_map/reduce_scatter | solution.py:661
  28.0 115.6 %copy-start.82 = (f32[1024]{0:T(1024)}, f32[1024]{0:T(1024)S(1)}, u32[]{:S(2)}) copy-start(f32[1024]{0:T(1024)S(1)} %get-tuple-element.140) | copy-start | bytes 12292
  28.0 126.7 %copy-start.90 = (f32[1024]{0:T(1024)}, f32[1024]{0:T(1024)S(1)}, u32[]{:S(2)}) copy-start(f32[1024]{0:T(1024)S(1)} %get-tuple-element.139) | copy-start | bytes 12292
  80.6 169.2 %copy-start.2 = (f32[768,576]{1,0:T(8,128)}, f32[768,576]{1,0:T(8,128)S(1)}, u32[]{:S(2)}) copy-start(f32[768,576]{1,0:T(8,128)S(1)} %slice.254.bias_ref) | copy-start | bytes 5308420
  115.3 28.3 %copy-start.88 = (f32[192]{0:T(256)}, f32[192]{0:T(256)S(1)}, u32[]{:S(2)}) copy-start(f32[192]{0:T(256)S(1)} %broadcast_multiply_fusion.6) | copy-start | bytes 2308
  116.4 26.0 %copy-start.99 = (f32[192]{0:T(256)}, f32[192]{0:T(256)S(1)}, u32[]{:S(2)}) copy-start(f32[192]{0:T(256)S(1)} %multiply_reduce_fusion.18) | copy-start | bytes 2308
  116.4 27.2 %copy-start.95 = (f32[192]{0:T(256)}, f32[192]{0:T(256)S(1)}, u32[]{:S(2)}) copy-start(f32[192]{0:T(256)S(1)} %fusion.132) | copy-start | bytes 2308
  154.3 13.2 %copy-start.97 = (f32[192]{0:T(256)}, f32[192]{0:T(256)S(1)}, u32[]{:S(2)}) copy-start(f32[192]{0:T(256)S(1)} %broadcast_multiply_fusion.5) | copy-start | bytes 2308
  253.2 14.8 %copy-start.25 = (f32[768,512]{1,0:T(8,128)S(1)}, f32[768,512]{1,0:T(8,128)}, u32[]{:S(2)}) copy-start(f32[768,512]{1,0:T(8,128)} %copy-done.24) | copy-start | bytes 4718596
  376.3 17.8 %slice-start.2 = ((s8[17825792]{0:T(1024)(128)(4,1)}), s8[4194304]{0:T(1024)(128)(4,1)S(1)}, s32[]{:S(2)}) async-start(s8[17825792]{0:T(1024)(128)(4,1)} %bitcast.187), calls=%async_computation.9 | async-start | bytes 8388608
  380.2 18.2 %copy-start.30 = (f32[192,1024]{1,0:T(8,128)}, f32[192,1024]{1,0:T(8,128)S(1)}, u32[]{:S(2)}) copy-start(f32[192,1024]{1,0:T(8,128)S(1)} %get-tuple-element.104) | copy-start | bytes 2359300
  381.1 13.1 %copy-start.106 = (f32[192]{0:T(256)S(1)}, f32[192]{0:T(256)}, u32[]{:S(2)}) copy-start(f32[192]{0:T(256)} %copy-done.105) | copy-start | bytes 2308
  381.1 13.1 %slice-start.3 = ((s8[17825792]{0:T(1024)(128)(4,1)}), s8[4194304]{0:T(1024)(128)(4,1)S(1)}, s32[]{:S(2)}) async-start(s8[17825792]{0:T(1024)(128)(4,1)} %bitcast.187), calls=%async_computation.10 | async-start | bytes 8388608
  381.1 13.1 %slice-start.4 = ((s8[17825792]{0:T(1024)(128)(4,1)}), s8[4194304]{0:T(1024)(128)(4,1)S(1)}, s32[]{:S(2)}) async-start(s8[17825792]{0:T(1024)(128)(4,1)} %bitcast.187), calls=%async_computation.11 | async-start | bytes 8388608
  381.2 13.1 %slice-start.5 = ((s8[17825792]{0:T(1024)(128)(4,1)}), s8[4194304]{0:T(1024)(128)(4,1)S(1)}, s32[]{:S(2)}) async-start(s8[17825792]{0:T(1024)(128)(4,1)} %bitcast.187), calls=%async_computation.12 | async-start | bytes 8388608
  381.2 13.1 %slice-start.6 = ((s8[17825792]{0:T(1024)(128)(4,1)}), s8[1048576]{0:T(1024)(128)(4,1)S(1)}, s32[]{:S(2)}) async-start(s8[17825792]{0:T(1024)(128)(4,1)} %bitcast.187), calls=%async_computation.13 | async-start | bytes 2097152
  440.9 148.8 %copy-start.46 = (f32[64,5056]{1,0:T(8,128)S(1)}, f32[64,5056]{1,0:T(8,128)}, u32[]{:S(2)}) copy-start(f32[64,5056]{1,0:T(8,128)} %param.33) | copy-start | bytes 3883012
  440.9 148.8 %copy-start.69 = (f32[64,5056]{1,0:T(8,128)S(1)}, f32[64,5056]{1,0:T(8,128)}, u32[]{:S(2)}) copy-start(f32[64,5056]{1,0:T(8,128)} %param.39) | copy-start | bytes 3883012
  592.7 23.1 %copy-start.47 = (f32[64,5056]{1,0:T(8,128)}, f32[64,5056]{1,0:T(8,128)S(1)}, u32[]{:S(2)}) copy-start(f32[64,5056]{1,0:T(8,128)S(1)} %get-tuple-element.88) | copy-start | bytes 3883012
  (106 other events, 438.3 us)
Sparse Core Ops, SparseCore 0:
  10.5 28.3 all-gather.5
  41.4 95.0 all-gather.7
  138.9 54.3 all-gather.9
  195.6 41.1 all-gather.11
  239.1 27.8 all-gather.13
  371.8 66.9 reduce-scatter.1

commit v4 on v3

--- a/solution.py
+++ b/solution.py
@@ -58,6 +58,12 @@
 def norm_back(h, gain, grad):
     result, pull = jax.vjp(layer_norm, h, gain)
     return pull(grad)
+
+
+def gelu_parts(before):
+    below = 0.5 * (1.0 + lax.erf(before * 0.5**0.5))
+    slope = below + before * jnp.exp(before * before * -0.5) * (0.5 / jnp.pi) ** 0.5
+    return before * below, slope
 
 
 def positions(coord, scale, width):
@@ -135,11 +141,9 @@
     do_ref,
     dot_ref,
     bias_ref,
-    lse_ref,
-    dqt_ref,
-    dk_ref,
-    dv_ref,
+    *rest,
 ):
+    *lse_ref, dqt_ref, dk_ref, dv_ref = rest
     per = LANES // size
     row_head = lax.broadcasted_iota(jnp.int32, qt_ref.shape, 0) // size
     lane_head = lax.broadcasted_iota(jnp.int32, dk_ref.shape, 1) // size
@@ -150,7 +154,11 @@
         query = jnp.where(row_head == j, qt_ref[...].astype(F32), 0.0).astype(BF)
         dout = jnp.where(row_head == j, dot_ref[...].astype(F32), 0.0).astype(BF)
         scores = matmul(k_ref[...], query) * factor + bias_ref[...]
-        probs = jnp.exp(scores - lse_ref[0, j : j + 1, :])
+        if lse_ref:
+            probs = jnp.exp(scores - lse_ref[0][0, j : j + 1, :])
+        else:
+            probs = jnp.exp(scores - jnp.max(scores, 0, keepdims=True))
+            probs = probs * (1.0 / jnp.sum(probs, 0, keepdims=True))
         dvalues = jnp.where(lane_head == j, matmul(probs.astype(BF), do_ref[...]), dvalues)
         dprobs = matmul(v_ref[...], dout)
         delta = jnp.sum(dprobs * probs, 0, keepdims=True)
@@ -185,8 +193,8 @@
             tall(queries),
             flat(queries),
             pl.BlockSpec((rows, queries), lambda g: (0, 0)),
-            pl.BlockSpec((1, per, queries), lambda g: (g, 0, 0)),
-        ],
+        ]
+        + [pl.BlockSpec((1, per, queries), lambda g: (g, 0, 0))] * (lse is not None),
         out_specs=(flat(queries), tall(rows), tall(rows)),
         compiler_params=pltpu.CompilerParams(vmem_limit_bytes=48 * 2**20),
         cost_estimate=pl.CostEstimate(
@@ -194,7 +202,7 @@
             bytes_accessed=4 * rows * queries,
             transcendentals=rows * queries * width // size,
         ),
-    )(query.T, query, keys, keys.T, values, dmixed, dmixed.T, bias, lse)
+    )(query.T, query, keys, keys.T, values, dmixed, dmixed.T, bias, *([] if lse is None else [lse]))
 
 
 MESH = pl.DeviceIdType.MESH
@@ -619,6 +627,404 @@
     )(vec, dec, *lefts, *rights)
 
 
+def encoder_pieces(shapes):
+    (own, width), (rows, _), (tall, _) = shapes
+    pieces = [(0, 0, own, 0, width, 0)]
+    pieces += [(1, 0, rows, n * D, D, (1, 2, 0)[n]) for n in range(3)]
+    pieces += [(1, 0, rows, 3 * D, D, 1)]
+    pieces += [(1, 0, rows, 4 * D + n * D, D, (2, 0, 1, 2)[n]) for n in range(FF // D)]
+    pieces += [(2, n * rows, rows, 0, D, (0, 1, 2, 0)[n]) for n in range(tall // rows)]
+    pieces += [(1, 0, rows, 4 * D + FF, DD, 0)]
+    return pieces
+
+
+def norm_rows(h, gain):
+    mean = jnp.mean(h, -1, keepdims=True)
+    cent = h - mean
+    var = jnp.mean(cent * cent, -1, keepdims=True)
+    return (cent * lax.rsqrt(var + EPS) * gain).astype(BF)
+
+
+def encoder_kernel(
+    picked_ref,
+    stats_ref,
+    pos_ref,
+    bias_ref,
+    gains_ref,
+    embed_ref,
+    wide_ref,
+    down_ref,
+    wide_out,
+    down_out,
+    stats_out,
+    inputs_ref,
+    start_ref,
+    a_ref,
+    qkv_ref,
+    mixed_ref,
+    middle_ref,
+    b_ref,
+    slope_ref,
+    hidden_ref,
+    end_ref,
+    z_ref,
+    seen_ref,
+    w_embed,
+    w_wide,
+    w_down,
+    v_in,
+    v_out,
+    load_sem,
+    store_sem,
+    send_sem,
+    recv_sem,
+    v_send,
+    v_recv,
+):
+    shards, gathered = (embed_ref, wide_ref, down_ref), (w_embed, w_wide, w_down)
+    pieces = encoder_pieces([ref.shape for ref in shards])
+    count = len(pieces)
+    z, f = lax.axis_index("dp"), lax.axis_index("fsdp")
+    core, place = f % 2, f // 2
+    x, y = place % 2, place // 2
+    f_x, f_y, f_far = f + 2 - 4 * x, f + 4 - 8 * y, f + 6 - 4 * x - 8 * y
+    partner = (z, f + 1 - 2 * core)
+    x_side, y_side, z_side = (z, f_x), (z, f_y), (z + 1 - 2 * (z % 2), f)
+    outer = (z == 0) | (z == 3)
+    inner = (z == 1) | (z == 2)
+    across = (3 - z, f)
+
+    barrier = pltpu.get_barrier_semaphore()
+    for device in (partner, x_side, y_side, z_side):
+        pl.semaphore_signal(barrier, inc=1, device_id=device, device_id_type=MESH)
+
+    @pl.when(outer)
+    def _():
+        pl.semaphore_wait(barrier, 4)
+
+    @pl.when(inner)
+    def _():
+        pl.semaphore_signal(barrier, inc=1, device_id=across, device_id_type=MESH)
+        pl.semaphore_wait(barrier, 5)
+
+    loads = [
+        pltpu.make_async_copy(shard, whole.at[f], load_sem.at[n])
+        for n, (shard, whole) in enumerate(zip(shards, gathered))
+    ]
+    for load in loads:
+        load.start()
+
+    def spot(t, owner, half=None):
+        array, row, rows, column, columns, _ = pieces[t]
+        if half is not None:
+            columns //= 2
+            column += half * columns
+        return gathered[array].at[owner, pl.ds(row, rows), pl.ds(column, columns)]
+
+    def move(t, owner, send, recv, device, half=None):
+        target = spot(t, owner, half)
+        source = target
+        if send < 3:
+            array, row, rows, column, columns, _ = pieces[t]
+            source = shards[array].at[pl.ds(row, rows), pl.ds(column, columns)]
+        return put(source, target, send_sem.at[t, send], recv_sem.at[t, recv], device)
+
+    def own_x(t):
+        return move(t, f, 0, 0, x_side)
+
+    def own_y(t):
+        return move(t, f, 1, 1, y_side)
+
+    def own_core(t):
+        return move(t, f, 2, 4, partner)
+
+    def far_x(t):
+        return move(t, f_y, 3, 2, x_side, 0)
+
+    def far_y(t):
+        return move(t, f_x, 4, 3, y_side, 1)
+
+    def to_core(t, n):
+        return move(t, (f_x, f_y, f_far)[n], 5 + n, 5 + n, partner)
+
+    def to_z(t, n):
+        return move(t, (f_x, f_y, f_far)[n], 8 + n, 8 + n, z_side)
+
+    def brings(t, then, other=None):
+        kind = pieces[t][5]
+        if kind == 0:
+            then()
+            return
+        pl.when(z % 2 == kind - 1)(then)
+        if other is not None:
+            pl.when(z % 2 != kind - 1)(other)
+
+    def first(t):
+        own_core(t).start()
+
+        def then():
+            own_x(t).start()
+            own_y(t).start()
+
+        brings(t, then)
+
+    def second(t):
+        def then():
+            own_x(t).wait_recv()
+            far_y(t).start()
+            own_y(t).wait_recv()
+            far_x(t).start()
+            for n in range(2):
+                to_core(t, n).start()
+                if pieces[t][5]:
+                    to_z(t, n).start()
+
+        brings(t, then)
+
+    def third(t):
+        def then():
+            far_x(t).wait_recv()
+            far_y(t).wait_recv()
+            to_core(t, 2).start()
+            if pieces[t][5]:
+                to_z(t, 2).start()
+
+        brings(t, then)
+
+    def taken(t, n):
+        def other():
+            to_z(t, n).wait_recv()
+            to_core(t, n).start()
+
+        brings(t, lambda: None, other)
+
+    def whole(t):
+        own_core(t).wait_recv()
+        for n in range(3):
+            to_core(t, n).wait_recv()
+
+    def drain(t):
+        own_core(t).wait_send()
+        for n in range(3):
+            to_core(t, n).wait_send()
+
+        def then():
+            for copy in (own_x(t), own_y(t), far_x(t), far_y(t)):
+                copy.wait_send()
+            if pieces[t][5]:
+                for n in range(3):
+                    to_z(t, n).wait_send()
+
+        brings(t, then)
+
+    def copy_v(step, device):
+        return put(v_out.at[step], v_in.at[step], v_send.at[step], v_recv.at[step], device)
+
+    sides = (partner, x_side, y_side)
+
+    def statistics(i):
+        if i <= 3:
+            if i == 0:
+                v_out[0] = stats_ref[...]
+            else:
+                copy_v(i - 1, sides[i - 1]).wait_recv()
+                v_out[i] = v_out[i - 1] + v_in[i - 1]
+            if i < 3:
+                copy_v(i, sides[i]).start()
+            else:
+
+                @pl.when(outer)
+                def _():
+                    copy_v(3, z_side).start()
+
+        if i == 4:
+
+            @pl.when(inner)
+            def _():
+                copy_v(3, z_side).wait_recv()
+                v_out[4] = v_out[3] + v_in[3]
+                copy_v(4, across).start()
+
+        if i == 5:
+
+            @pl.when(inner)
+            def _():
+                copy_v(4, across).wait_recv()
+                v_out[5] = v_out[4] + v_in[4]
+                copy_v(5, z_side).start()
+                stats_out[...] = v_out[5]
+
+            @pl.when(outer)
+            def _():
+                copy_v(5, z_side).wait_recv()
+                stats_out[...] = v_in[5]
+
+    def columns_of(t):
+        array, row, rows, column, columns, _ = pieces[t]
+        weight = gathered[array][:, row : row + rows, column : column + columns]
+        return weight.reshape(-1, columns)
+
+    def embed_step():
+        pixels = stats_out[6:7, :] * (PATCH * PATCH)
+        for band in range(BANDS):
+            mean = stats_out[band : band + 1, :] / pixels
+            var = stats_out[BANDS + band : BANDS + band + 1, :] / pixels - mean * mean
+            rate = lax.rsqrt(var + EPS)
+            for part in range(PATCH * PATCH // LANES):
+                lanes = pl.ds(band * PATCH * PATCH + part * LANES, LANES)
+                inputs_ref[:, lanes] = ((picked_ref[:, lanes] - mean) * rate).astype(BF)
+        start_ref[...] = matmul(inputs_ref[...], columns_of(0)) + pos_ref[...]
+        a_ref[...] = norm_rows(start_ref[...], gains_ref[0:1, :])
+
+    def qkv_step(n):
+        qkv_ref[:, n * D : (n + 1) * D] = matmul(a_ref[...], columns_of(1 + n)).astype(BF)
+
+    def attention_step():
+        size = D // HEADS
+        lane_head = lax.broadcasted_iota(jnp.int32, (VIS, LANES), 1) // size
+
+        def group(g, _):
+            query, keys, values = [
+                qkv_ref[:, pl.ds(pl.multiple_of(n * D + g * LANES, LANES), LANES)] for n in range(3)
+            ]
+            mixed = jnp.zeros((VIS, LANES), F32)
+            for j in range(LANES // size):
+                one = jnp.where(lane_head == j, query.astype(F32), 0.0).astype(BF)
+                scores = right_t(one, keys) * size ** (-0.5) + bias_ref[...]
+                probs = jnp.exp(scores - jnp.max(scores, -1, keepdims=True))
+                probs = probs * (1.0 / jnp.sum(probs, -1, keepdims=True))
+                mixed = jnp.where(lane_head == j, matmul(probs.astype(BF), values), mixed)
+            mixed_ref[:, pl.ds(pl.multiple_of(g * LANES, LANES), LANES)] = mixed.astype(BF)
+            return 0
+
+        lax.fori_loop(0, D // LANES, group, 0)
+
+    def out_step():
+        middle_ref[...] = start_ref[...] + matmul(mixed_ref[...], columns_of(4))
+        b_ref[...] = norm_rows(middle_ref[...], gains_ref[1:2, :])
+
+    def up_step(n):
+        columns = slice(n * D, (n + 1) * D)
+        after, slope = gelu_parts(matmul(b_ref[...], columns_of(5 + n)))
+        hidden_ref[:, columns] = after.astype(BF)
+        slope_ref[:, columns] = slope
+
+    def down_step(n):
+        rows, owners = w_wide.shape[1], w_down.shape[0]
+        tall = w_down.shape[1]
+        parts = [hidden_ref[:, o * tall + n * rows : o * tall + (n + 1) * rows] for o in range(owners)]
+        total = matmul(jnp.concatenate(parts, 1), columns_of(9 + n))
+        end_ref[...] = (middle_ref[...] if n == 0 else end_ref[...]) + total
+
+    def link_step():
+        z_ref[...] = norm_rows(end_ref[...], gains_ref[2:3, :])
+        seen_ref[...] = matmul(z_ref[...], columns_of(count - 1))
+
+    work = [(6, 0, embed_step), (6, 1, partial(qkv_step, 0)), (7, 2, partial(qkv_step, 1))]
+    work += [(8, 3, partial(qkv_step, 2)), (8, None, attention_step), (9, 4, out_step)]
+    work += [(at, 5 + n, partial(up_step, n)) for n, at in enumerate((10, 10, 12, 13))]
+    work += [(at, 9 + n, partial(down_step, n)) for n, at in enumerate((13, 15, 16, 16))]
+    work += [(17, count - 1, link_step)]
+    stores = []
+
+    for load in loads:
+        load.wait()
+    first(0)
+    first(1)
+    for i in range(18):
+        if i + 2 < count:
+            first(i + 2)
+        statistics(i)
+        if i < count:
+            second(i)
+        if 0 <= i - 1 < count:
+            third(i - 1)
+        if 0 <= i - 3 < count:
+            taken(i - 3, 0)
+            taken(i - 3, 1)
+        if 0 <= i - 4 < count:
+            taken(i - 4, 2)
+        for at, piece, run in work:
+            if at != i:
+                continue
+            if piece is not None:
+                whole(piece)
+                array, row, rows, column, columns, _ = pieces[piece]
+                if array:
+                    where = (slice(None), pl.ds(row, rows), pl.ds(column, columns))
+                    store = pltpu.make_async_copy(
+                        gathered[array].at[where],
+                        (None, wide_out, down_out)[array].at[where],
+                        store_sem.at[piece],
+                    )
+                    store.start()
+                    stores.append(store)
+            run()
+    for store in stores:
+        store.wait()
+    for t in range(count):
+        drain(t)
+    for step in range(3):
+        copy_v(step, sides[step]).wait_send()
+
+    @pl.when(outer)
+    def _():
+        copy_v(3, z_side).wait_send()
+
+    @pl.when(inner)
+    def _():
+        copy_v(4, across).wait_send()
+        copy_v(5, z_side).wait_send()
+
+
+def encoder_forward(picked, stats, pos, bias, gains, embed, wide, down):
+    owners = lax.axis_size("fsdp")
+    shapes = [w.shape for w in (embed, wide, down)]
+    count = len(encoder_pieces(shapes))
+    full = [jax.ShapeDtypeStruct((owners, *shape), BF) for shape in shapes[1:]]
+    local = [
+        jax.ShapeDtypeStruct((8, LANES), F32),
+        jax.ShapeDtypeStruct((VIS, PD), BF),
+        jax.ShapeDtypeStruct((VIS, D), F32),
+        jax.ShapeDtypeStruct((VIS, D), BF),
+        jax.ShapeDtypeStruct((VIS, 3 * D), BF),
+        jax.ShapeDtypeStruct((VIS, D), BF),
+        jax.ShapeDtypeStruct((VIS, D), F32),
+        jax.ShapeDtypeStruct((VIS, D), BF),
+        jax.ShapeDtypeStruct((VIS, FF), F32),
+        jax.ShapeDtypeStruct((VIS, FF), BF),
+        jax.ShapeDtypeStruct((VIS, D), F32),
+        jax.ShapeDtypeStruct((VIS, D), BF),
+        jax.ShapeDtypeStruct((VIS, DD), F32),
+    ]
+    vmem, anywhere = pl.BlockSpec(memory_space=pltpu.VMEM), pl.BlockSpec(memory_space=pl.ANY)
+    dma = pltpu.SemaphoreType.DMA
+    wide_full, down_full, *rest = pl.pallas_call(
+        encoder_kernel,
+        out_shape=(*full, *local),
+        in_specs=[vmem] * 5 + [anywhere] * 3,
+        out_specs=(anywhere,) * 2 + (vmem,) * len(local),
+        scratch_shapes=[pltpu.VMEM((owners, *shape), BF) for shape in shapes]
+        + [
+            pltpu.VMEM((6, 8, LANES), F32),
+            pltpu.VMEM((6, 8, LANES), F32),
+            dma((3,)),
+            dma((count,)),
+            dma((count, 11)),
+            dma((count, 11)),
+            dma((6,)),
+            dma((6,)),
+        ],
+        compiler_params=pltpu.CompilerParams(
+            collective_id=1, has_side_effects=True, vmem_limit_bytes=56 * 2**20
+        ),
+        cost_estimate=pl.CostEstimate(
+            flops=2 * VIS * 14 * 2**20, bytes_accessed=200 * 2**20, transcendentals=0
+        ),
+    )(picked, stats, pos, bias, gains, embed, wide, down)
+    return (wide_full.reshape(D, -1), down_full.reshape(FF, D), *rest)
+
+
 def block_forward(h, weights, gains, bias, heads, skip):
     wqkv, wout, wup, wdown = weights
     width = h.shape[1]
@@ -629,19 +1035,18 @@
     mixed_t, lse = attend(query.T, keys, values.T, bias, width // heads)
     middle = h[skip:] + left_t(mixed_t, wout)
     normed_b = layer_norm(middle, gains[1]).astype(BF)
-    before = matmul(normed_b, wup)
-    hidden = jax.nn.gelu(before, approximate=False).astype(BF)
+    after, slope = gelu_parts(matmul(normed_b, wup))
+    hidden = after.astype(BF)
     end = middle + matmul(hidden, wdown)
-    return end, (h, normed_a, query, keys, values, mixed_t, lse, middle, normed_b, before, hidden)
+    return end, (h, normed_a, query, keys, values, mixed_t, lse, middle, normed_b, slope, hidden)
 
 
 def block_backward(saved, grad, weights, gains, bias, heads, skip):
     wqkv, wout, wup, wdown = weights
-    h, normed_a, query, keys, values, mixed_t, lse, middle, normed_b, before, hidden = saved
+    h, normed_a, query, keys, values, mixed_t, lse, middle, normed_b, slope, hidden = saved
     width = h.shape[1]
     dbranch = grad.astype(BF)
-    after, gelu_pull = jax.vjp(partial(jax.nn.gelu, approximate=False), before)
-    dbefore = gelu_pull(right_t(dbranch, wdown))[0].astype(BF)
+    dbefore = (right_t(dbranch, wdown) * slope).astype(BF)
     dmiddle, dgain_two = norm_back(middle, gains[1], right_t(dbefore, wup))
     dmiddle = dmiddle + grad
     dattn = dmiddle.astype(BF)
@@ -771,11 +1176,10 @@
     vector_avg,
 ):
     slots = pixels.shape[0]
-    w_embed, w_enc, w_enc_down, w_dec, w_dec_down = [
-        lax.all_gather(w.astype(BF), "fsdp", axis=0, tiled=True)
-        for w in (embed, wide_enc, enc_down, wide_dec, dec_down)
+    fast = (lax.axis_size("dp"), lax.axis_size("fsdp")) == (4, 8)
+    w_dec, w_dec_down = [
+        lax.all_gather(w.astype(BF), "fsdp", axis=0, tiled=True) for w in (wide_dec, dec_down)
     ]
-    enc_weights, w_link = enc_split(w_enc, w_enc_down)
     dec_weights, w_head = dec_split(w_dec, w_dec_down)
     rows_ok = valid.astype(jnp.float32)
     flags = rows_ok * masked.astype(jnp.float32)
@@ -784,12 +1188,7 @@
     band_sum = jnp.sum(weighted, axis=(0, 2))
     counts = jnp.stack([jnp.sum(rows_ok), jnp.sum(flags)])
     band_sq = jnp.sum(weighted * bands, axis=(0, 2))
-    stats = lax.psum(jnp.concatenate([band_sum, band_sq, counts]), ("dp", "fsdp"))
-    band_sum, band_sq, counts = stats[:3], stats[3:6], stats[6:]
-    n_pix = counts[0] * (PATCH * PATCH)
-    mean = band_sum / n_pix
-    var = band_sq / n_pix - mean * mean
-    count = counts[1]
+    stats = jnp.concatenate([band_sum, band_sq, counts])
 
     pick, n_seen, n_hid = arrange(valid, masked, scene_ids)
     picked_pixels = exact_pick(pick, pixels)
@@ -797,8 +1196,6 @@
         pick, jnp.concatenate([(scene_ids % 2)[:, None], coords], 1).astype(BF)
     )
     odd, coord = small[:, 0], small[:, 1:]
-    cent = picked_pixels.reshape(slots, BANDS, PATCH * PATCH) - mean[None, :, None]
-    normed = (cent * lax.rsqrt(var + EPS)[None, :, None]).reshape(slots, PD)
     level = jnp.where(odd == 0, gsd_index[0], gsd_index[1]).astype(jnp.float32)
     scale = jnp.exp2(0.5 * level - 1.0)
     index = jnp.arange(slots, dtype=jnp.int32)
@@ -817,11 +1214,37 @@
     gain_dec_out = vectors[base + 2 * DD : base + 3 * DD]
     token = vectors[base + 3 * DD :]
 
-    inputs = normed[:VIS].astype(BF)
-    h_start = matmul(inputs, w_embed) + positions(coord[:VIS], scale[:VIS], D)
-    h_end, enc_saved = block_forward(h_start, enc_weights, gains_enc, bias_enc, HEADS, 0)
-    encoded = layer_norm(h_end, gain_enc_out).astype(BF)
-    seen_out = matmul(encoded, w_link)
+    pos_enc = positions(coord[:VIS], scale[:VIS], D)
+    low_enc = [w.astype(BF) for w in (embed, wide_enc, enc_down)]
+    if fast:
+        gains = jnp.pad(vectors[: 3 * D].reshape(3, D), ((0, 5), (0, 0)))
+        stats = jnp.broadcast_to(stats[:, None], (8, LANES))
+        w_enc, w_enc_down, stats, inputs, h_start, *saved, h_end, encoded, seen_out = encoder_forward(
+            picked_pixels[:VIS], stats, pos_enc, bias_enc.T, gains, *low_enc
+        )
+        normed_a, qkv, mixed, *saved = saved
+        enc_saved = (h_start, normed_a, *jnp.split(qkv, 3, 1), mixed.T, None, *saved)
+        enc_weights, w_link = enc_split(w_enc, w_enc_down)
+        stats = stats[:, 0]
+    else:
+        stats = lax.psum(stats, ("dp", "fsdp"))
+    band_sum, band_sq, counts = stats[:3], stats[3:6], stats[6:]
+    n_pix = counts[0] * (PATCH * PATCH)
+    mean = band_sum / n_pix
+    var = band_sq / n_pix - mean * mean
+    count = counts[1]
+    cent = picked_pixels.reshape(slots, BANDS, PATCH * PATCH) - mean[None, :, None]
+    normed = (cent * lax.rsqrt(var + EPS)[None, :, None]).reshape(slots, PD)
+    if not fast:
+        w_embed, w_enc, w_enc_down = [
+            lax.all_gather(w, "fsdp", axis=0, tiled=True) for w in low_enc
+        ]
+        enc_weights, w_link = enc_split(w_enc, w_enc_down)
+        inputs = normed[:VIS].astype(BF)
+        h_start = matmul(inputs, w_embed) + pos_enc
+        h_end, enc_saved = block_forward(h_start, enc_weights, gains_enc, bias_enc, HEADS, 0)
+        encoded = layer_norm(h_end, gain_enc_out).astype(BF)
+        seen_out = matmul(encoded, w_link)
     y_start = positions(coord, scale, DD) + jnp.concatenate(
         [jnp.where(kept[:, None], seen_out, token), jnp.broadcast_to(token, (HID, DD))]
     )
@@ -864,7 +1287,7 @@
             dtoken,
         ]
     )
-    if (lax.axis_size("dp"), lax.axis_size("fsdp")) == (4, 8):
+    if fast:
         enc_parts, dec_sum, vector_grad, loss_sum = sum_gradients(
             enc_factors, encoded, dseen, inputs, dh_low, dec_sum, vector_grad, local_loss
         )

time: 633 us -> 587 us (0.927)
  Pallas kernels: 200 us -> 308 us
  waiting for transfers between devices: 79.7 us -> 0.07 us
  matrix products: 127 us -> 77.1 us
  blocking collectives: 42.4 us -> 0 us
  local copies, waits for them, and re-layouts: 80.1 us -> 89.3 us
  other arithmetic: 76.7 us -> 83.3 us
    pallas_call x0 -> x1, Pallas kernels: none -> 111 us  [encoder_forward(): pl.pallas_call(encoder_kernel, out_shape=(*full, *local), in_specs=[vmem]...]
    all_gather x5 -> x2, waiting for transfers between devices: 72.5 us -> 0.02 us  [body(): lax.all_gather(w.astype(BF), 'fsdp', axis=0, tiled=True)]
    dot_general x22 -> x15, matrix products: 85.8 us -> 35.6 us  [matmul(): return jnp.dot(left, right, preferred_element_type=jnp.float32)]
    psum x1 -> x0, blocking collectives: 42.4 us -> none  [body(): lax.psum(jnp.concatenate([band_sum, band_sq, counts]), ('dp', 'fsdp'))]
    transpose x0 -> x8, local copies, waits for them, and re-layouts: none -> 12.4 us  [the longest x3 7.24 us: block_backward(): factors = ((normed_a.T, dqkv), (mixed_t, dattn), (normed_b.T, dbefore), (...]
    reduce_scatter x1, waiting for transfers between devices: 7.08 us -> 0.01 us  [reduce_rows(): lax.psum_scatter(grad.astype(BF), 'fsdp', scatter_dimension=0, tiled=True)]
    convert_element_type x5 -> x2, other arithmetic: 9.92 us -> 3.11 us  [body(): w.astype(BF)]
    reshape x4 -> x1, local copies, waits for them, and re-layouts: 7.82 us -> 1.14 us  [sum_gradients(): first = inputs.T.reshape(owners, own, VIS)]
  transfers between devices with their start and end apart: 6 -> 3, of which waited for: 4 -> 0; matrix products, arithmetic and copies ran while one was open for 28% -> 24% of each run, Pallas kernels for 4% -> 23%
where the time goes in v4:
time: 587 us; the launch traced here: 577 us
  Pallas kernels  308 us (52%)
  local copies, waits for them, and re-layouts  89.3 us (15%)
  other arithmetic  83.3 us (14%)
  matrix products  77.1 us (13%)
  between operations  18.7 us (3%)
    pallas_call x1, Pallas kernels, sum_products(): pl.pallas_call(partial(sum_kernel, blocks, units, spots), out_shape=tuple...  149 us
    pallas_call x1, Pallas kernels, encoder_forward(): pl.pallas_call(encoder_kernel, out_shape=(*full, *local), in_specs=[vmem]...  111 us
    dot_general x10, matrix products, right_t(): lax.dot_general(left, right, (((1,), (1,)), ((), ())), preferred_element_...  37.8 us
    dot_general x15, matrix products, matmul(): return jnp.dot(left, right, preferred_element_type=jnp.float32)  35.6 us
    pallas_call x2, Pallas kernels, attend_back(): pl.pallas_call(partial(attend_back_kernel, size), grid=(groups,), out_sha...  33 us
    unnamed x195, local copies, waits for them, and re-layouts  20.4 us
    convert_element_type x5, other arithmetic, body(): outs += [buf, new, avg, new.astype(jnp.bfloat16)]  16 us
    pallas_call x1, Pallas kernels, attend(): pl.pallas_call(partial(attend_kernel, size), grid=(groups,), out_shape=(j...  14.8 us
  transfers between devices with their start and end apart: 3, of which 0 were waited for; matrix products, arithmetic and copies ran while one was open for 24% of the time, Pallas kernels for 23%

profile of v4, /device:TPU:0, one launch (start us, length us, event | category | flops | bytes accessed | tf_op | source)
XLA Modules:
  0.0 577.0 jit_solution(6446335488331710081)
XLA Ops:
  30.3 3.0 copy.147
  37.9 4.0 convert_element_type.191.wide_ref
  47.5 111.5 %shard_map.423 = (bf16[8,128,8704]{2,1,0:T(8,128)(2,1)}, bf16[8,512,1024]{2,1,0:T(8,128)(2,1)}, f32[8,128]{1,0:T(8,128)}, bf16[192,768]{1,0:T(8,128)(2,1)}, f32[...) custom-call(f32[192,768]{1,0:T(8,128)} %slice.243.picked_ref, ...), custom_call_target="tpu_custom_call" | custom-call | flops 5637144576 | bytes 209715200 | tf_op jit(solution)/shard_map/pallas_call | solution.py:1002
  163.7 3.4 reshape.351
  169.8 3.0 reduce_sum.422
  174.9 3.7 reshape.353
  202.0 14.8 %shard_map.424 = (bf16[512,576]{1,0:T(8,128)(2,1)S(1)}, f32[4,4,576]{2,1,0:T(4,128)S(1)}) custom-call(bf16[512,576]{1,0:T(8,128)(2,1)S(1)} %copy-done.3, bf16[768,512]{1,0:T(8,128)(2,1)S(1)} %copy.153.k_ref, bf16[512,768]{1,0:T(8,128)(2,1)S(1)} %copy-done.1, f32[768,576]{1,0:T(8,128)S(1)} %slice.255.bias_ref), custom_call_target="tpu_custom_call" | custom-call | flops 3623878656 | bytes 1769472 | tf_op jit(solution)/shard_map/pallas_call | solution.py:108
  218.8 5.7 multiply_convert_fusion.1
  224.5 3.8 fusion.119
  238.8 3.2 convolution_convert_fusion.1
  242.0 4.0 multiply_convert_fusion
  246.1 3.3 convolution_convert_fusion.2
  255.8 25.7 %shard_map.425 = (bf16[512,576]{1,0:T(8,128)(2,1)S(1)}, bf16[768,512]{1,0:T(8,128)(2,1)S(1)}, bf16[768,512]{1,0:T(8,128)(2,1)S(1)}) custom-call(bf16[512,576]{1,0:T(8,128)(2,1)S(1)} %copy-done.4, bf16[576,512]{1,0:T(8,128)(2,1)S(1)} %copy-done.6, bf16[768,512]{1,0:T(8,128)(2,1)S(1)} %copy.153.k_ref, bf16[512,768]{1,0:T(8,128)(2,1)} %bitcast.106, ...), custom_call_target="tpu_custom_call" | custom-call | flops 9059696640 | bytes 1769472 | tf_op jit(solution)/shard_map/pallas_call | solution.py:179
  283.6 4.3 convolution_convert_fusion
  287.9 3.7 multiply_reduce_fusion.1
  299.5 12.0 %concatenate.38 = bf16[512,7104]{1,0:T(8,128)(2,1)} concatenate(bf16[512,1536]{1,0:T(8,128)(2,1)} %convolution_convert_fusion, bf16[512,512]{1,0:T(8,128)(2,1)} %convolution_convert_fusion.8, bf16[512,2048]{1,0:T(8,128)(2,1)} %convolution_convert_fusion.2, bf16[512,960]{1,0:T(8,128)(2,1)S(1)} %copy.158, bf16[512,2048]{1,0:T(8,128)(2,1)S(1)} %bitcast.91), dimensions={1} | concatenate | bytes 14548992 | tf_op jit(solution)/shard_map/concatenate | solution.py:1266
  324.1 4.2 copy.167
  341.5 6.4 %fusion.4.refs_8_ = bf16[192,4096]{1,0:T(8,128)(2,1)S(1)} fusion(f32[192,4096]{1,0:T(8,128)S(1)} %copy-done.45, bf16[192,1024]{1,0:T(8,128)(2,1)S(1)} %add_convert_fusion.3.refs_9_, bf16[4096,1024]{1,0:T(8,128)(2,1)} %bitcast.92), kind=kOutput, calls=%fused_computation.5 | convolution fusion | flops 1612185600 | bytes 13500416 | tf_op jit(solution)/shard_map/dot_general | solution.py:46
  347.9 7.8 %multiply_reduce_fusion.12 = (f32[1024]{0:T(1024)}, f32[192]{0:T(256)S(1)}, f32[192,1024]{1,0:T(8,128)S(1)}) fusion(f32[192,1024]{1,0:T(8,128)S(1)} %copy-done.36, f32[192]{0:T(256)S(1)} %fusion.83, f32[192]{0:T(256)S(1)} %broadcast_multiply_fusion.4, f32[1024]{0:T(1024)S(1)} %get-tuple-element.162, bf16[192,4096]{1,0:T(8,128)(2,1)S(1)} %fusion.4.refs_8_, ...), kind=kOutput, calls=%fused_computation.109 | convolution fusion | flops 1611987712 | bytes 11544832 | tf_op jit(solution)/shard_map/dot_general | solution.py:46
  360.4 7.3 %shard_map.426 = (bf16[1024,192]{1,0:T(8,128)(2,1)S(1)}, bf16[192,1024]{1,0:T(8,128)(2,1)S(1)}, bf16[192,1024]{1,0:T(8,128)(2,1)S(1)}) custom-call(bf16[1024,192]{1,0:T(8,128)(2,1)S(1)} %copy.160.qt_ref, bf16[192,1024]{1,0:T(8,128)(2,1)S(1)} %get-tuple-element.160.q_ref, bf16[192,1024]{1,0:T(8,128)(2,1)S(1)} %copy.161.k_ref, ...), custom_call_target="tpu_custom_call" | custom-call | flops 754974720 | bytes 147456 | tf_op jit(solution)/shard_map/pallas_call | solution.py:179
  373.1 6.4 %multiply_reduce_fusion.10 = (f32[192]{0:T(256)}, f32[1024]{0:T(1024)}, f32[192,1024]{1,0:T(8,128)S(1)}) fusion(f32[192,1024]{1,0:T(8,128)} %get-tuple-element.55, f32[1024]{0:T(1024)S(1)} %get-tuple-element.161, f32[192]{0:T(256)} %copy-done.82, f32[192]{0:T(256)} %fusion.81, bf16[1024,8704]{1,0:T(8,128)(2,1)} %bitcast.128, ...), kind=kOutput, calls=%fused_computation.107 | convolution fusion | flops 1212873472 | bytes 9054976 | tf_op jit(solution)/shard_map/dot_general | solution.py:46
  388.6 149.1 %shard_map.427 = (bf16[96,1024]{1,0:T(8,128)(2,1)}, bf16[128,8704]{1,0:T(8,128)(2,1)}, bf16[512,1024]{1,0:T(8,128)(2,1)}, bf16[64,7168]{1,0:T(8,128)(2,1)}, f32[48,128]{1,0:T(8,128)}) custom-call(f32[48,128]{1,0:T(8,128)} %bitcast.120, bf16[64,7168]{1,0:T(8,128)(2,1)} %pad.31.dec_ref, bf16[4,2,128,192]{3,2,1,0:T(8,128)(2,1)} %bitcast.110, ...), custom_call_target="tpu_custom_call" | custom-call | flops 5435817984 | bytes 314572800 | tf_op jit(solution)/shard_map/pallas_call | solution.py:584
  546.6 7.9 %fusion.100 = (bf16[128,8704]{1,0:T(8,128)(2,1)}, f32[128,8704]{1,0:T(8,128)S(1)}, f32[128,8704]{1,0:T(8,128)}) fusion(f32[128,8704]{1,0:T(8,128)} %param.31, bf16[128,8704]{1,0:T(8,128)(2,1)S(1)} %copy-done.47, f32[128,8704]{1,0:T(8,128)} %param.37), kind=kLoop, calls=%fused_computation.256 | loop fusion | flops 11141120 | bytes 22282240 | tf_op jit(solution)/shard_map/convert_element_type | solution.py:1323
  554.5 6.7 %multiply_add_fusion = f32[128,8704]{1,0:T(8,128)} fusion(f32[128,8704]{1,0:T(8,128)S(1)} %get-tuple-element.122, f32[128,8704]{1,0:T(8,128)} %param.43), kind=kLoop, calls=%fused_computation.11 | loop fusion | flops 3342336 | bytes 13369344 | tf_op jit(solution)/shard_map/add | solution.py:1124
  (373 shorter events, 153.4 us)
Async XLA Ops:
  7.2 7.6 %copy-start.25 = (f32[768,768]{1,0:T(8,128)S(1)}, f32[768,768]{1,0:T(8,128)}, u32[]{:S(2)}) copy-start(f32[768,768]{1,0:T(8,128)} %param.24) | copy-start | bytes 7077892
  7.2 180.6 %all-gather.3.cloned.1.call-start = ((), (), s32[]{:S(2)}) async-start(), calls=%async_computation.1 | async-start | bytes 5898240 | tf_op jit(solution)/shard_map/all_gather | solution.py:1181
  9.7 214.8 %all-gather.5.cloned.1.call-start = ((), (), s32[]{:S(2)}) async-start(), calls=%async_computation.2 | async-start | bytes 2359296 | tf_op jit(solution)/shard_map/all_gather | solution.py:1181
  10.5 375.9 %reduce-scatter.2.cloned.1.call-start = ((), (), s32[]{:S(2)}) async-start(), calls=%async_computation.3 | async-start | bytes 8257536 | tf_op jit(solution)/shard_map/reduce_scatter | solution.py:1066
  26.8 172.9 %copy-start = (f32[768,576]{1,0:T(8,128)}, f32[768,576]{1,0:T(8,128)S(1)}, u32[]{:S(2)}) copy-start(f32[768,576]{1,0:T(8,128)S(1)} %slice.255.bias_ref) | copy-start | bytes 5308420
  47.5 114.3 %copy-start.30 = (f32[768,768]{0,1:T(8,128)S(1)}, f32[768,768]{0,1:T(8,128)}, u32[]{:S(2)}) copy-start(f32[768,768]{0,1:T(8,128)} %copy.147) | copy-start | bytes 7077892
  189.7 5.0 copy-start.5
  202.0 14.8 %copy-start.17 = (f32[768,512]{1,0:T(8,128)S(1)}, f32[768,512]{1,0:T(8,128)}, u32[]{:S(2)}) copy-start(f32[768,512]{1,0:T(8,128)} %copy-done.16) | copy-start | bytes 4718596
  316.4 6.7 %copy-start.66 = (bf16[192,1024]{1,0:T(8,128)(2,1)S(1)}, bf16[192,1024]{1,0:T(8,128)(2,1)}, u32[]{:S(2)}) copy-start(bf16[192,1024]{1,0:T(8,128)(2,1)} %get-tuple-element.76) | copy-start | bytes 1179652
  339.5 16.6 %copy-start.22 = (f32[192,1024]{1,0:T(8,128)}, f32[192,1024]{1,0:T(8,128)S(1)}, u32[]{:S(2)}) copy-start(f32[192,1024]{1,0:T(8,128)S(1)} %get-tuple-element.132) | copy-start | bytes 2359300
  339.5 16.6 %copy-start.80 = (f32[192]{0:T(256)}, f32[192]{0:T(256)S(1)}, u32[]{:S(2)}) copy-start(f32[192]{0:T(256)S(1)} %negate_multiply_fusion.5) | copy-start | bytes 2308
  339.7 8.2 %copy-start.54 = (bf16[192,1024]{1,0:T(8,128)(2,1)}, bf16[192,1024]{1,0:T(8,128)(2,1)S(1)}, u32[]{:S(2)}) copy-start(bf16[192,1024]{1,0:T(8,128)(2,1)S(1)} %add_convert_fusion.3.refs_9_) | copy-start | bytes 1179652
  341.5 6.4 %copy-start.36 = (f32[192,1024]{1,0:T(8,128)S(1)}, f32[192,1024]{1,0:T(8,128)}, u32[]{:S(2)}) copy-start(f32[192,1024]{1,0:T(8,128)} %get-tuple-element.69) | copy-start | bytes 2359300
  347.9 7.9 %copy-start.55 = (bf16[192,4096]{1,0:T(8,128)(2,1)}, bf16[192,4096]{1,0:T(8,128)(2,1)S(1)}, u32[]{:S(2)}) copy-start(bf16[192,4096]{1,0:T(8,128)(2,1)S(1)} %fusion.4.refs_8_) | copy-start | bytes 4718596
  373.1 9.3 %copy-start.34 = (f32[192,1024]{1,0:T(8,128)S(1)}, f32[192,1024]{1,0:T(8,128)}, u32[]{:S(2)}) copy-start(f32[192,1024]{1,0:T(8,128)} %get-tuple-element.55) | copy-start | bytes 2359300
  373.1 9.3 %copy-start.83 = (f32[192]{0:T(256)S(1)}, f32[192]{0:T(256)}, u32[]{:S(2)}) copy-start(f32[192]{0:T(256)} %copy-done.82) | copy-start | bytes 2308
  388.5 150.2 %copy-start.42 = (f32[64,5056]{1,0:T(8,128)S(1)}, f32[64,5056]{1,0:T(8,128)}, u32[]{:S(2)}) copy-start(f32[64,5056]{1,0:T(8,128)} %param.33) | copy-start | bytes 3883012
  388.6 150.2 %copy-start.59 = (f32[64,5056]{1,0:T(8,128)S(1)}, f32[64,5056]{1,0:T(8,128)}, u32[]{:S(2)}) copy-start(f32[64,5056]{1,0:T(8,128)} %param.39) | copy-start | bytes 3883012
  541.6 24.1 %copy-start.43 = (f32[64,5056]{1,0:T(8,128)}, f32[64,5056]{1,0:T(8,128)S(1)}, u32[]{:S(2)}) copy-start(f32[64,5056]{1,0:T(8,128)S(1)} %get-tuple-element.116) | copy-start | bytes 3883012
  545.7 8.8 %copy-start.58 = (f32[96,1024]{1,0:T(8,128)}, f32[96,1024]{1,0:T(8,128)S(1)}, u32[]{:S(2)}) copy-start(f32[96,1024]{1,0:T(8,128)S(1)} %get-tuple-element.125) | copy-start | bytes 1179652
  554.5 6.8 %copy-start.21 = (f32[128,8704]{1,0:T(8,128)}, f32[128,8704]{1,0:T(8,128)S(1)}, u32[]{:S(2)}) copy-start(f32[128,8704]{1,0:T(8,128)S(1)} %get-tuple-element.122) | copy-start | bytes 13369348
  554.5 6.8 %copy-start.29 = (f32[512,1024]{1,0:T(8,128)S(1)}, f32[512,1024]{1,0:T(8,128)}, u32[]{:S(2)}) copy-start(f32[512,1024]{1,0:T(8,128)} %param.32) | copy-start | bytes 6291460
  554.5 6.8 %copy-start.48 = (f32[512,1024]{1,0:T(8,128)S(1)}, f32[512,1024]{1,0:T(8,128)}, u32[]{:S(2)}) copy-start(f32[512,1024]{1,0:T(8,128)} %param.38) | copy-start | bytes 6291460
  554.5 6.7 %copy-start.61 = (bf16[512,1024]{1,0:T(8,128)(2,1)S(1)}, bf16[512,1024]{1,0:T(8,128)(2,1)}, u32[]{:S(2)}) copy-start(bf16[512,1024]{1,0:T(8,128)(2,1)} %get-tuple-element.82) | copy-start | bytes 3145732
  (77 other events, 183.5 us)
Sparse Core Ops, SparseCore 0:
  10.5 43.8 all-gather.2
  56.9 36.5 all-gather.4
  311.6 67.7 reduce-scatter.1

commit v5 on v4

--- a/solution.py
+++ b/solution.py
@@ -1025,6 +1025,314 @@
     return (wide_full.reshape(D, -1), down_full.reshape(FF, D), *rest)
 
 
+LOWP = 256
+HEADP = PD + LOWP
+BLOCK = HID // 2
+
+
+def normalize(h):
+    cent = h - jnp.mean(h, -1, keepdims=True)
+    rate = lax.rsqrt(jnp.mean(cent * cent, -1, keepdims=True) + EPS)
+    return cent * rate, rate
+
+
+def normalize_back(unit, rate, gain, grad):
+    scaled = grad * gain
+    along = jnp.mean(scaled * unit, -1, keepdims=True)
+    dh = rate * (scaled - jnp.mean(scaled, -1, keepdims=True) - unit * along)
+    return dh, jnp.sum(grad * unit, 0, keepdims=True)
+
+
+def exact_product(array, weight):
+    high = array.astype(BF)
+    rest = array - high.astype(F32)
+    mid = rest.astype(BF)
+    low = (rest - mid.astype(F32)).astype(BF)
+    return matmul(high, weight) + matmul(mid, weight) + matmul(low, weight)
+
+
+def decoder_kernel(
+    owners,
+    pos_ref,
+    seen_ref,
+    kept_ref,
+    flag_ref,
+    picked_ref,
+    stats_ref,
+    bias_ref,
+    gains_ref,
+    pool_ref,
+    spread_ref,
+    wide_ref,
+    down_ref,
+    grads_ref,
+    dy_ref,
+    vec_ref,
+    y_ref,
+    a_ref,
+    q_ref,
+    k_ref,
+    v_ref,
+    mixed_t,
+    mixed_ref,
+    lse_ref,
+    head_ref,
+    b_ref,
+    hidden_ref,
+    z_ref,
+    dpred_ref,
+    dbranch_ref,
+    dbefore_ref,
+    dattn_ref,
+    dmixed_ref,
+    dmiddle_ref,
+    dq_ref,
+    dk_ref,
+    dv_ref,
+    loss_ref,
+):
+    size = DD // DHEADS
+    per = LANES // size
+    factor = size ** (-0.5)
+    gain_one, gain_two, gain_out = [gains_ref[n : n + 1, :] for n in range(3)]
+    token = gains_ref[3:4, :]
+    lane_head = lax.broadcasted_iota(jnp.int32, (HID, LANES), 1) // size
+    key_head = lax.broadcasted_iota(jnp.int32, (TOK_DEV, LANES), 1) // size
+    vec_ref[...] = jnp.zeros_like(vec_ref)
+    loss_ref[...] = jnp.zeros_like(loss_ref)
+    head_ref[...] = jnp.zeros_like(head_ref)
+    head_ref[:, : PD + LOWD] = wide_ref[:, 4 * DD + DFF :]
+
+    def project(rows, with_query):
+        a = (normalize(y_ref[rows, :])[0] * gain_one).astype(BF)
+        a_ref[rows, :] = a
+        k_ref[rows, :] = matmul(a, wide_ref[:, DD : 2 * DD]).astype(BF)
+        v_ref[rows, :] = matmul(a, wide_ref[:, 2 * DD : 3 * DD]).astype(BF)
+        return a
+
+    y_ref[:VIS, :] = pos_ref[:VIS, :] + jnp.where(kept_ref[...] > 0, seen_ref[...], token)
+    y_ref[VIS:, :] = pos_ref[VIS:, :] + token
+    project(slice(0, VIS), False)
+
+    def hidden_rows(n):
+        start = pl.multiple_of(n * BLOCK, BLOCK)
+        return pl.ds(start, BLOCK), pl.ds(pl.multiple_of(start + VIS, 32), BLOCK)
+
+    def project_hidden(n, _):
+        rows, all_rows = hidden_rows(n)
+        a = project(all_rows, True)
+        q_ref[rows, :] = matmul(a, wide_ref[:, :DD]).astype(BF)
+        return 0
+
+    lax.fori_loop(0, 2, project_hidden, 0)
+
+    def only(array, head_of, j):
+        return jnp.where(head_of == j, array.astype(F32), 0.0).astype(BF)
+
+    def attend_group(g, _):
+        lanes = pl.ds(pl.multiple_of(g * LANES, LANES), LANES)
+        keys, query = k_ref[:, lanes], q_ref[:, lanes]
+        values_t = v_ref[:, lanes].T
+        for j in range(per):
+            scores = right_t(keys, only(query, lane_head, j)) * factor + bias_ref[...]
+            top = jnp.max(scores, 0, keepdims=True)
+            probs = jnp.exp(scores - top)
+            total = jnp.sum(probs, 0, keepdims=True)
+            probs = (probs * (1.0 / total)).astype(BF)
+            rows = slice(j * size, (j + 1) * size)
+            mixed_t[g, rows, :] = matmul(values_t[rows, :], probs).astype(BF)
+            lse_ref[g, j : j + 1, :] = top + jnp.log(total)
+        mixed_ref[:, lanes] = mixed_t[g].T
+        return 0
+
+    lax.fori_loop(0, DD // LANES, attend_group, 0)
+
+    pixels = stats_ref[6:7, :] * (PATCH * PATCH)
+    flagged = stats_ref[7:8, 0:1]
+
+    def follow(n, _):
+        rows, all_rows = hidden_rows(n)
+        middle = y_ref[all_rows, :] + matmul(mixed_ref[rows, :], wide_ref[:, 3 * DD : 4 * DD])
+        unit_b, rate_b = normalize(middle)
+        b = (unit_b * gain_two).astype(BF)
+        b_ref[rows, :] = b
+        after, slope = gelu_parts(matmul(b, wide_ref[:, 4 * DD : 4 * DD + DFF]))
+        hidden_ref[rows, :] = after.astype(BF)
+        unit_z, rate_z = normalize(middle + matmul(hidden_ref[rows, :], down_ref[...]))
+        z = (unit_z * gain_out).astype(BF)
+        z_ref[rows, :] = z
+        pred = matmul(z, head_ref[...])
+        parts = []
+        for part in range(PD // LANES):
+            band = part * LANES // (PATCH * PATCH)
+            mean = stats_ref[band : band + 1, :] / pixels
+            var = stats_ref[BANDS + band : BANDS + band + 1, :] / pixels - mean * mean
+            lanes = slice(part * LANES, (part + 1) * LANES)
+            parts.append((picked_ref[rows, lanes] - mean) * lax.rsqrt(var + EPS))
+        normed = jnp.concatenate(parts, 1)
+        coarse = exact_product(normed, pool_ref[...])
+        err_high = pred[:, :PD] - (normed - exact_product(coarse, spread_ref[...]))
+        err_low = pred[:, PD:] - coarse
+        flag = flag_ref[rows, :]
+        length = jnp.sqrt(err_high * err_high + 1.0)
+        loss_ref[:, :PD] += jnp.sum((length - 1.0) * flag, 0, keepdims=True) * (1.0 / PD)
+        loss_ref[:, PD:] += jnp.sum(err_low * err_low * flag, 0, keepdims=True) * (1.0 / LOWD)
+        share = flag / flagged
+        dpred_ref[rows, :PD] = (err_high / length * (share * (1.0 / PD))).astype(BF)
+        dpred_ref[rows, PD:] = (err_low * (share * (2.0 / LOWD))).astype(BF)
+        dz = right_t(dpred_ref[rows, :], head_ref[...])
+        dend, dgain = normalize_back(unit_z, rate_z, gain_out, dz)
+        vec_ref[2:3, :] += dgain
+        dbranch_ref[rows, :] = dend.astype(BF)
+        dhidden = right_t(dbranch_ref[rows, :], down_ref[...])
+        dbefore_ref[rows, :] = (dhidden * slope).astype(BF)
+        db = right_t(dbefore_ref[rows, :], wide_ref[:, 4 * DD : 4 * DD + DFF])
+        dmiddle, dgain = normalize_back(unit_b, rate_b, gain_two, db)
+        vec_ref[1:2, :] += dgain
+        dmiddle = dmiddle + dend
+        dmiddle_ref[rows, :] = dmiddle
+        dattn_ref[rows, :] = dmiddle.astype(BF)
+        dmixed = right_t(dattn_ref[rows, :], wide_ref[:, 3 * DD : 4 * DD])
+        dmixed_ref[rows, :] = dmixed.astype(BF)
+        return 0
+
+    lax.fori_loop(0, 2, follow, 0)
+
+    tall = DFF // owners
+    rows = DD // owners
+    down_grad = left_t(hidden_ref[...], dbranch_ref[...]).astype(BF)
+    for owner in range(owners):
+        for part in range(tall // rows):
+            start = owner * tall + part * rows
+            grads_ref[owner * rows : (owner + 1) * rows, part * DD : (part + 1) * DD] = down_grad[
+                start : start + rows, :
+            ]
+    wide = DFF
+    for g in range(DD // LANES):
+        grads_ref[g * LANES : (g + 1) * LANES, wide + 3 * DD : wide + 4 * DD] = matmul(
+            mixed_t[g], dattn_ref[...]
+        ).astype(BF)
+    grads_ref[:, wide + 4 * DD : wide + 4 * DD + DFF] = left_t(
+        b_ref[...], dbefore_ref[...]
+    ).astype(BF)
+    grads_ref[:, wide + 4 * DD + DFF :] = left_t(z_ref[...], dpred_ref[...]).astype(BF)[
+        :, : PD + LOWD
+    ]
+
+    def attend_back_group(g, _):
+        lanes = pl.ds(pl.multiple_of(g * LANES, LANES), LANES)
+        query, keys, values, dout = [r[:, lanes] for r in (q_ref, k_ref, v_ref, dmixed_ref)]
+        keys_t = keys.T
+        dkeys = jnp.zeros((TOK_DEV, LANES), F32)
+        dvalues = jnp.zeros((TOK_DEV, LANES), F32)
+        dquery = []
+        for j in range(per):
+            scores = right_t(keys, only(query, lane_head, j)) * factor + bias_ref[...]
+            probs = jnp.exp(scores - lse_ref[g, j : j + 1, :])
+            dvalues = jnp.where(key_head == j, matmul(probs.astype(BF), dout), dvalues)
+            dprobs = right_t(values, only(dout, lane_head, j))
+            delta = jnp.sum(dprobs * probs, 0, keepdims=True)
+            dscores = (probs * (dprobs - delta)).astype(BF)
+            dkeys = jnp.where(key_head == j, matmul(dscores, query), dkeys)
+            dquery.append(matmul(keys_t[j * size : (j + 1) * size, :], dscores))
+        dq_ref[:, lanes] = (jnp.concatenate(dquery, 0) * factor).astype(BF).T
+        dk_ref[:, lanes] = (dkeys * factor).astype(BF)
+        dv_ref[:, lanes] = dvalues.astype(BF)
+        return 0
+
+    lax.fori_loop(0, DD // LANES, attend_back_group, 0)
+
+    for n, ref in enumerate((dk_ref, dv_ref)):
+        grads_ref[:, wide + (n + 1) * DD : wide + (n + 2) * DD] = left_t(
+            a_ref[...], ref[...]
+        ).astype(BF)
+    grads_ref[:, wide : wide + DD] = left_t(a_ref[VIS:, :], dq_ref[...]).astype(BF)
+
+    def start_rows(rows, da):
+        unit, rate = normalize(y_ref[rows, :])
+        da = da + right_t(dk_ref[rows, :], wide_ref[:, DD : 2 * DD])
+        da = da + right_t(dv_ref[rows, :], wide_ref[:, 2 * DD : 3 * DD])
+        dh, dgain = normalize_back(unit, rate, gain_one, da)
+        vec_ref[0:1, :] += dgain
+        return dh
+
+    dy = start_rows(slice(0, VIS), 0.0)
+    dy_ref[...] = dy
+    vec_ref[3:4, :] += jnp.sum(jnp.where(kept_ref[...] > 0, 0.0, dy), 0, keepdims=True)
+
+    def start_hidden(n, _):
+        rows, all_rows = hidden_rows(n)
+        dy = start_rows(all_rows, right_t(dq_ref[rows, :], wide_ref[:, :DD]))
+        vec_ref[3:4, :] += jnp.sum(dy + dmiddle_ref[rows, :], 0, keepdims=True)
+        return 0
+
+    lax.fori_loop(0, 2, start_hidden, 0)
+    vec_ref[4:5, :] = loss_ref[:, :DD] + loss_ref[:, DD:]
+
+
+def decoder_step(pos, seen, kept, flag, picked, stats, bias, vectors, wide, down):
+    index = jnp.arange(PD)
+    band, row, column = index // PATCH**2, index // PATCH % PATCH, index % PATCH
+    low = band * (PATCH // 2) ** 2 + row // 2 * (PATCH // 2) + column // 2
+    spread = low[None, :] == jnp.arange(LOWP)[:, None]
+    gains = jnp.pad(vectors.reshape(4, DD), ((0, 4), (0, 0)))
+    owners = lax.axis_size("fsdp")
+    scratch = [
+        ((TOK_DEV, DD), F32),
+        ((TOK_DEV, DD), BF),
+        ((HID, DD), BF),
+        ((TOK_DEV, DD), BF),
+        ((TOK_DEV, DD), BF),
+        ((DD // LANES, LANES, HID), BF),
+        ((HID, DD), BF),
+        ((DD // LANES, LANES * DHEADS // DD, HID), F32),
+        ((DD, HEADP), BF),
+        ((HID, DD), BF),
+        ((HID, DFF), BF),
+        ((HID, DD), BF),
+        ((HID, HEADP), BF),
+        ((HID, DD), BF),
+        ((HID, DFF), BF),
+        ((HID, DD), BF),
+        ((HID, DD), BF),
+        ((HID, DD), F32),
+        ((HID, DD), BF),
+        ((TOK_DEV, DD), BF),
+        ((TOK_DEV, DD), BF),
+        ((1, HEADP), F32),
+    ]
+    vmem = pl.BlockSpec(memory_space=pltpu.VMEM)
+    grads, dy, vec = pl.pallas_call(
+        partial(decoder_kernel, owners),
+        out_shape=(
+            jax.ShapeDtypeStruct((DD, DFF + wide.shape[1]), BF),
+            jax.ShapeDtypeStruct((VIS, DD), F32),
+            jax.ShapeDtypeStruct((8, DD), F32),
+        ),
+        in_specs=[vmem] * 12,
+        out_specs=(vmem,) * 3,
+        scratch_shapes=[pltpu.VMEM(*entry) for entry in scratch],
+        compiler_params=pltpu.CompilerParams(vmem_limit_bytes=60 * 2**20),
+        cost_estimate=pl.CostEstimate(
+            flops=40 * 10**9, bytes_accessed=40 * 2**20, transcendentals=2 * 10**7
+        ),
+    )(
+        pos,
+        seen,
+        kept.astype(F32)[:, None],
+        flag[:, None],
+        picked,
+        stats,
+        bias,
+        gains,
+        (spread.T * 0.25).astype(BF),
+        spread.astype(BF),
+        wide,
+        down,
+    )
+    return grads, dy, vec[:3], vec[3], jnp.sum(vec[4])
+
+
 def block_forward(h, weights, gains, bias, heads, skip):
     wqkv, wout, wup, wdown = weights
     width = h.shape[1]
@@ -1107,13 +1415,6 @@
     return (
         (wide[:, : 3 * D], wide[:, 3 * D : 4 * D], wide[:, 4 * D : 4 * D + FF], down),
         wide[:, 4 * D + FF :],
-    )
-
-
-def dec_split(wide, down):
-    return (
-        (wide[:, : 3 * DD], wide[:, 3 * DD : 4 * DD], wide[:, 4 * DD : 4 * DD + DFF], down),
-        wide[:, 4 * DD + DFF :],
     )
 
 
@@ -1180,7 +1481,6 @@
     w_dec, w_dec_down = [
         lax.all_gather(w.astype(BF), "fsdp", axis=0, tiled=True) for w in (wide_dec, dec_down)
     ]
-    dec_weights, w_head = dec_split(w_dec, w_dec_down)
     rows_ok = valid.astype(jnp.float32)
     flags = rows_ok * masked.astype(jnp.float32)
     bands = pixels.reshape(slots, BANDS, PATCH * PATCH)
@@ -1209,11 +1509,6 @@
 
     gains_enc = (vectors[:D], vectors[D : 2 * D])
     gain_enc_out = vectors[2 * D : 3 * D]
-    base = 3 * D
-    gains_dec = (vectors[base : base + DD], vectors[base + DD : base + 2 * DD])
-    gain_dec_out = vectors[base + 2 * DD : base + 3 * DD]
-    token = vectors[base + 3 * DD :]
-
     pos_enc = positions(coord[:VIS], scale[:VIS], D)
     low_enc = [w.astype(BF) for w in (embed, wide_enc, enc_down)]
     if fast:
@@ -1225,52 +1520,37 @@
         normed_a, qkv, mixed, *saved = saved
         enc_saved = (h_start, normed_a, *jnp.split(qkv, 3, 1), mixed.T, None, *saved)
         enc_weights, w_link = enc_split(w_enc, w_enc_down)
-        stats = stats[:, 0]
     else:
-        stats = lax.psum(stats, ("dp", "fsdp"))
-    band_sum, band_sq, counts = stats[:3], stats[3:6], stats[6:]
-    n_pix = counts[0] * (PATCH * PATCH)
-    mean = band_sum / n_pix
-    var = band_sq / n_pix - mean * mean
-    count = counts[1]
-    cent = picked_pixels.reshape(slots, BANDS, PATCH * PATCH) - mean[None, :, None]
-    normed = (cent * lax.rsqrt(var + EPS)[None, :, None]).reshape(slots, PD)
+        stats = jnp.broadcast_to(lax.psum(stats, ("dp", "fsdp"))[:, None], (8, LANES))
+    count = stats[7, 0]
     if not fast:
         w_embed, w_enc, w_enc_down = [
             lax.all_gather(w, "fsdp", axis=0, tiled=True) for w in low_enc
         ]
         enc_weights, w_link = enc_split(w_enc, w_enc_down)
-        inputs = normed[:VIS].astype(BF)
+        mean = jnp.repeat(stats[:3, 0] / (stats[6, 0] * (PATCH * PATCH)), PATCH * PATCH)
+        square = jnp.repeat(stats[3:6, 0] / (stats[6, 0] * (PATCH * PATCH)), PATCH * PATCH)
+        rate = lax.rsqrt(square - mean * mean + EPS)
+        inputs = ((picked_pixels[:VIS] - mean) * rate).astype(BF)
         h_start = matmul(inputs, w_embed) + pos_enc
         h_end, enc_saved = block_forward(h_start, enc_weights, gains_enc, bias_enc, HEADS, 0)
         encoded = layer_norm(h_end, gain_enc_out).astype(BF)
         seen_out = matmul(encoded, w_link)
-    y_start = positions(coord, scale, DD) + jnp.concatenate(
-        [jnp.where(kept[:, None], seen_out, token), jnp.broadcast_to(token, (HID, DD))]
+    pos_dec = positions(coord, scale, DD)
+    dec_grads, dy_seen, dgains_dec, dtoken, local_loss = decoder_step(
+        pos_dec,
+        seen_out,
+        kept,
+        hidden_ok.astype(F32),
+        picked_pixels[VIS:],
+        stats,
+        bias_dec,
+        vectors[3 * D :],
+        w_dec,
+        w_dec_down,
     )
-    y_end, dec_saved = block_forward(y_start, dec_weights, gains_dec, bias_dec, DHEADS, VIS)
-    decoded = layer_norm(y_end, gain_dec_out).astype(BF)
-    pred = matmul(decoded, w_head)
-    flag = hidden_ok.astype(jnp.float32)
-    losses, loss_pull = jax.vjp(lambda values: row_loss(values, normed[VIS:]), pred)
-    local_loss = jnp.sum(flag * losses)
-    dpred = loss_pull(flag / count)[0].astype(BF)
-    dy_end, dgain_dec_out = norm_back(y_end, gain_dec_out, right_t(dpred, w_head))
-    dy_start, dec_factors, dgains_dec = block_backward(
-        dec_saved, dy_end, dec_weights, gains_dec, bias_dec, DHEADS, VIS
-    )
-    owners = lax.axis_size("fsdp")
-    dec_grads = [matmul(*pair).astype(BF) for pair in dec_factors]
-    down_grad = dec_grads[3].reshape(owners, -1, DD // owners, DD)
-    down_grad = down_grad.transpose(0, 2, 1, 3).reshape(DD, DFF)
-    dec_grads = jnp.concatenate(
-        [*dec_grads[:3], left_t(decoded, dpred).astype(BF), down_grad], 1
-    )
-    dy_start, dec_grads = lax.optimization_barrier((dy_start, dec_grads))
     dec_sum = reduce_rows(dec_grads)
-    picked = dy_start[:VIS] * keptf
-    dtoken = jnp.sum(dy_start, 0) - jnp.sum(picked, 0)
-    dseen = picked.astype(BF)
+    dseen = (dy_seen * keptf).astype(BF)
     dh_end, dgain_enc_out = norm_back(h_end, gain_enc_out, right_t(dseen, w_link))
     dh_start, enc_factors, dgains_enc = block_backward(
         enc_saved, dh_end, enc_weights, gains_enc, bias_enc, HEADS, 0
@@ -1281,9 +1561,7 @@
             dgains_enc[0],
             dgains_enc[1],
             dgain_enc_out,
-            dgains_dec[0],
-            dgains_dec[1],
-            dgain_dec_out,
+            dgains_dec.reshape(-1),
             dtoken,
         ]
     )
@@ -1307,9 +1585,8 @@
         vector_grad, loss_sum = lax.psum((vector_grad, local_loss), ("dp", "fsdp"))
         dec_sum = lax.psum(dec_sum, "dp")
     rows = dec_sum.shape[0]
-    wide = wide_dec.shape[1]
-    down = dec_sum[:, wide:].reshape(rows, -1, DD).transpose(1, 0, 2).reshape(-1, DD)
-    dec_parts = (dec_sum[:, :wide], down)
+    down = dec_sum[:, :DFF].reshape(rows, -1, DD).transpose(1, 0, 2).reshape(-1, DD)
+    dec_parts = (dec_sum[:, DFF:], down)
     shard_grads = [g.astype(F32) for g in (*enc_parts, *dec_parts)]
     rate = STEP_UNIT * (PD * TOK_DEV * lax.axis_size("dp") * lax.axis_size("fsdp")) ** 0.5
     weights = (embed, wide_enc, enc_down, wide_dec, dec_down)

time: 587 us -> 518 us (0.88)
  matrix products: 77.1 us -> 30.2 us
  local copies, waits for them, and re-layouts: 89.3 us -> 43.9 us
  Pallas kernels: 308 us -> 352 us
  other arithmetic: 83.3 us -> 64.6 us
    pallas_call x1, Pallas kernels: 14.8 us -> 72.2 us  [decoder_step(): pl.pallas_call(partial(decoder_kernel, owners), out_shape=(jax.ShapeDtype...]
    dot_general x15 -> x5, matrix products: 35.6 us -> 4.66 us  [matmul(): return jnp.dot(left, right, preferred_element_type=jnp.float32)]
    pallas_call x2 -> x1, Pallas kernels: 33 us -> 7.25 us  [attend_back(): pl.pallas_call(partial(attend_back_kernel, size), grid=(groups,), out_sha...]
    unnamed x195 -> x120, local copies, waits for them, and re-layouts: 20.4 us -> 6.29 us
    dot_general x10 -> x5, matrix products: 37.8 us -> 25.5 us  [right_t(): lax.dot_general(left, right, (((1,), (1,)), ((), ())), preferred_element_...]
    concatenate x1 -> x0, local copies, waits for them, and re-layouts: 12 us -> none  [body(): jnp.concatenate([*dec_grads[:3], left_t(decoded, dpred).astype(BF), down_...]
    reshape x4 -> x1, local copies, waits for them, and re-layouts: 11.5 us -> 0.01 us  [body(): dgains_dec.reshape(-1)]
    reduce_sum x6 -> x1, other arithmetic: 8.54 us -> 0.6 us  [decoder_step(): return (grads, dy, vec[:3], vec[3], jnp.sum(vec[4]))]
  transfers between devices with their start and end apart: 3 -> 3, of which waited for: 0 -> 1; matrix products, arithmetic and copies ran while one was open for 24% -> 19% of each run, Pallas kernels for 23% -> 25%
where the time goes in v5:
time: 518 us; the launch traced here: 509 us
  Pallas kernels  352 us (68%)
  other arithmetic  64.6 us (12%)
  local copies, waits for them, and re-layouts  43.9 us (8%)
  matrix products  30.2 us (6%)
  between operations  17 us (3%)
    pallas_call x1, Pallas kernels, sum_products(): pl.pallas_call(partial(sum_kernel, blocks, units, spots), out_shape=tuple...  153 us
    pallas_call x1, Pallas kernels, encoder_forward(): pl.pallas_call(encoder_kernel, out_shape=(*full, *local), in_specs=[vmem]...  119 us
    pallas_call x1, Pallas kernels, decoder_step(): pl.pallas_call(partial(decoder_kernel, owners), out_shape=(jax.ShapeDtype...  72.2 us
    dot_general x5, matrix products, right_t(): lax.dot_general(left, right, (((1,), (1,)), ((), ())), preferred_element_...  25.5 us
    convert_element_type x5, other arithmetic, body(): outs += [buf, new, avg, new.astype(jnp.bfloat16)]  15.6 us
    add x6, other arithmetic, advance(): return (buf, new, AVERAGE * avg + (1.0 - AVERAGE) * new)  12.2 us
  transfers between devices with their start and end apart: 3, of which 1 were waited for; matrix products, arithmetic and copies ran while one was open for 19% of the time, Pallas kernels for 25%

profile of v5, /device:TPU:0, one launch (start us, length us, event | category | flops | bytes accessed | tf_op | source)
XLA Modules:
  0.0 508.5 jit_solution(14281344501701215940)
XLA Ops:
  9.3 2.2 convert_element_type.144
  31.0 4.3 convert_element_type.138.wide_ref
  44.5 2.8 multiply_sine_fusion.1
  50.9 118.8 %shard_map.423 = (bf16[8,128,8704]{2,1,0:T(8,128)(2,1)}, bf16[8,512,1024]{2,1,0:T(8,128)(2,1)}, f32[8,128]{1,0:T(8,128)}, bf16[192,768]{1,0:T(8,128)(2,1)}, f32[...) custom-call(f32[192,768]{1,0:T(8,128)} %slice.175.picked_ref, ...), custom_call_target="tpu_custom_call" | custom-call | flops 5637144576 | bytes 209715200 | tf_op jit(solution)/shard_map/pallas_call | solution.py:1002
  169.8 72.2 %shard_map.424 = (bf16[512,7104]{1,0:T(8,128)(2,1)}, f32[192,512]{1,0:T(8,128)}, f32[8,512]{1,0:T(8,128)}) custom-call(f32[768,512]{1,0:T(8,128)} %pad_maximum_fusion.pos_ref, f32[192,512]{1,0:T(8,128)} %get-tuple-element.53.seen_ref, f32[192,1]{1,0:T(8,128)} %copy.97.kept_ref, f32[576,1]{1,0:T(8,128)} %reshape.309.flag_ref, f32[576,768]{1,0:T(8,128)} %slice.182.picked_ref, ...), custom_call_target="tpu_custom_call" | custom-call | flops 40000000000 | bytes 41943040 | tf_op jit(solution)/shard_map/pallas_call | solution.py:1305
  246.7 2.0 fusion.93
  250.1 4.0 copy.106
  255.0 2.0 copy.103
  257.0 2.0 copy.104
  259.1 2.0 copy.105
  261.1 2.0 copy.107
  263.1 2.0 pad.19
  267.8 1.9 multiply_reduce_fusion.2
  272.0 7.6 %fusion.4.refs_8_ = bf16[192,4096]{1,0:T(8,128)(2,1)S(1)} fusion(f32[192,4096]{1,0:T(8,128)S(1)} %copy-done.23, bf16[192,1024]{1,0:T(8,128)(2,1)S(1)} %add_convert_fusion.1.refs_9_, bf16[4096,1024]{1,0:T(8,128)(2,1)} %bitcast.60), kind=kOutput, calls=%fused_computation.5 | convolution fusion | flops 1612185600 | bytes 13500416 | tf_op jit(solution)/shard_map/dot_general | solution.py:46
  279.7 7.2 %multiply_reduce_fusion.3 = (f32[1024]{0:T(1024)S(1)}, f32[192]{0:T(256)S(1)}, f32[192,1024]{1,0:T(8,128)S(1)}) fusion(f32[192,1024]{1,0:T(8,128)S(1)} %copy-done.15, f32[192]{0:T(256)S(1)} %fusion.74, f32[192]{0:T(256)S(1)} %broadcast_multiply_fusion, f32[1024]{0:T(1024)S(1)} %get-tuple-element.134, bf16[192,4096]{1,0:T(8,128)(2,1)S(1)} %fusion.4.refs_8_, ...), kind=kOutput, calls=%fused_computation.56 | convolution fusion | flops 1611987712 | bytes 11544832 | tf_op jit(solution)/shard_map/dot_general | solution.py:46
  288.8 2.4 fusion.19.do_ref
  291.5 7.2 %shard_map.425 = (bf16[1024,192]{1,0:T(8,128)(2,1)S(1)}, bf16[192,1024]{1,0:T(8,128)(2,1)S(1)}, bf16[192,1024]{1,0:T(8,128)(2,1)S(1)}) custom-call(bf16[1024,192]{1,0:T(8,128)(2,1)S(1)} %copy.100.qt_ref, bf16[192,1024]{1,0:T(8,128)(2,1)S(1)} %get-tuple-element.132.q_ref, bf16[192,1024]{1,0:T(8,128)(2,1)S(1)} %copy.101.k_ref, ...), custom_call_target="tpu_custom_call" | custom-call | flops 754974720 | bytes 147456 | tf_op jit(solution)/shard_map/pallas_call | solution.py:179
  303.0 6.4 %multiply_reduce_fusion.1 = (f32[192]{0:T(256)S(1)}, f32[1024]{0:T(1024)S(1)}, f32[192,1024]{1,0:T(8,128)}) fusion(f32[192,1024]{1,0:T(8,128)} %get-tuple-element.51, f32[1024]{0:T(1024)S(1)} %get-tuple-element.133, f32[192]{0:T(256)S(1)} %broadcast_multiply_fusion.2, f32[192]{0:T(256)S(1)} %copy-done.57, bf16[1024,8704]{1,0:T(8,128)(2,1)} %bitcast.87, ...), kind=kOutput, calls=%fused_computation.54 | convolution fusion | flops 1212873472 | bytes 9054464 | tf_op jit(solution)/shard_map/dot_general | solution.py:46
  315.5 2.2 pad.18.dec_ref
  317.6 153.4 %shard_map.426 = (bf16[96,1024]{1,0:T(8,128)(2,1)}, bf16[128,8704]{1,0:T(8,128)(2,1)}, bf16[512,1024]{1,0:T(8,128)(2,1)}, bf16[64,7168]{1,0:T(8,128)(2,1)}, f32[48,128]{1,0:T(8,128)}) custom-call(f32[48,128]{1,0:T(8,128)} %bitcast.77, bf16[64,7168]{1,0:T(8,128)(2,1)} %pad.18.dec_ref, bf16[4,2,128,192]{3,2,1,0:T(8,128)(2,1)} %bitcast.67, ...), custom_call_target="tpu_custom_call" | custom-call | flops 5435817984 | bytes 314572800 | tf_op jit(solution)/shard_map/pallas_call | solution.py:584
  472.1 2.8 fusion.79
  475.9 8.4 %fusion.83 = (bf16[128,8704]{1,0:T(8,128)(2,1)}, f32[128,8704]{1,0:T(8,128)S(1)}, f32[128,8704]{1,0:T(8,128)}) fusion(f32[128,8704]{1,0:T(8,128)} %param.31, bf16[128,8704]{1,0:T(8,128)(2,1)} %get-tuple-element.73, f32[128,8704]{1,0:T(8,128)} %param.37), kind=kLoop, calls=%fused_computation.202 | loop fusion | flops 11141120 | bytes 22282240 | tf_op jit(solution)/shard_map/convert_element_type | solution.py:1600
  484.3 6.7 %multiply_add_fusion = f32[128,8704]{1,0:T(8,128)} fusion(f32[128,8704]{1,0:T(8,128)S(1)} %get-tuple-element.106, f32[128,8704]{1,0:T(8,128)} %param.43), kind=kLoop, calls=%fused_computation.6 | loop fusion | flops 3342336 | bytes 13369344 | tf_op jit(solution)/shard_map/add | solution.py:1425
  491.1 2.4 fusion.81
  (241 shorter events, 66.5 us)
Async XLA Ops:
  7.2 8.7 %copy-start.8 = (f32[768,768]{1,0:T(8,128)S(1)}, f32[768,768]{1,0:T(8,128)}, u32[]{:S(2)}) copy-start(f32[768,768]{1,0:T(8,128)} %param.24) | copy-start | bytes 7077892
  7.2 162.5 %all-gather.5.cloned.1.call-start = ((), (), s32[]{:S(2)}) async-start(), calls=%async_computation.2 | async-start | bytes 2359296 | tf_op jit(solution)/shard_map/all_gather | solution.py:1482
  9.2 160.6 %all-gather.3.cloned.1.call-start = ((), (), s32[]{:S(2)}) async-start(), calls=%async_computation.1 | async-start | bytes 5898240 | tf_op jit(solution)/shard_map/all_gather | solution.py:1482
  11.5 303.9 %reduce-scatter.2.cloned.1.call-start = ((), (), s32[]{:S(2)}) async-start(), calls=%async_computation.3 | async-start | bytes 8257536 | tf_op jit(solution)/shard_map/reduce_scatter | solution.py:1374
  35.3 6.8 %slice-start.2 = ((f32[768]{0:T(1024)}), f32[192]{0:T(256)S(1)}, s32[]{:S(2)}) async-start(f32[768]{0:T(1024)} %copy-done.55), calls=%async_computation.6 | async-start | bytes 2048 | tf_op jit(solution)/shard_map/slice | solution.py:1512
  245.3 4.6 copy-start.12
  259.1 8.6 %copy-start.45 = (f32[5120]{0:T(1024)S(1)}, f32[5120]{0:T(1024)}, u32[]{:S(2)}) copy-start(f32[5120]{0:T(1024)} %param.35) | copy-start | bytes 61444
  263.1 4.5 copy-start.38
  263.1 4.6 copy-start.17
  270.1 17.1 %copy-start.6 = (f32[192,1024]{1,0:T(8,128)}, f32[192,1024]{1,0:T(8,128)S(1)}, u32[]{:S(2)}) copy-start(f32[192,1024]{1,0:T(8,128)S(1)} %get-tuple-element.116) | copy-start | bytes 2359300
  270.2 9.4 %copy-start.28 = (bf16[192,1024]{1,0:T(8,128)(2,1)}, bf16[192,1024]{1,0:T(8,128)(2,1)S(1)}, u32[]{:S(2)}) copy-start(bf16[192,1024]{1,0:T(8,128)(2,1)S(1)} %add_convert_fusion.1.refs_9_) | copy-start | bytes 1179652
  272.0 7.6 %copy-start.15 = (f32[192,1024]{1,0:T(8,128)S(1)}, f32[192,1024]{1,0:T(8,128)}, u32[]{:S(2)}) copy-start(f32[192,1024]{1,0:T(8,128)} %get-tuple-element.60) | copy-start | bytes 2359300
  279.6 7.2 %copy-start.29 = (bf16[192,4096]{1,0:T(8,128)(2,1)}, bf16[192,4096]{1,0:T(8,128)(2,1)S(1)}, u32[]{:S(2)}) copy-start(bf16[192,4096]{1,0:T(8,128)(2,1)S(1)} %fusion.4.refs_8_) | copy-start | bytes 4718596
  291.5 10.8 %copy-start.54 = (f32[8,512]{1,0:T(8,128)S(1)}, f32[8,512]{1,0:T(8,128)}, u32[]{:S(2)}) copy-start(f32[8,512]{1,0:T(8,128)} %get-tuple-element.64) | copy-start | bytes 49156
  291.5 11.5 %copy-start.57 = (f32[192]{0:T(256)S(1)}, f32[192]{0:T(256)}, u32[]{:S(2)}) copy-start(f32[192]{0:T(256)} %fusion.72) | copy-start | bytes 2308
  303.0 7.8 %copy-start.53 = (f32[192]{0:T(256)S(1)}, f32[192]{0:T(256)}, u32[]{:S(2)}) copy-start(f32[192]{0:T(256)} %copy-done.52) | copy-start | bytes 2308
  303.0 7.9 %copy-start.13 = (f32[192,1024]{1,0:T(8,128)S(1)}, f32[192,1024]{1,0:T(8,128)}, u32[]{:S(2)}) copy-start(f32[192,1024]{1,0:T(8,128)} %get-tuple-element.51) | copy-start | bytes 2359300
  317.6 154.4 %copy-start.20 = (f32[64,5056]{1,0:T(8,128)S(1)}, f32[64,5056]{1,0:T(8,128)}, u32[]{:S(2)}) copy-start(f32[64,5056]{1,0:T(8,128)} %param.33) | copy-start | bytes 3883012
  317.6 154.4 %copy-start.33 = (f32[64,5056]{1,0:T(8,128)S(1)}, f32[64,5056]{1,0:T(8,128)}, u32[]{:S(2)}) copy-start(f32[64,5056]{1,0:T(8,128)} %param.39) | copy-start | bytes 3883012
  474.8 20.7 %copy-start.21 = (f32[64,5056]{1,0:T(8,128)}, f32[64,5056]{1,0:T(8,128)S(1)}, u32[]{:S(2)}) copy-start(f32[64,5056]{1,0:T(8,128)S(1)} %get-tuple-element.100) | copy-start | bytes 3883012
  484.3 6.8 %copy-start.5 = (f32[128,8704]{1,0:T(8,128)}, f32[128,8704]{1,0:T(8,128)S(1)}, u32[]{:S(2)}) copy-start(f32[128,8704]{1,0:T(8,128)S(1)} %get-tuple-element.106) | copy-start | bytes 13369348
  484.3 6.8 %copy-start.11 = (f32[512,1024]{1,0:T(8,128)S(1)}, f32[512,1024]{1,0:T(8,128)}, u32[]{:S(2)}) copy-start(f32[512,1024]{1,0:T(8,128)} %param.32) | copy-start | bytes 6291460
  484.3 6.8 %copy-start.24 = (f32[512,1024]{1,0:T(8,128)S(1)}, f32[512,1024]{1,0:T(8,128)}, u32[]{:S(2)}) copy-start(f32[512,1024]{1,0:T(8,128)} %param.38) | copy-start | bytes 6291460
  484.3 6.8 %copy-start.35 = (bf16[512,1024]{1,0:T(8,128)(2,1)S(1)}, bf16[512,1024]{1,0:T(8,128)(2,1)}, u32[]{:S(2)}) copy-start(bf16[512,1024]{1,0:T(8,128)(2,1)} %get-tuple-element.74) | copy-start | bytes 3145732
  (42 other events, 95.8 us)
Sparse Core Ops, SparseCore 0:
  10.5 30.6 all-gather.4
  43.6 57.7 all-gather.2
  242.2 73.2 reduce-scatter.1

commit v6 on v5

--- a/solution.py
+++ b/solution.py
@@ -224,17 +224,38 @@
     )
 
 
-def sum_kernel(blocks, units, spots, vec_ref, dec_ref, *refs):
+def back_kernel(
+    dec_units,
+    blocks,
+    units,
+    spots,
+    dy_ref,
+    kept_ref,
+    vec_ref,
+    gains_ref,
+    bias_ref,
+    qkv_ref,
+    dec_ref,
+    end_ref,
+    middle_ref,
+    start_ref,
+    slope_ref,
+    wide_ref,
+    down_ref,
+    *refs,
+):
     n_left = max(b[0] for b in blocks) + 1
-    n_right = max(u[1] for u in units) + 1
-    lefts, rights = refs[:n_left], refs[n_left : n_left + n_right]
-    outs = refs[n_left + n_right : n_left + n_right + 3]
-    dec_out, vec_out = refs[n_left + n_right + 3 : n_left + n_right + 5]
+    lefts, refs = refs[:n_left], refs[n_left:]
+    outs, refs = refs[:5], refs[5:]
+    vec_out, refs = refs[0], refs[1:]
     (
         xo,
         xp,
         yo,
         yp,
+        do,
+        dp,
+        products,
         a_out,
         a_in,
         b_out,
@@ -245,6 +266,21 @@
         z_two,
         v_in,
         v_out,
+        wide_buf,
+        down_buf,
+        slope_buf,
+        h_buf,
+        dend_ref,
+        dmid_ref,
+        dbranch_ref,
+        dmixed_ref,
+        dqkv_ref,
+        grad_vec,
+        wide_sem,
+        down_sem,
+        slope_sem,
+        h_sem,
+        dec_sem,
         left_sem,
         right_sem,
         a_send,
@@ -256,9 +292,8 @@
         v_send,
         v_recv,
         store_sem,
-    ) = refs[n_left + n_right + 5 :]
-    count = len(units)
-    extra = z_one.shape[0] - count
+    ) = refs
+    count = dec_units + len(units)
     z, f = lax.axis_index("dp"), lax.axis_index("fsdp")
     core, place = f % 2, f // 2
     x, y = place % 2, place // 2
@@ -273,6 +308,41 @@
     across = (3 - z, f)
     outward = (jnp.where(low, 0, 3), f)
 
+    ring = wide_buf.shape[0]
+    up_chunks, out_chunks, qkv_chunks = FF // UNIT, D // UNIT, 3 * D // UNIT
+    chunks = 1 + up_chunks + out_chunks + qkv_chunks
+
+    def wide_copy(w):
+        inside = jnp.where(w < 1 + up_chunks, 4 * D + UNIT * (w - 1), 3 * D + UNIT * (w - 1 - up_chunks))
+        column = jnp.where(
+            w == 0,
+            4 * D + FF,
+            jnp.where(w < 1 + up_chunks + out_chunks, inside, UNIT * (w - 1 - up_chunks - out_chunks)),
+        )
+        return pltpu.make_async_copy(
+            wide_ref.at[:, pl.ds(pl.multiple_of(column, UNIT), UNIT)],
+            wide_buf.at[w % ring],
+            wide_sem.at[w % ring],
+        )
+
+    def down_copy(j):
+        rows = pl.ds(pl.multiple_of(j * UNIT, UNIT), UNIT)
+        return pltpu.make_async_copy(down_ref.at[rows], down_buf.at[j % 2], down_sem.at[j % 2])
+
+    def slope_copy(j):
+        columns = pl.ds(pl.multiple_of(j * UNIT, UNIT), UNIT)
+        return pltpu.make_async_copy(slope_ref.at[:, columns], slope_buf.at[j % 2], slope_sem.at[j % 2])
+
+    def h_copy(source):
+        return pltpu.make_async_copy(source, h_buf, h_sem.at[0])
+
+    h_copy(end_ref).start()
+    for n in range(ring):
+        wide_copy(n).start()
+    for n in range(2):
+        down_copy(n).start()
+        slope_copy(n).start()
+
     barrier = pltpu.get_barrier_semaphore()
     for device in (partner, x_side, y_side):
         pl.semaphore_signal(barrier, inc=1, device_id=device, device_id_type=MESH)
@@ -288,34 +358,50 @@
         pl.semaphore_signal(barrier, inc=1, device_id=outward, device_id_type=MESH)
         pl.semaphore_wait(barrier, 5)
 
+    def swap_dec(source, n):
+        return put(source, dp.at[n], dec_sem.at[n, 1], dec_sem.at[n, 2], partner)
+
     def swap_left(source, b):
         return put(source, xp.at[b], left_sem.at[b, 1], left_sem.at[b, 2], partner)
 
-    def swap_right(source, u):
-        return put(source, yp.at[u], right_sem.at[u, 1], right_sem.at[u, 2], partner)
-
-    for number, (block, right, column) in enumerate(units):
-        if number == 0 or block != units[number - 1][0]:
-            left, sub = blocks[block]
-            rows = pl.ds(sub * ROWS, ROWS)
-            swap_left(lefts[left].at[:, 1 - core, rows], block).start()
-            pltpu.make_async_copy(
-                lefts[left].at[:, core, rows], xo.at[block], left_sem.at[block, 0]
-            ).start()
-        piece = rights[right].at[:, pl.ds(column, UNIT)]
-        swap_right(piece, number).start()
-        pltpu.make_async_copy(piece, yo.at[number], right_sem.at[number, 0]).start()
-
-    starts = [n for n in range(1, count) if units[n][0] != units[n - 1][0]]
-
-    def block_of(u):
-        return sum([jnp.where(u >= n, 1, 0) for n in starts], jnp.int32(0))
+    def swap_right(r):
+        return put(yo.at[r], yp.at[r], right_sem.at[r, 0], right_sem.at[r, 1], partner)
+
+    for n in range(dec_units):
+        swap_dec(dec_ref.at[:, 1 - core, n], n).start()
+        pltpu.make_async_copy(dec_ref.at[:, core, n], do.at[n], dec_sem.at[n, 0]).start()
+    for b, (left, sub) in enumerate(blocks):
+        rows = pl.ds(sub * ROWS, ROWS)
+        swap_left(lefts[left].at[:, 1 - core, rows], b).start()
+        pltpu.make_async_copy(lefts[left].at[:, core, rows], xo.at[b], left_sem.at[b, 0]).start()
+
+    firsts = 1 + out_chunks
+    single = next(n for n in range(1, len(units)) if units[n][1] >= firsts)
+    starts = [n for n in range(1, len(units)) if units[n][0] != units[n - 1][0]]
+
+    def block_of(e):
+        return sum([jnp.where(e >= n, 1, 0) for n in starts], jnp.int32(0))
+
+    def right_of(e):
+        early = jnp.where(e == 0, 0, 1 + (e + out_chunks - 1) % out_chunks)
+        return jnp.where(e < single, early, e - single + firsts)
 
     first, second = pl.ds(0, HALF), pl.ds(HALF, HALF)
 
-    def part(u, owner, columns):
-        b = block_of(u)
-        return matmul(xo[b, owner], yo[u, :, columns]) + matmul(xp[b, owner], yp[u, :, columns])
+    def part(u, owner, columns, k):
+        @pl.when(u < dec_units)
+        def _():
+            n = jnp.minimum(u, dec_units - 1)
+            products[k] = do[n, owner, :, columns].astype(F32) + dp[n, owner, :, columns].astype(F32)
+
+        @pl.when(u >= dec_units)
+        def _():
+            e = jnp.maximum(u - dec_units, 0)
+            b, r = block_of(e), right_of(e)
+            total = matmul(xo[b, owner], yo[r, :, columns])
+            products[k] = total + matmul(xp[b, owner], yp[r, :, columns])
+
+        return products[k]
 
     def copy_a(u, side):
         slot = u % a_out.shape[0]
@@ -337,11 +423,13 @@
             (y_side, x_side)[side],
         )
 
+    z_slots = z_out.shape[0]
+
     def copy_in(u):
-        return put(z_out.at[u], z_one.at[u], z_send.at[u, 0], z_recv.at[u, 0], inward)
+        return put(z_out.at[u % z_slots], z_one.at[u], z_send.at[u, 0], z_recv.at[u, 0], inward)
 
     def copy_across(u):
-        return put(z_out.at[u], z_two.at[u], z_send.at[u, 0], z_recv.at[u, 1], across)
+        return put(z_out.at[u % z_slots], z_two.at[u], z_send.at[u, 0], z_recv.at[u, 1], across)
 
     def copy_out(u):
         return put(z_one.at[u], z_one.at[u], z_send.at[u, 1], z_recv.at[u, 0], outward)
@@ -349,28 +437,126 @@
     def copy_v(step, device):
         return put(v_out.at[step], v_in.at[step], v_send.at[step], v_recv.at[step], device)
 
-    def ready(n):
-        halves = [
-            dec_ref[:, pl.ds(pl.multiple_of((2 * n + part) * UNIT, UNIT), UNIT)] for part in range(2)
-        ]
-        return jnp.concatenate(halves, 0).astype(F32)
-
-    def send_in(u, value):
-        z_out[u] = value.astype(BF)
-        copy_in(u).start()
-
-    def add_in(u, value):
-        copy_in(u).wait_recv()
-        z_out[u] = (value + z_one[u].astype(F32)).astype(BF)
-        copy_across(u).start()
-
-    def add_across(u):
-        copy_across(u).wait_recv()
-        z_one[u] = (z_out[u].astype(F32) + z_two[u].astype(F32)).astype(BF)
-        copy_out(u).start()
-
-    def take(u):
-        copy_out(u).wait_recv()
+    gain_one, gain_two, gain_out = [gains_ref[n : n + 1, :] for n in range(3)]
+
+    def give(r, value):
+        yo[r] = value
+        swap_right(r).start()
+
+    def columns_at(n):
+        return slice(n * UNIT, (n + 1) * UNIT)
+
+    def back_link():
+        dseen = jnp.where(kept_ref[...] > 0, dy_ref[...], 0.0).astype(BF)
+        give(0, dseen)
+        wide_copy(0).wait()
+        h_copy(end_ref).wait()
+        unit, rate = normalize(h_buf[...])
+        dend, dgain = normalize_back(unit, rate, gain_out, right_t(dseen, wide_buf[0]))
+        grad_vec[...] = vec_ref[...]
+        grad_vec[2:3, :] = dgain
+        dend_ref[...] = dend
+        dbranch_ref[...] = dend.astype(BF)
+        for n in range(out_chunks):
+            give(1 + n, dbranch_ref[:, columns_at(n)])
+        wide_copy(ring).start()
+        h_copy(middle_ref).start()
+        dmid_ref[...] = jnp.zeros_like(dmid_ref)
+
+    def back_hidden(j):
+        w = 1 + j
+        down_copy(j).wait()
+        slope_copy(j).wait()
+        wide_copy(w).wait()
+        dhidden = right_t(dbranch_ref[...], down_buf[j % 2])
+        dbefore = (dhidden * slope_buf[j % 2]).astype(BF)
+        give(firsts + j, dbefore)
+        dmid_ref[...] += right_t(dbefore, wide_buf[w % ring])
+        wide_copy(w + ring).start()
+
+        @pl.when(j + 2 < up_chunks)
+        def _():
+            down_copy(j + 2).start()
+            slope_copy(j + 2).start()
+
+    def back_out():
+        h_copy(middle_ref).wait()
+        unit, rate = normalize(h_buf[...])
+        dmiddle, dgain = normalize_back(unit, rate, gain_two, dmid_ref[...])
+        grad_vec[1:2, :] = dgain
+        dmiddle = dmiddle + dend_ref[...]
+        dend_ref[...] = dmiddle
+        dattn = dmiddle.astype(BF)
+        dmixed = jnp.zeros((VIS, D), F32)
+        for n in range(out_chunks):
+            w = 1 + up_chunks + n
+            piece = dattn[:, columns_at(n)]
+            give(firsts + up_chunks + n, piece)
+            wide_copy(w).wait()
+            dmixed = dmixed + right_t(piece, wide_buf[w % ring])
+            wide_copy(w + ring).start()
+        dmixed_ref[...] = dmixed.astype(BF)
+        h_copy(start_ref).start()
+        dmid_ref[...] = jnp.zeros_like(dmid_ref)
+
+    size = D // HEADS
+    lane_head = lax.broadcasted_iota(jnp.int32, (VIS, LANES), 1) // size
+
+    def only(array, j):
+        return jnp.where(lane_head == j, array.astype(F32), 0.0).astype(BF)
+
+    def back_attention(g):
+        at = [pl.ds(pl.multiple_of(n * D + g * LANES, LANES), LANES) for n in range(3)]
+        query, keys, values = [qkv_ref[:, lanes] for lanes in at]
+        dout = dmixed_ref[:, at[0]]
+        keys_t = keys.T
+        factor = size ** (-0.5)
+        dkeys, dvalues = jnp.zeros((VIS, LANES), F32), jnp.zeros((VIS, LANES), F32)
+        dquery = []
+        for j in range(LANES // size):
+            scores = right_t(keys, only(query, j)) * factor + bias_ref[...]
+            probs = jnp.exp(scores - jnp.max(scores, 0, keepdims=True))
+            probs = probs * (1.0 / jnp.sum(probs, 0, keepdims=True))
+            dvalues = jnp.where(lane_head == j, matmul(probs.astype(BF), dout), dvalues)
+            dprobs = right_t(values, only(dout, j))
+            delta = jnp.sum(dprobs * probs, 0, keepdims=True)
+            dscores = (probs * (dprobs - delta)).astype(BF)
+            dkeys = jnp.where(lane_head == j, matmul(dscores, query), dkeys)
+            dquery.append(matmul(keys_t[j * size : (j + 1) * size, :], dscores))
+        dqkv_ref[:, at[0]] = (jnp.concatenate(dquery, 0) * factor).astype(BF).T
+        dqkv_ref[:, at[1]] = (dkeys * factor).astype(BF)
+        dqkv_ref[:, at[2]] = dvalues.astype(BF)
+
+    def give_qkv():
+        for c in range(qkv_chunks):
+            give(firsts + up_chunks + out_chunks + c, dqkv_ref[:, columns_at(c)])
+
+    def back_qkv(c):
+        w = 1 + up_chunks + out_chunks + c
+        wide_copy(w).wait()
+        piece = dqkv_ref[:, pl.ds(pl.multiple_of(c * UNIT, UNIT), UNIT)]
+        dmid_ref[...] += right_t(piece, wide_buf[w % ring])
+
+        @pl.when(w + ring < chunks)
+        def _():
+            wide_copy(w + ring).start()
+
+    def back_start():
+        h_copy(start_ref).wait()
+        unit, rate = normalize(h_buf[...])
+        dh, dgain = normalize_back(unit, rate, gain_one, dmid_ref[...])
+        grad_vec[0:1, :] = dgain
+        dh = (dh + dend_ref[...]).astype(BF)
+        for n in range(out_chunks):
+            give(firsts + up_chunks + out_chunks + qkv_chunks + n, dh[:, columns_at(n)])
+
+    at_hidden = 1
+    at_out = at_hidden + up_chunks
+    at_attention = at_out + 1
+    groups = D // LANES
+    at_qkv = at_attention + groups
+    at_start = at_qkv + qkv_chunks
+    at_vec = at_start + 1
 
     def step(i, _):
         def stage(lag, also=None):
@@ -385,15 +571,23 @@
         @when
         def _():
             u = u0
-            b = block_of(u)
-
-            @pl.when((u == 0) | (b != block_of(u - 1)))
+
+            @pl.when(u < dec_units)
             def _():
-                pltpu.make_async_copy(xo.at[b], xo.at[b], left_sem.at[b, 0]).wait()
-                swap_left(xo.at[b], b).wait()
-
-            pltpu.make_async_copy(yo.at[u], yo.at[u], right_sem.at[u, 0]).wait()
-            swap_right(yo.at[u], u).wait()
+                pltpu.make_async_copy(do.at[u], do.at[u], dec_sem.at[u, 0]).wait()
+                swap_dec(do.at[u], u).wait()
+
+            @pl.when(u == dec_units)
+            def _():
+                for b in range(len(blocks)):
+                    pltpu.make_async_copy(xo.at[b], xo.at[b], left_sem.at[b, 0]).wait()
+                    swap_left(xo.at[b], b).wait()
+                for r in range(firsts):
+                    swap_right(r).wait()
+
+            @pl.when(u >= dec_units + single)
+            def _():
+                swap_right(u - dec_units - single + firsts).wait()
 
             @pl.when(u >= a_out.shape[0])
             def _():
@@ -401,11 +595,11 @@
                     copy_a(u - a_out.shape[0], side).wait_send()
 
             slot = u % a_out.shape[0]
-            a_out[slot, 0, 0] = part(u, at_x, first).astype(BF)
-            a_out[slot, 0, 1] = part(u, at_far, first).astype(BF)
+            a_out[slot, 0, 0] = part(u, at_x, first, 0).astype(BF)
+            a_out[slot, 0, 1] = part(u, at_far, first, 1).astype(BF)
             copy_a(u, 0).start()
-            a_out[slot, 1, 0] = part(u, at_y, second).astype(BF)
-            a_out[slot, 1, 1] = part(u, at_far, second).astype(BF)
+            a_out[slot, 1, 0] = part(u, at_y, second, 2).astype(BF)
+            a_out[slot, 1, 1] = part(u, at_far, second, 3).astype(BF)
             copy_a(u, 1).start()
 
         u1, when = stage(LAGS[0])
@@ -421,10 +615,10 @@
                     copy_b(u - b_out.shape[0], side).wait_send()
 
             copy_a(u, 0).wait_recv()
-            b_out[slot, 0] = (part(u, at_y, first) + a_in[u, 0, 1].astype(F32)).astype(BF)
+            b_out[slot, 0] = (part(u, at_y, first, 0) + a_in[u, 0, 1].astype(F32)).astype(BF)
             copy_b(u, 0).start()
             copy_a(u, 1).wait_recv()
-            b_out[slot, 1] = (part(u, at_x, second) + a_in[u, 1, 1].astype(F32)).astype(BF)
+            b_out[slot, 1] = (part(u, at_x, second, 1) + a_in[u, 1, 1].astype(F32)).astype(BF)
             copy_b(u, 1).start()
 
         u2, when = stage(LAGS[1])
@@ -435,61 +629,79 @@
             copy_b(u, 0).wait_recv()
             copy_b(u, 1).wait_recv()
             for side, columns in enumerate((first, second)):
-                total = part(u, place, columns) + a_in[u, side, 0].astype(F32)
+                total = part(u, place, columns, side) + a_in[u, side, 0].astype(F32)
                 sums[u % 4, :, columns] = total + b_in[u, side].astype(F32)
 
             @pl.when(outer)
             def _():
-                send_in(u + extra, sums[u % 4])
+                @pl.when(u >= z_slots)
+                def _():
+                    copy_in(u - z_slots).wait_send()
+
+                z_out[u % z_slots] = sums[u % 4].astype(BF)
+                copy_in(u).start()
 
         u3, when = stage(LAGS[2], inner)
 
         @when
         def _():
-            add_in(u3 + extra, sums[u3 % 4])
+            u = u3
+            copy_in(u).wait_recv()
+
+            @pl.when(u >= z_slots)
+            def _():
+                copy_across(u - z_slots).wait_send()
+
+            z_out[u % z_slots] = (sums[u % 4] + z_one[u].astype(F32)).astype(BF)
+            copy_across(u).start()
 
         u4, when = stage(LAGS[3], inner)
 
         @when
         def _():
-            add_across(u4 + extra)
+            u = u4
+            copy_across(u).wait_recv()
+            z_one[u] = (z_out[u % z_slots].astype(F32) + z_two[u].astype(F32)).astype(BF)
+            copy_out(u).start()
 
         u5, when = stage(LAGS[4], outer)
 
         @when
         def _():
-            take(u5 + extra)
-
-        @pl.when((i < extra) & outer)
+            copy_out(u5).wait_recv()
+
+        pl.when(i == 0)(back_link)
+
+        @pl.when((i >= at_hidden) & (i < at_hidden + up_chunks))
         def _():
-            send_in(i, ready(i))
-
-        one, two, three = [lag - LAGS[1] for lag in LAGS[2:]]
-
-        @pl.when((i >= one) & (i < extra + one) & inner)
+            back_hidden(i - at_hidden)
+
+        pl.when(i == at_out)(back_out)
+
+        @pl.when((i >= at_attention) & (i < at_attention + groups))
         def _():
-            add_in(i - one, ready(i - one))
-
-        @pl.when((i >= two) & (i < extra + two) & inner)
+            back_attention(i - at_attention)
+
+        pl.when(i == at_qkv)(give_qkv)
+
+        @pl.when((i >= at_qkv) & (i < at_qkv + qkv_chunks))
         def _():
-            add_across(i - two)
-
-        @pl.when((i >= three) & (i < extra + three) & outer)
-        def _():
-            take(i - three)
+            back_qkv(i - at_qkv)
+
+        pl.when(i == at_start)(back_start)
 
         for number, device in enumerate((partner, x_side, y_side)):
 
-            @pl.when(i == number)
+            @pl.when(i == at_vec + number)
             def _():
                 if number == 0:
-                    v_out[0] = vec_ref[...]
+                    v_out[0] = grad_vec[...]
                 else:
                     copy_v(number - 1, (partner, x_side, y_side)[number - 1]).wait_recv()
                     v_out[number] = v_out[number - 1] + v_in[number - 1]
                 copy_v(number, device).start()
 
-        @pl.when(i == 3)
+        @pl.when(i == at_vec + 3)
         def _():
             copy_v(2, y_side).wait_recv()
             v_out[3] = v_out[2] + v_in[2]
@@ -498,20 +710,20 @@
             def _():
                 copy_v(3, inward).start()
 
-        @pl.when((i == 4) & inner)
+        @pl.when((i == at_vec + 4) & inner)
         def _():
             copy_v(3, inward).wait_recv()
             v_out[4] = v_out[3] + v_in[3]
             copy_v(4, across).start()
 
-        @pl.when((i == 5) & inner)
+        @pl.when((i == at_vec + 5) & inner)
         def _():
             copy_v(4, across).wait_recv()
             v_out[5] = v_out[4] + v_in[4]
             copy_v(5, outward).start()
             vec_out[...] = v_out[5]
 
-        @pl.when((i == 7) & outer)
+        @pl.when((i == at_vec + 7) & outer)
         def _():
             copy_v(5, outward).wait_recv()
             vec_out[...] = v_in[5]
@@ -521,20 +733,12 @@
     lax.fori_loop(0, count + LAGS[4], step, 0)
 
     stores = []
-    for number, (out, row, rows, column, columns) in enumerate(spots):
+    for n, (u, start, out, row, rows, column) in enumerate(spots):
         stores.append(
             pltpu.make_async_copy(
-                z_one.at[extra + number, pl.ds(0, rows), pl.ds(0, columns)],
-                outs[out].at[pl.ds(row, rows), pl.ds(column, columns)],
-                store_sem.at[number],
-            )
-        )
-    for number in range(2 * extra):
-        stores.append(
-            pltpu.make_async_copy(
-                z_one.at[number // 2, pl.ds(number % 2 * HALF_ROWS, HALF_ROWS)],
-                dec_out.at[:, pl.ds(number * UNIT, UNIT)],
-                store_sem.at[count + number],
+                z_one.at[u, pl.ds(start, rows)],
+                outs[out].at[pl.ds(row, rows), pl.ds(column, UNIT)],
+                store_sem.at[n],
             )
         )
     for store in stores:
@@ -547,84 +751,123 @@
             copy_b(u, side).wait_send()
     for number, device in enumerate((partner, x_side, y_side)):
         copy_v(number, device).wait_send()
-
     for store in stores:
         store.wait()
 
     @pl.when(outer)
     def _():
         copy_v(3, inward).wait_send()
-
-        def drain(u, _):
+        for u in range(count - z_slots, count):
             copy_in(u).wait_send()
-            return 0
-
-        lax.fori_loop(0, count + extra, drain, 0)
 
     @pl.when(inner)
     def _():
         copy_v(4, across).wait_send()
         copy_v(5, outward).wait_send()
+        for u in range(count - z_slots, count):
+            copy_across(u).wait_send()
 
         def drain(u, _):
-            copy_across(u).wait_send()
             copy_out(u).wait_send()
             return 0
 
-        lax.fori_loop(0, count + extra, drain, 0)
-
-
-def sum_products(blocks, units, spots, shapes, lefts, rights, dec, vec):
-    count, depth = len(units), rights[0].shape[0]
-    extra = dec.shape[1] // (2 * UNIT)
-    full = count + extra
-    lefts = [a.reshape(4, 2, a.shape[0] // 8, depth) for a in lefts]
+        lax.fori_loop(0, count, drain, 0)
+
+
+def encoder_back(dy, kept, vec, gains, bias, qkv, dec, states, wide, down, lefts):
+    owners = lax.axis_size("fsdp")
+    own = PD // owners
+    dec_units = dec.shape[1] * dec.shape[2] // ROWS
+    dec = dec.reshape(4, 2, dec_units, ROWS, UNIT)
+    half = ROWS // 2
+    blocks, units, spots = [], [], []
+    for n in range(2 * dec_units):
+        place = (4, n * half, half, 0) if n < DFF // DD else (3, 0, half, (n - DFF // DD) * UNIT)
+        spots.append((n // 2, n % 2 * half, *place))
+
+    def add(left, sub, right, out, row, rows, column, columns):
+        blocks.append((left, sub))
+        for n in range(columns // UNIT):
+            spots.append((dec_units + len(units), 0, out, row, rows, column + n * UNIT))
+            units.append((len(blocks) - 1, right + n))
+
+    subs = FF // owners // ROWS
+    add(0, 0, 0, 1, 0, ROWS, 4 * D + FF, DD)
+    for n in range(subs):
+        add(1, n, 1, 2, n * ROWS, ROWS, 0, D)
+    right = 1 + D // UNIT
+    add(2, 0, right, 1, 0, ROWS, 4 * D, FF)
+    right += FF // UNIT
+    add(3, 0, right, 1, 0, ROWS, 3 * D, D)
+    right += D // UNIT
+    add(4, 0, right, 1, 0, ROWS, 0, 3 * D)
+    right += 3 * D // UNIT
+    add(5, 0, right, 0, 0, own, 0, D)
+    right += D // UNIT
+    count = dec_units + len(units)
+    shapes = ((own, D), (ROWS, 4 * D + FF + DD), (FF // owners, D), (half, 10 * UNIT), (DFF // owners, DD))
+    lefts = [a.reshape(4, 2, -1, VIS) for a in lefts]
     slots = 3
     dma = pltpu.SemaphoreType.DMA
+    vmem, anywhere = pl.BlockSpec(memory_space=pltpu.VMEM), pl.BlockSpec(memory_space=pl.ANY)
     return pl.pallas_call(
-        partial(sum_kernel, blocks, units, spots),
-        out_shape=tuple(jax.ShapeDtypeStruct(shape, BF) for shape in (*shapes, dec.shape))
+        partial(back_kernel, dec_units, tuple(blocks), tuple(units), tuple(spots)),
+        out_shape=tuple(jax.ShapeDtypeStruct(shape, BF) for shape in shapes)
         + (jax.ShapeDtypeStruct(vec.shape, F32),),
-        in_specs=[pl.BlockSpec(memory_space=pltpu.VMEM)] * 2
-        + [pl.BlockSpec(memory_space=pl.ANY)] * (len(lefts) + len(rights)),
-        out_specs=(pl.BlockSpec(memory_space=pl.ANY),) * (len(shapes) + 1)
-        + (pl.BlockSpec(memory_space=pltpu.VMEM),),
+        in_specs=[vmem] * 6 + [anywhere] * (7 + len(lefts)),
+        out_specs=(anywhere,) * len(shapes) + (vmem,),
         scratch_shapes=[
-            pltpu.VMEM((len(blocks), 4, ROWS, depth), BF),
-            pltpu.VMEM((len(blocks), 4, ROWS, depth), BF),
-            pltpu.VMEM((count, depth, UNIT), BF),
-            pltpu.VMEM((count, depth, UNIT), BF),
+            pltpu.VMEM((len(blocks), 4, ROWS, VIS), BF),
+            pltpu.VMEM((len(blocks), 4, ROWS, VIS), BF),
+            pltpu.VMEM((right, VIS, UNIT), BF),
+            pltpu.VMEM((right, VIS, UNIT), BF),
+            pltpu.VMEM((dec_units, 4, ROWS, UNIT), BF),
+            pltpu.VMEM((dec_units, 4, ROWS, UNIT), BF),
+            pltpu.VMEM((4, ROWS, HALF), F32),
             pltpu.VMEM((slots, 2, 2, ROWS, HALF), BF),
             pltpu.VMEM((count, 2, 2, ROWS, HALF), BF),
             pltpu.VMEM((slots, 2, ROWS, HALF), BF),
             pltpu.VMEM((count, 2, ROWS, HALF), BF),
             pltpu.VMEM((4, ROWS, UNIT), F32),
-            pltpu.VMEM((full, ROWS, UNIT), BF),
-            pltpu.VMEM((full, ROWS, UNIT), BF),
-            pltpu.VMEM((full, ROWS, UNIT), BF),
+            pltpu.VMEM((6, ROWS, UNIT), BF),
+            pltpu.VMEM((count, ROWS, UNIT), BF),
+            pltpu.VMEM((count, ROWS, UNIT), BF),
             pltpu.VMEM((6, *vec.shape), F32),
             pltpu.VMEM((6, *vec.shape), F32),
+            pltpu.VMEM((3, D, UNIT), BF),
+            pltpu.VMEM((2, UNIT, D), BF),
+            pltpu.VMEM((2, VIS, UNIT), F32),
+            pltpu.VMEM((VIS, D), F32),
+            pltpu.VMEM((VIS, D), F32),
+            pltpu.VMEM((VIS, D), F32),
+            pltpu.VMEM((VIS, D), BF),
+            pltpu.VMEM((VIS, D), BF),
+            pltpu.VMEM((VIS, 3 * D), BF),
+            pltpu.VMEM(vec.shape, F32),
+            dma((3,)),
+            dma((2,)),
+            dma((2,)),
+            dma((1,)),
+            dma((dec_units, 3)),
             dma((len(blocks), 3)),
-            dma((count, 3)),
+            dma((right, 2)),
             dma((slots, 2)),
             dma((count, 2)),
             dma((slots, 2)),
             dma((count, 2)),
-            dma((full, 2)),
-            dma((full, 2)),
+            dma((count, 2)),
+            dma((count, 2)),
             dma((6,)),
             dma((6,)),
-            dma((count + 2 * extra,)),
+            dma((count + dec_units,)),
         ],
         compiler_params=pltpu.CompilerParams(
-            collective_id=0, has_side_effects=True, vmem_limit_bytes=58 * 2**20
+            collective_id=0, has_side_effects=True, vmem_limit_bytes=61 * 2**20
         ),
         cost_estimate=pl.CostEstimate(
-            flops=8 * 2 * count * ROWS * UNIT * depth,
-            bytes_accessed=300 * 2**20,
-            transcendentals=0,
+            flops=30 * 10**9, bytes_accessed=300 * 2**20, transcendentals=0
         ),
-    )(vec, dec, *lefts, *rights)
+    )(dy, kept, vec, gains, bias, qkv, dec, *states, wide, down, *lefts)
 
 
 def encoder_pieces(shapes):
@@ -657,18 +900,24 @@
     wide_out,
     down_out,
     stats_out,
+    inputs_t,
+    a_t,
+    mixed_t,
+    b_t,
+    hidden_t,
+    z_t,
+    start_ref,
+    qkv_ref,
+    middle_ref,
+    slope_ref,
+    end_ref,
+    seen_ref,
     inputs_ref,
-    start_ref,
     a_ref,
-    qkv_ref,
     mixed_ref,
-    middle_ref,
     b_ref,
-    slope_ref,
     hidden_ref,
-    end_ref,
     z_ref,
-    seen_ref,
     w_embed,
     w_wide,
     w_down,
@@ -859,6 +1108,10 @@
                 copy_v(5, z_side).wait_recv()
                 stats_out[...] = v_in[5]
 
+    def turn(source, target, start=0, width=D):
+        for lane in range(start, start + width, LANES):
+            target[lane : lane + LANES, :] = source[:, lane : lane + LANES].T
+
     def columns_of(t):
         array, row, rows, column, columns, _ = pieces[t]
         weight = gathered[array][:, row : row + rows, column : column + columns]
@@ -875,6 +1128,14 @@
                 inputs_ref[:, lanes] = ((picked_ref[:, lanes] - mean) * rate).astype(BF)
         start_ref[...] = matmul(inputs_ref[...], columns_of(0)) + pos_ref[...]
         a_ref[...] = norm_rows(start_ref[...], gains_ref[0:1, :])
+        own = w_embed.shape[1]
+        flipped = jnp.concatenate(
+            [inputs_ref[:, lane : lane + LANES].T for lane in range(0, PD, LANES)], 0
+        )
+        inputs_t[...] = jnp.zeros_like(inputs_t)
+        for owner in range(w_embed.shape[0]):
+            inputs_t[owner, :own, :] = flipped[owner * own : (owner + 1) * own, :]
+        turn(a_ref, a_t)
 
     def qkv_step(n):
         qkv_ref[:, n * D : (n + 1) * D] = matmul(a_ref[...], columns_of(1 + n)).astype(BF)
@@ -900,14 +1161,17 @@
         lax.fori_loop(0, D // LANES, group, 0)
 
     def out_step():
+        turn(mixed_ref, mixed_t)
         middle_ref[...] = start_ref[...] + matmul(mixed_ref[...], columns_of(4))
         b_ref[...] = norm_rows(middle_ref[...], gains_ref[1:2, :])
+        turn(b_ref, b_t)
 
     def up_step(n):
         columns = slice(n * D, (n + 1) * D)
         after, slope = gelu_parts(matmul(b_ref[...], columns_of(5 + n)))
         hidden_ref[:, columns] = after.astype(BF)
         slope_ref[:, columns] = slope
+        turn(hidden_ref, hidden_t, n * D)
 
     def down_step(n):
         rows, owners = w_wide.shape[1], w_down.shape[0]
@@ -918,6 +1182,7 @@
 
     def link_step():
         z_ref[...] = norm_rows(end_ref[...], gains_ref[2:3, :])
+        turn(z_ref, z_t)
         seen_ref[...] = matmul(z_ref[...], columns_of(count - 1))
 
     work = [(6, 0, embed_step), (6, 1, partial(qkv_step, 0)), (7, 2, partial(qkv_step, 1))]
@@ -984,17 +1249,13 @@
     full = [jax.ShapeDtypeStruct((owners, *shape), BF) for shape in shapes[1:]]
     local = [
         jax.ShapeDtypeStruct((8, LANES), F32),
-        jax.ShapeDtypeStruct((VIS, PD), BF),
+        jax.ShapeDtypeStruct((owners, ROWS, VIS), BF),
+        *[jax.ShapeDtypeStruct((width, VIS), BF) for width in (D, D, D, FF, D)],
         jax.ShapeDtypeStruct((VIS, D), F32),
-        jax.ShapeDtypeStruct((VIS, D), BF),
         jax.ShapeDtypeStruct((VIS, 3 * D), BF),
-        jax.ShapeDtypeStruct((VIS, D), BF),
         jax.ShapeDtypeStruct((VIS, D), F32),
-        jax.ShapeDtypeStruct((VIS, D), BF),
         jax.ShapeDtypeStruct((VIS, FF), F32),
-        jax.ShapeDtypeStruct((VIS, FF), BF),
         jax.ShapeDtypeStruct((VIS, D), F32),
-        jax.ShapeDtypeStruct((VIS, D), BF),
         jax.ShapeDtypeStruct((VIS, DD), F32),
     ]
     vmem, anywhere = pl.BlockSpec(memory_space=pltpu.VMEM), pl.BlockSpec(memory_space=pl.ANY)
@@ -1004,7 +1265,8 @@
         out_shape=(*full, *local),
         in_specs=[vmem] * 5 + [anywhere] * 3,
         out_specs=(anywhere,) * 2 + (vmem,) * len(local),
-        scratch_shapes=[pltpu.VMEM((owners, *shape), BF) for shape in shapes]
+        scratch_shapes=[pltpu.VMEM((VIS, width), BF) for width in (PD, D, D, D, FF, D)]
+        + [pltpu.VMEM((owners, *shape), BF) for shape in shapes]
         + [
             pltpu.VMEM((6, 8, LANES), F32),
             pltpu.VMEM((6, 8, LANES), F32),
@@ -1198,26 +1460,24 @@
 
     lax.fori_loop(0, 2, follow, 0)
 
-    tall = DFF // owners
     rows = DD // owners
+
+    def store(block, grad):
+        grads_ref[:, block] = grad.astype(BF).reshape(owners, rows, UNIT)
+
+    parts = DFF // DD
     down_grad = left_t(hidden_ref[...], dbranch_ref[...]).astype(BF)
-    for owner in range(owners):
-        for part in range(tall // rows):
-            start = owner * tall + part * rows
-            grads_ref[owner * rows : (owner + 1) * rows, part * DD : (part + 1) * DD] = down_grad[
-                start : start + rows, :
-            ]
-    wide = DFF
-    for g in range(DD // LANES):
-        grads_ref[g * LANES : (g + 1) * LANES, wide + 3 * DD : wide + 4 * DD] = matmul(
-            mixed_t[g], dattn_ref[...]
-        ).astype(BF)
-    grads_ref[:, wide + 4 * DD : wide + 4 * DD + DFF] = left_t(
-        b_ref[...], dbefore_ref[...]
-    ).astype(BF)
-    grads_ref[:, wide + 4 * DD + DFF :] = left_t(z_ref[...], dpred_ref[...]).astype(BF)[
-        :, : PD + LOWD
-    ]
+    down_grad = down_grad.reshape(owners, parts, rows, UNIT)
+    for part in range(parts):
+        grads_ref[:, part] = down_grad[:, part]
+    store(
+        parts + 3,
+        jnp.concatenate([matmul(mixed_t[g], dattn_ref[...]) for g in range(DD // LANES)], 0),
+    )
+    for n in range(DFF // UNIT):
+        store(parts + 4 + n, left_t(b_ref[...], dbefore_ref[:, n * UNIT : (n + 1) * UNIT]))
+    for n in range(HEADP // UNIT):
+        store(parts + 8 + n, left_t(z_ref[...], dpred_ref[:, n * UNIT : (n + 1) * UNIT]))
 
     def attend_back_group(g, _):
         lanes = pl.ds(pl.multiple_of(g * LANES, LANES), LANES)
@@ -1242,11 +1502,9 @@
 
     lax.fori_loop(0, DD // LANES, attend_back_group, 0)
 
-    for n, ref in enumerate((dk_ref, dv_ref)):
-        grads_ref[:, wide + (n + 1) * DD : wide + (n + 2) * DD] = left_t(
-            a_ref[...], ref[...]
-        ).astype(BF)
-    grads_ref[:, wide : wide + DD] = left_t(a_ref[VIS:, :], dq_ref[...]).astype(BF)
+    store(parts, left_t(a_ref[VIS:, :], dq_ref[...]))
+    store(parts + 1, left_t(a_ref[...], dk_ref[...]))
+    store(parts + 2, left_t(a_ref[...], dv_ref[...]))
 
     def start_rows(rows, da):
         unit, rate = normalize(y_ref[rows, :])
@@ -1305,7 +1563,7 @@
     grads, dy, vec = pl.pallas_call(
         partial(decoder_kernel, owners),
         out_shape=(
-            jax.ShapeDtypeStruct((DD, DFF + wide.shape[1]), BF),
+            jax.ShapeDtypeStruct((owners, DFF // DD + 10, DD // owners, UNIT), BF),
             jax.ShapeDtypeStruct((VIS, DD), F32),
             jax.ShapeDtypeStruct((8, DD), F32),
         ),
@@ -1330,7 +1588,7 @@
         wide,
         down,
     )
-    return grads, dy, vec[:3], vec[3], jnp.sum(vec[4])
+    return grads, dy, vec[:4].reshape(-1), jnp.sum(vec[4])
 
 
 def block_forward(h, weights, gains, bias, heads, skip):
@@ -1372,43 +1630,6 @@
 
 def reduce_rows(grad):
     return lax.psum_scatter(grad.astype(BF), "fsdp", scatter_dimension=0, tiled=True)
-
-
-def sum_gradients(factors, encoded, dseen, inputs, dh_low, dec, vector_grad, local_loss):
-    lefts = [pair[0] for pair in factors] + [encoded.T]
-    owners = lax.axis_size("fsdp")
-    own = PD // owners
-    first = inputs.T.reshape(owners, own, VIS)
-    lefts.append(jnp.pad(first, ((0, 0), (0, ROWS - own), (0, 0))).reshape(-1, VIS))
-    rights = [pair[1] for pair in factors] + [dseen, dh_low]
-    blocks, units, spots = [], [], []
-
-    def add(left, sub, right, out, row, rows, column, columns):
-        blocks.append((left, sub))
-        for n in range(0, columns, UNIT):
-            units.append((len(blocks) - 1, right, n))
-            spots.append((out, row, rows, column + n, UNIT))
-
-    add(4, 0, 4, 1, 0, ROWS, 4 * D + FF, DD)
-    for n in range(FF // owners // ROWS):
-        add(3, n, 3, 2, n * ROWS, ROWS, 0, D)
-    add(2, 0, 2, 1, 0, ROWS, 4 * D, FF)
-    add(1, 0, 1, 1, 0, ROWS, 3 * D, D)
-    add(0, 0, 0, 1, 0, ROWS, 0, 3 * D)
-    add(5, 0, 5, 0, 0, own, 0, D)
-    shapes = ((own, D), (ROWS, 4 * D + FF + DD), (FF // owners, D))
-    length = vector_grad.shape[0]
-    rows = -(-(length + 1) // (8 * LANES)) * 8
-    vec = jnp.concatenate(
-        [vector_grad, local_loss[None], jnp.zeros((rows * LANES - length - 1,), F32)]
-    )
-    used = dec.shape[1]
-    dec = jnp.pad(dec, ((0, 0), (0, -used % (2 * UNIT))))
-    *parts, dec, vec = sum_products(
-        tuple(blocks), tuple(units), tuple(spots), shapes, lefts, rights, dec, vec.reshape(rows, LANES)
-    )
-    vec = vec.reshape(-1)
-    return parts, dec[:, :used], vec[:length], vec[length]
 
 
 def enc_split(wide, down):
@@ -1514,12 +1735,9 @@
     if fast:
         gains = jnp.pad(vectors[: 3 * D].reshape(3, D), ((0, 5), (0, 0)))
         stats = jnp.broadcast_to(stats[:, None], (8, LANES))
-        w_enc, w_enc_down, stats, inputs, h_start, *saved, h_end, encoded, seen_out = encoder_forward(
-            picked_pixels[:VIS], stats, pos_enc, bias_enc.T, gains, *low_enc
+        w_enc, w_enc_down, stats, *factors, h_start, qkv, middle, slope, h_end, seen_out = (
+            encoder_forward(picked_pixels[:VIS], stats, pos_enc, bias_enc.T, gains, *low_enc)
         )
-        normed_a, qkv, mixed, *saved = saved
-        enc_saved = (h_start, normed_a, *jnp.split(qkv, 3, 1), mixed.T, None, *saved)
-        enc_weights, w_link = enc_split(w_enc, w_enc_down)
     else:
         stats = jnp.broadcast_to(lax.psum(stats, ("dp", "fsdp"))[:, None], (8, LANES))
     count = stats[7, 0]
@@ -1537,7 +1755,7 @@
         encoded = layer_norm(h_end, gain_enc_out).astype(BF)
         seen_out = matmul(encoded, w_link)
     pos_dec = positions(coord, scale, DD)
-    dec_grads, dy_seen, dgains_dec, dtoken, local_loss = decoder_step(
+    dec_grads, dy_seen, dec_vec, local_loss = decoder_step(
         pos_dec,
         seen_out,
         kept,
@@ -1549,32 +1767,37 @@
         w_dec,
         w_dec_down,
     )
-    dec_sum = reduce_rows(dec_grads)
-    dseen = (dy_seen * keptf).astype(BF)
-    dh_end, dgain_enc_out = norm_back(h_end, gain_enc_out, right_t(dseen, w_link))
-    dh_start, enc_factors, dgains_enc = block_backward(
-        enc_saved, dh_end, enc_weights, gains_enc, bias_enc, HEADS, 0
-    )
-    dh_low = dh_start.astype(BF)
-    vector_grad = jnp.concatenate(
-        [
-            dgains_enc[0],
-            dgains_enc[1],
-            dgain_enc_out,
-            dgains_dec.reshape(-1),
-            dtoken,
-        ]
-    )
+    wide = wide_dec.shape[1]
     if fast:
-        enc_parts, dec_sum, vector_grad, loss_sum = sum_gradients(
-            enc_factors, encoded, dseen, inputs, dh_low, dec_sum, vector_grad, local_loss
+        vec = jnp.concatenate([jnp.zeros((3 * D,), F32), dec_vec, local_loss[None]])
+        vec = jnp.pad(vec, (0, 8 * D - vec.shape[0])).reshape(8, D)
+        inputs_t, a_t, mixed_t, b_t, hidden_t, z_t = factors
+        *enc_parts, dec_wide, dec_tall, vec = encoder_back(
+            dy_seen,
+            keptf,
+            vec,
+            gains,
+            bias_enc,
+            qkv,
+            dec_grads,
+            (h_end, middle, h_start, slope),
+            w_enc,
+            w_enc_down,
+            (z_t, hidden_t, b_t, mixed_t, a_t, inputs_t),
         )
+        dec_parts = (dec_wide[:, :wide], dec_tall)
+        vector_grad, loss_sum = vec[:5].reshape(-1), vec[5, 0]
     else:
+        dseen = (dy_seen * keptf).astype(BF)
+        dh_end, dgain_enc_out = norm_back(h_end, gain_enc_out, right_t(dseen, w_link))
+        dh_start, enc_factors, dgains_enc = block_backward(
+            enc_saved, dh_end, enc_weights, gains_enc, bias_enc, HEADS, 0
+        )
         enc_grads = [matmul(*pair).astype(BF) for pair in enc_factors]
         link_grad = left_t(encoded, dseen).astype(BF)
         enc_parts = lax.psum(
             (
-                reduce_rows(left_t(inputs, dh_low)),
+                reduce_rows(left_t(inputs, dh_start.astype(BF))),
                 reduce_rows(
                     jnp.concatenate([enc_grads[0], enc_grads[1], enc_grads[2], link_grad], 1)
                 ),
@@ -1582,11 +1805,14 @@
             ),
             "dp",
         )
+        dec_sum = lax.psum(reduce_rows(dec_grads), "dp")[0]
+        rows, parts = dec_sum.shape[1], DFF // DD
+        dec_parts = (
+            dec_sum[parts:].transpose(1, 0, 2).reshape(rows, -1)[:, :wide],
+            dec_sum[:parts].reshape(-1, DD),
+        )
+        vector_grad = jnp.concatenate([*dgains_enc, dgain_enc_out, dec_vec])
         vector_grad, loss_sum = lax.psum((vector_grad, local_loss), ("dp", "fsdp"))
-        dec_sum = lax.psum(dec_sum, "dp")
-    rows = dec_sum.shape[0]
-    down = dec_sum[:, :DFF].reshape(rows, -1, DD).transpose(1, 0, 2).reshape(-1, DD)
-    dec_parts = (dec_sum[:, DFF:], down)
     shard_grads = [g.astype(F32) for g in (*enc_parts, *dec_parts)]
     rate = STEP_UNIT * (PD * TOK_DEV * lax.axis_size("dp") * lax.axis_size("fsdp")) ** 0.5
     weights = (embed, wide_enc, enc_down, wide_dec, dec_down)

time: 518 us -> 480 us (0.927)
  local copies, waits for them, and re-layouts: 43.9 us -> 16.8 us
  matrix products: 30.2 us -> 4.65 us
  Pallas kernels: 352 us -> 377 us
  other arithmetic: 64.6 us -> 56 us
    dot_general x5 -> x0, matrix products: 25.5 us -> none  [right_t(): lax.dot_general(left, right, (((1,), (1,)), ((), ())), preferred_element_...]
    pallas_call x2 -> x1, Pallas kernels: 161 us -> 181 us  [encoder_back(): pl.pallas_call(partial(back_kernel, dec_units, tuple(blocks), tuple(units...]
    transpose x8 -> x1, local copies, waits for them, and re-layouts: 15.3 us -> 0.79 us  [body(): w_enc, w_enc_down, stats, *factors, h_start, qkv, middle, slope, h_end, s...]
    pallas_call x1, Pallas kernels: 119 us -> 124 us  [encoder_forward(): pl.pallas_call(encoder_kernel, out_shape=(*full, *local), in_specs=[vmem]...]
  transfers between devices with their start and end apart: 3 -> 2, of which waited for: 1 -> 0; matrix products, arithmetic and copies ran while one was open for 19% -> 9% of each run, Pallas kernels for 25% -> 26%
where the time goes in v6:
time: 480 us; the launch traced here: 471 us
  Pallas kernels  377 us (79%)
  other arithmetic  56 us (12%)
  local copies, waits for them, and re-layouts  16.8 us (4%)
  between operations  16.8 us (4%)
    pallas_call x1, Pallas kernels, encoder_back(): pl.pallas_call(partial(back_kernel, dec_units, tuple(blocks), tuple(units...  181 us
    pallas_call x1, Pallas kernels, encoder_forward(): pl.pallas_call(encoder_kernel, out_shape=(*full, *local), in_specs=[vmem]...  124 us
    pallas_call x1, Pallas kernels, decoder_step(): pl.pallas_call(partial(decoder_kernel, owners), out_shape=(jax.ShapeDtype...  72 us
    convert_element_type x5, other arithmetic, body(): outs += [buf, new, avg, new.astype(jnp.bfloat16)]  14.4 us
    add x6, other arithmetic, advance(): return (buf, new, AVERAGE * avg + (1.0 - AVERAGE) * new)  12.2 us
  transfers between devices with their start and end apart: 2, of which 0 were waited for; matrix products, arithmetic and copies ran while one was open for 9% of the time, Pallas kernels for 26%

profile of v6, /device:TPU:0, one launch (start us, length us, event | category | flops | bytes accessed | tf_op | source)
XLA Modules:
  0.0 471.5 jit_solution(1894873949022818964)
XLA Ops:
  7.3 1.9 convert_element_type.111
  9.3 2.2 convert_element_type.110
  15.8 1.2 fusion.4
  17.1 1.3 fusion.3
  18.4 1.3 add_add_fusion
  20.6 1.3 slice.139.picked_ref
  23.0 1.3 fusion.59
  24.4 1.3 multiply_exponential_fusion
  27.6 1.8 slice.140.bias_ref
  32.3 4.0 convert_element_type.106.wide_ref
  41.0 1.4 pad_maximum_fusion.2
  42.4 1.4 multiply_sine_fusion.3
  45.4 124.3 %shard_map.423 = (bf16[8,128,8704]{2,1,0:T(8,128)(2,1)}, bf16[8,512,1024]{2,1,0:T(8,128)(2,1)}, f32[8,128]{1,0:T(8,128)}, bf16[8,128,192]{2,1,0:T(8,128)(2,1)}, ...) custom-call(f32[192,768]{1,0:T(8,128)} %slice.135.picked_ref, ...), custom_call_target="tpu_custom_call" | custom-call | flops 5637144576 | bytes 209715200 | tf_op jit(solution)/shard_map/pallas_call | solution.py:1263
  171.0 2.8 multiply_sine_fusion.1
  173.8 1.2 pad_maximum_fusion.pos_ref
  176.8 72.0 %shard_map.424 = (bf16[8,14,64,512]{3,2,1,0:T(8,128)(2,1)}, f32[192,512]{1,0:T(8,128)}, f32[8,512]{1,0:T(8,128)}) custom-call(f32[768,512]{1,0:T(8,128)} %pad_maximum_fusion.pos_ref, f32[192,512]{1,0:T(8,128)} %get-tuple-element.49.seen_ref, f32[192,1]{1,0:T(8,128)} %copy.55.kept_ref, f32[576,1]{1,0:T(8,128)} %reshape.220.flag_ref, ...), custom_call_target="tpu_custom_call" | custom-call | flops 40000000000 | bytes 41943040 | tf_op jit(solution)/shard_map/pallas_call | solution.py:1563
  249.5 1.3 slice_reduce_fusion.1
  252.2 180.8 %shard_map.425 = (bf16[96,1024]{1,0:T(8,128)(2,1)}, bf16[128,8704]{1,0:T(8,128)(2,1)}, bf16[512,1024]{1,0:T(8,128)(2,1)}, bf16[64,5120]{1,0:T(8,128)(2,1)}, bf16[256,512]{1,0:T(8,128)(2,1)}, /*index=5*/f32[8,1024]{1,0:T(8,128)}) custom-call(f32[192,512]{1,0:T(8,128)} %get-tuple-element.51.dy_ref, f32[192,1]{1,0:T(8,128)} %copy.55.kept_ref, ...), custom_call_target="tpu_custom_call" | custom-call | flops 30000001024 | bytes 314572800 | tf_op jit(solution)/shard_map/pallas_call | solution.py:813
  434.9 8.4 %fusion.69 = (bf16[128,8704]{1,0:T(8,128)(2,1)}, f32[128,8704]{1,0:T(8,128)S(1)}, f32[128,8704]{1,0:T(8,128)}) fusion(f32[128,8704]{1,0:T(8,128)} %param.31, bf16[128,8704]{1,0:T(8,128)(2,1)} %get-tuple-element.68, f32[128,8704]{1,0:T(8,128)} %param.37), kind=kLoop, calls=%fused_computation.159 | loop fusion | flops 11141120 | bytes 22282240 | tf_op jit(solution)/shard_map/convert_element_type | solution.py:1826
  443.3 6.7 %multiply_add_fusion = f32[128,8704]{1,0:T(8,128)} fusion(f32[128,8704]{1,0:T(8,128)S(1)} %get-tuple-element.96, f32[128,8704]{1,0:T(8,128)} %param.43), kind=kLoop, calls=%fused_computation | loop fusion | flops 3342336 | bytes 13369344 | tf_op jit(solution)/shard_map/add | solution.py:1646
  450.1 2.4 fusion.67
  452.5 1.8 multiply_add_fusion.2
  455.8 1.7 fusion.65
  457.6 1.3 multiply_add_fusion.4
  (132 shorter events, 29.3 us)
Async XLA Ops:
  7.2 4.3 copy-start.23
  7.2 4.3 copy-start.26
  7.2 8.6 %copy-start.1 = (f32[768,768]{1,0:T(8,128)S(1)}, f32[768,768]{1,0:T(8,128)}, u32[]{:S(2)}) copy-start(f32[768,768]{1,0:T(8,128)} %param.24) | copy-start | bytes 7077892
  7.2 169.5 %all-gather.5.cloned.1.call-start = ((), (), s32[]{:S(2)}) async-start(), calls=%async_computation.1 | async-start | bytes 2359296 | tf_op jit(solution)/shard_map/all_gather | solution.py:1703
  9.2 167.5 %all-gather.3.cloned.1.call-start = ((), (), s32[]{:S(2)}) async-start(), calls=%async_computation | async-start | bytes 5898240 | tf_op jit(solution)/shard_map/all_gather | solution.py:1703
  25.7 3.8 copy-start.27
  32.3 4.0 copy-start.3
  36.3 3.5 slice-start.1
  36.3 6.1 %slice-start.2 = ((f32[768]{0:T(1024)}), f32[192]{0:T(256)S(1)}, s32[]{:S(2)}) async-start(f32[768]{0:T(1024)} %copy-done.27), calls=%async_computation.4 | async-start | bytes 2048 | tf_op jit(solution)/shard_map/slice | solution.py:1733
  443.3 6.8 %copy-start = (f32[128,8704]{1,0:T(8,128)}, f32[128,8704]{1,0:T(8,128)S(1)}, u32[]{:S(2)}) copy-start(f32[128,8704]{1,0:T(8,128)S(1)} %get-tuple-element.96) | copy-start | bytes 13369348
  443.3 6.8 %copy-start.6 = (f32[512,1024]{1,0:T(8,128)S(1)}, f32[512,1024]{1,0:T(8,128)}, u32[]{:S(2)}) copy-start(f32[512,1024]{1,0:T(8,128)} %param.38) | copy-start | bytes 6291460
  443.3 6.8 %copy-start.14 = (bf16[512,1024]{1,0:T(8,128)(2,1)S(1)}, bf16[512,1024]{1,0:T(8,128)(2,1)}, u32[]{:S(2)}) copy-start(bf16[512,1024]{1,0:T(8,128)(2,1)} %get-tuple-element.69) | copy-start | bytes 3145732
  450.1 2.4 copy-start.7
  452.4 2.3 copy-start.4
  452.4 3.2 copy-start.12
  452.5 3.4 copy-start.15
  457.5 3.3 copy-start.5
  457.5 3.2 copy-start.17
  458.8 2.9 copy-start.19
  458.8 2.9 copy-start.21
  460.8 2.8 copy-start.8
  460.8 2.8 copy-start.22
  460.8 2.8 copy-start.24
  460.8 2.8 copy-start.25
  (12 other events, 22.8 us)
Sparse Core Ops, SparseCore 0:
  10.5 30.5 all-gather.4
  43.6 61.2 all-gather.2

commit v7 on v6

--- a/solution.py
+++ b/solution.py
@@ -889,10 +889,11 @@
 
 
 def encoder_kernel(
-    picked_ref,
-    stats_ref,
-    pos_ref,
-    bias_ref,
+    pixels_ref,
+    row_ref,
+    column_ref,
+    scale_ref,
+    omega_ref,
     gains_ref,
     embed_ref,
     wide_ref,
@@ -900,6 +901,11 @@
     wide_out,
     down_out,
     stats_out,
+    by_row,
+    by_column,
+    picked_out,
+    pos_out,
+    bias_out,
     inputs_t,
     a_t,
     mixed_t,
@@ -921,6 +927,14 @@
     w_embed,
     w_wide,
     w_down,
+    stage_ref,
+    pick_ref,
+    high_ref,
+    mid_ref,
+    low_ref,
+    picked_ref,
+    pos_ref,
+    bias_ref,
     v_in,
     v_out,
     load_sem,
@@ -956,12 +970,18 @@
         pl.semaphore_signal(barrier, inc=1, device_id=across, device_id_type=MESH)
         pl.semaphore_wait(barrier, 5)
 
-    loads = [
-        pltpu.make_async_copy(shard, whole.at[f], load_sem.at[n])
-        for n, (shard, whole) in enumerate(zip(shards, gathered))
-    ]
-    for load in loads:
-        load.start()
+    stages = stage_ref.shape[0]
+
+    def load(t):
+        array, row, rows, column, columns, _ = pieces[t]
+        return pltpu.make_async_copy(
+            shards[array].at[pl.ds(row, rows), pl.ds(column, columns)],
+            stage_ref.at[t % stages, pl.ds(0, rows), pl.ds(0, columns)],
+            load_sem.at[t % stages],
+        )
+
+    for t in range(stages):
+        load(t).start()
 
     def spot(t, owner, half=None):
         array, row, rows, column, columns, _ = pieces[t]
@@ -972,11 +992,7 @@
 
     def move(t, owner, send, recv, device, half=None):
         target = spot(t, owner, half)
-        source = target
-        if send < 3:
-            array, row, rows, column, columns, _ = pieces[t]
-            source = shards[array].at[pl.ds(row, rows), pl.ds(column, columns)]
-        return put(source, target, send_sem.at[t, send], recv_sem.at[t, recv], device)
+        return put(target, target, send_sem.at[t, send], recv_sem.at[t, recv], device)
 
     def own_x(t):
         return move(t, f, 0, 0, x_side)
@@ -1009,6 +1025,11 @@
             pl.when(z % 2 != kind - 1)(other)
 
     def first(t):
+        load(t).wait()
+        array, row, rows, column, columns, _ = pieces[t]
+        spot(t, f)[...] = stage_ref[t % stages, :rows, :columns].astype(BF)
+        if t + stages < count:
+            load(t + stages).start()
         own_core(t).start()
 
         def then():
@@ -1073,9 +1094,7 @@
 
     def statistics(i):
         if i <= 3:
-            if i == 0:
-                v_out[0] = stats_ref[...]
-            else:
+            if i > 0:
                 copy_v(i - 1, sides[i - 1]).wait_recv()
                 v_out[i] = v_out[i - 1] + v_in[i - 1]
             if i < 3:
@@ -1116,6 +1135,66 @@
         array, row, rows, column, columns, _ = pieces[t]
         weight = gathered[array][:, row : row + rows, column : column + columns]
         return weight.reshape(-1, columns)
+
+    def local_statistics():
+        pixels = pixels_ref[...]
+        weighted = pixels * column_ref[:, 0:1]
+        sums = jnp.sum(weighted, 0, keepdims=True)
+        squares = jnp.sum(weighted * pixels, 0, keepdims=True)
+        live = row_ref[0:1, :]
+        totals = [r[:, n * PATCH**2 : (n + 1) * PATCH**2] for r in (sums, squares) for n in range(BANDS)]
+        for n, total in enumerate((*totals, live, live * row_ref[1:2, :])):
+            v_out[0, n : n + 1, :] = jnp.broadcast_to(jnp.sum(total, 1, keepdims=True), (1, LANES))
+
+    def arrange_step():
+        slots = (TOK_DEV, TOK_DEV)
+        down, along = [lax.broadcasted_iota(jnp.int32, slots, n) for n in range(2)]
+        live, masked = row_ref[0:1, :], row_ref[1:2, :]
+        seen, hid = live * (1.0 - masked), live * masked
+        kind = lax.broadcasted_iota(jnp.int32, row_ref.shape, 0)
+        kinds = jnp.where(kind == 0, seen, jnp.where(kind == 1, hid, 1.0 - live))
+        ranks = matmul(kinds.astype(BF), jnp.where(down < along, 1.0, 0.0).astype(BF))
+        n_seen, n_hid = [jnp.sum(r, 1, keepdims=True) for r in (seen, hid)]
+        empty = ranks[2:3, :]
+        place = jnp.where(empty < VIS - n_seen, n_seen + empty, n_seen + n_hid + empty)
+        place = jnp.where(hid > 0, VIS + ranks[1:2, :], place)
+        place = jnp.where(seen > 0, ranks[0:1, :], place)
+        pick_ref[...] = jnp.where(down == place.astype(jnp.int32), 1.0, 0.0).astype(BF)
+        facts = row_ref[...].astype(BF)
+        by_row[...] = right_t(facts, pick_ref[...])
+        by_column[...] = right_t(pick_ref[...], facts)
+        pixels = pixels_ref[...]
+        high = pixels.astype(BF)
+        rest = pixels - high.astype(F32)
+        mid = rest.astype(BF)
+        high_ref[...], mid_ref[...] = high, mid
+        low_ref[...] = (rest - mid.astype(F32)).astype(BF)
+
+    def pick_rows(rows):
+        pick = pick_ref[rows, :]
+        return matmul(pick, high_ref[...]) + matmul(pick, mid_ref[...]) + matmul(pick, low_ref[...])
+
+    def pick_step():
+        picked_ref[...] = pick_rows(slice(0, VIS))
+        same = by_column[:VIS, 2:3] == by_row[2:3, :VIS]
+        shape = (VIS, VIS)
+        bias_out[...] = mask_bias(by_column[:VIS, 0:1] > 0, same, shape, 0)
+        bias_ref[...] = mask_bias(by_row[0:1, :VIS] > 0, same, shape, 0, 1)
+
+    def position_rows(target, rows, width, row):
+        quarter = width // 4
+        odd = by_column[rows, 2:3] > 0
+        scale = jnp.where(odd, scale_ref[1:2, 0:1], scale_ref[0:1, 0:1])
+        for n in range(2):
+            angle = by_column[rows, 3 + n : 4 + n] * scale * omega_ref[row : row + 1, :quarter]
+            target[rows, 2 * n * quarter : (2 * n + 1) * quarter] = jnp.sin(angle)
+            target[rows, (2 * n + 1) * quarter : (2 * n + 2) * quarter] = jnp.cos(angle)
+
+    def hidden_step(n):
+        rows = slice(n * VIS, (n + 1) * VIS)
+        if n > 0:
+            picked_out[(n - 1) * VIS : n * VIS, :] = pick_rows(rows)
+        position_rows(pos_out, rows, DD, 1)
 
     def embed_step():
         pixels = stats_out[6:7, :] * (PATCH * PATCH)
@@ -1185,16 +1264,18 @@
         turn(z_ref, z_t)
         seen_ref[...] = matmul(z_ref[...], columns_of(count - 1))
 
-    work = [(6, 0, embed_step), (6, 1, partial(qkv_step, 0)), (7, 2, partial(qkv_step, 1))]
+    work = [(0, None, arrange_step), (1, None, pick_step)]
+    work += [(2, None, partial(position_rows, pos_ref, slice(0, VIS), D, 0))]
+    work += [(at, None, partial(hidden_step, n)) for n, at in enumerate((3, 4, 11, 14))]
+    work += [(6, 0, embed_step), (6, 1, partial(qkv_step, 0)), (7, 2, partial(qkv_step, 1))]
     work += [(8, 3, partial(qkv_step, 2)), (8, None, attention_step), (9, 4, out_step)]
     work += [(at, 5 + n, partial(up_step, n)) for n, at in enumerate((10, 10, 12, 13))]
     work += [(at, 9 + n, partial(down_step, n)) for n, at in enumerate((13, 15, 16, 16))]
     work += [(17, count - 1, link_step)]
     stores = []
 
-    for load in loads:
-        load.wait()
     first(0)
+    local_statistics()
     first(1)
     for i in range(18):
         if i + 2 < count:
@@ -1242,13 +1323,22 @@
         copy_v(5, z_side).wait_send()
 
 
-def encoder_forward(picked, stats, pos, bias, gains, embed, wide, down):
+def encoder_forward(pixels, facts, scale, gains, embed, wide, down):
     owners = lax.axis_size("fsdp")
     shapes = [w.shape for w in (embed, wide, down)]
     count = len(encoder_pieces(shapes))
+    omega = [
+        10000.0 ** (-jnp.arange(width // 4, dtype=jnp.float32) / (width // 4)) for width in (D, DD)
+    ]
+    omega = jnp.stack([omega[0], jnp.pad(omega[1], (0, D // 4 - DD // 4))] + [omega[0]] * 6)
     full = [jax.ShapeDtypeStruct((owners, *shape), BF) for shape in shapes[1:]]
     local = [
         jax.ShapeDtypeStruct((8, LANES), F32),
+        jax.ShapeDtypeStruct((8, TOK_DEV), F32),
+        jax.ShapeDtypeStruct((TOK_DEV, 8), F32),
+        jax.ShapeDtypeStruct((HID, PD), F32),
+        jax.ShapeDtypeStruct((TOK_DEV, DD), F32),
+        jax.ShapeDtypeStruct((VIS, VIS), F32),
         jax.ShapeDtypeStruct((owners, ROWS, VIS), BF),
         *[jax.ShapeDtypeStruct((width, VIS), BF) for width in (D, D, D, FF, D)],
         jax.ShapeDtypeStruct((VIS, D), F32),
@@ -1263,14 +1353,19 @@
     wide_full, down_full, *rest = pl.pallas_call(
         encoder_kernel,
         out_shape=(*full, *local),
-        in_specs=[vmem] * 5 + [anywhere] * 3,
+        in_specs=[vmem] * 6 + [anywhere] * 3,
         out_specs=(anywhere,) * 2 + (vmem,) * len(local),
         scratch_shapes=[pltpu.VMEM((VIS, width), BF) for width in (PD, D, D, D, FF, D)]
         + [pltpu.VMEM((owners, *shape), BF) for shape in shapes]
         + [
+            pltpu.VMEM((4, ROWS, D), F32),
+            *[pltpu.VMEM((TOK_DEV, PD), BF)] * 4,
+            pltpu.VMEM((VIS, PD), F32),
+            pltpu.VMEM((VIS, D), F32),
+            pltpu.VMEM((VIS, VIS), F32),
             pltpu.VMEM((6, 8, LANES), F32),
             pltpu.VMEM((6, 8, LANES), F32),
-            dma((3,)),
+            dma((4,)),
             dma((count,)),
             dma((count, 11)),
             dma((count, 11)),
@@ -1278,18 +1373,23 @@
             dma((6,)),
         ],
         compiler_params=pltpu.CompilerParams(
-            collective_id=1, has_side_effects=True, vmem_limit_bytes=56 * 2**20
+            collective_id=1, has_side_effects=True, vmem_limit_bytes=60 * 2**20
         ),
         cost_estimate=pl.CostEstimate(
             flops=2 * VIS * 14 * 2**20, bytes_accessed=200 * 2**20, transcendentals=0
         ),
-    )(picked, stats, pos, bias, gains, embed, wide, down)
+    )(pixels, facts, facts.T, scale, omega, gains, embed, wide, down)
     return (wide_full.reshape(D, -1), down_full.reshape(FF, D), *rest)
 
 
 LOWP = 256
 HEADP = PD + LOWP
 BLOCK = HID // 2
+
+
+def mask_bias(live, same, shape, offset, keys=0):
+    key, query = [lax.broadcasted_iota(jnp.int32, shape, (keys + n) % 2) for n in range(2)]
+    return jnp.where((live & same) | (key + offset == query), 0.0, NEGATIVE)
 
 
 def normalize(h):
@@ -1317,11 +1417,10 @@
     owners,
     pos_ref,
     seen_ref,
-    kept_ref,
-    flag_ref,
+    row_ref,
+    column_ref,
     picked_ref,
     stats_ref,
-    bias_ref,
     gains_ref,
     pool_ref,
     spread_ref,
@@ -1352,6 +1451,7 @@
     dk_ref,
     dv_ref,
     loss_ref,
+    bias_ref,
 ):
     size = DD // DHEADS
     per = LANES // size
@@ -1360,6 +1460,15 @@
     token = gains_ref[3:4, :]
     lane_head = lax.broadcasted_iota(jnp.int32, (HID, LANES), 1) // size
     key_head = lax.broadcasted_iota(jnp.int32, (TOK_DEV, LANES), 1) // size
+    kept = column_ref[:VIS, 0:1] > 0
+    for start in range(0, TOK_DEV, VIS):
+        rows = slice(start, start + VIS)
+        bias_ref[rows, :] = mask_bias(
+            column_ref[rows, 0:1] > 0,
+            column_ref[rows, 2:3] == row_ref[2:3, VIS:],
+            (VIS, HID),
+            start - VIS,
+        )
     vec_ref[...] = jnp.zeros_like(vec_ref)
     loss_ref[...] = jnp.zeros_like(loss_ref)
     head_ref[...] = jnp.zeros_like(head_ref)
@@ -1372,7 +1481,7 @@
         v_ref[rows, :] = matmul(a, wide_ref[:, 2 * DD : 3 * DD]).astype(BF)
         return a
 
-    y_ref[:VIS, :] = pos_ref[:VIS, :] + jnp.where(kept_ref[...] > 0, seen_ref[...], token)
+    y_ref[:VIS, :] = pos_ref[:VIS, :] + jnp.where(kept, seen_ref[...], token)
     y_ref[VIS:, :] = pos_ref[VIS:, :] + token
     project(slice(0, VIS), False)
 
@@ -1435,7 +1544,7 @@
         coarse = exact_product(normed, pool_ref[...])
         err_high = pred[:, :PD] - (normed - exact_product(coarse, spread_ref[...]))
         err_low = pred[:, PD:] - coarse
-        flag = flag_ref[rows, :]
+        flag = column_ref[all_rows, 0:1]
         length = jnp.sqrt(err_high * err_high + 1.0)
         loss_ref[:, :PD] += jnp.sum((length - 1.0) * flag, 0, keepdims=True) * (1.0 / PD)
         loss_ref[:, PD:] += jnp.sum(err_low * err_low * flag, 0, keepdims=True) * (1.0 / LOWD)
@@ -1516,7 +1625,7 @@
 
     dy = start_rows(slice(0, VIS), 0.0)
     dy_ref[...] = dy
-    vec_ref[3:4, :] += jnp.sum(jnp.where(kept_ref[...] > 0, 0.0, dy), 0, keepdims=True)
+    vec_ref[3:4, :] += jnp.sum(jnp.where(kept, 0.0, dy), 0, keepdims=True)
 
     def start_hidden(n, _):
         rows, all_rows = hidden_rows(n)
@@ -1528,7 +1637,7 @@
     vec_ref[4:5, :] = loss_ref[:, :DD] + loss_ref[:, DD:]
 
 
-def decoder_step(pos, seen, kept, flag, picked, stats, bias, vectors, wide, down):
+def decoder_step(pos, seen, by_row, by_column, picked, stats, vectors, wide, down):
     index = jnp.arange(PD)
     band, row, column = index // PATCH**2, index // PATCH % PATCH, index % PATCH
     low = band * (PATCH // 2) ** 2 + row // 2 * (PATCH // 2) + column // 2
@@ -1558,6 +1667,7 @@
         ((TOK_DEV, DD), BF),
         ((TOK_DEV, DD), BF),
         ((1, HEADP), F32),
+        ((TOK_DEV, HID), F32),
     ]
     vmem = pl.BlockSpec(memory_space=pltpu.VMEM)
     grads, dy, vec = pl.pallas_call(
@@ -1567,7 +1677,7 @@
             jax.ShapeDtypeStruct((VIS, DD), F32),
             jax.ShapeDtypeStruct((8, DD), F32),
         ),
-        in_specs=[vmem] * 12,
+        in_specs=[vmem] * 11,
         out_specs=(vmem,) * 3,
         scratch_shapes=[pltpu.VMEM(*entry) for entry in scratch],
         compiler_params=pltpu.CompilerParams(vmem_limit_bytes=60 * 2**20),
@@ -1577,11 +1687,10 @@
     )(
         pos,
         seen,
-        kept.astype(F32)[:, None],
-        flag[:, None],
+        by_row,
+        by_column,
         picked,
         stats,
-        bias,
         gains,
         (spread.T * 0.25).astype(BF),
         spread.astype(BF),
@@ -1644,6 +1753,45 @@
     buf = MOMENTUM * mom + grad
     new = weight - rate * (grad + MOMENTUM * buf)
     return (buf, new, AVERAGE * avg + (1.0 - AVERAGE) * new)
+
+
+def advance_kernel(rate, *refs):
+    grads, weights, moms, avgs, outs = [refs[5 * n : 5 * n + 5] for n in range(4)] + [refs[20:]]
+
+    def update(n):
+        weight = weights[n][...]
+        grad = grads[n][:, : weight.shape[1]].astype(F32)
+        buf, new, avg = advance(weight, moms[n][...], avgs[n][...], grad, rate)
+        outs[4 * n][...] = buf
+        outs[4 * n + 1][...] = new
+        outs[4 * n + 2][...] = avg
+        outs[4 * n + 3][...] = new.astype(BF)
+
+    pl.when(pl.program_id(0) == 0)(partial(update, 0))
+    for n in range(1, 5):
+        update(n)
+
+
+def advance_all(rate, grads, weights, moms, avgs):
+    steps = weights[3].shape[0] // 16
+
+    def spec(n, array):
+        if n == 0:
+            return pl.BlockSpec(array.shape, lambda i: (0, 0))
+        return pl.BlockSpec((array.shape[0] // steps, array.shape[1]), lambda i: (i, 0))
+
+    arrays = [a for group in (grads, weights, moms, avgs) for a in group]
+    outs = [(n, jax.ShapeDtypeStruct(w.shape, t)) for n, w in enumerate(weights) for t in (F32, F32, F32, BF)]
+    size = sum(w.size for w in weights)
+    return pl.pallas_call(
+        partial(advance_kernel, rate),
+        grid=(steps,),
+        out_shape=[out for _, out in outs],
+        in_specs=[spec(n % 5, a) for n, a in enumerate(arrays)],
+        out_specs=[spec(n, out) for n, out in outs],
+        compiler_params=pltpu.CompilerParams(vmem_limit_bytes=58 * 2**20),
+        cost_estimate=pl.CostEstimate(flops=12 * size, bytes_accessed=28 * size, transcendentals=0),
+    )(*arrays)
 
 
 def arrange(valid, masked, scene_ids):
@@ -1702,72 +1850,68 @@
     w_dec, w_dec_down = [
         lax.all_gather(w.astype(BF), "fsdp", axis=0, tiled=True) for w in (wide_dec, dec_down)
     ]
-    rows_ok = valid.astype(jnp.float32)
-    flags = rows_ok * masked.astype(jnp.float32)
-    bands = pixels.reshape(slots, BANDS, PATCH * PATCH)
-    weighted = bands * rows_ok[:, None, None]
-    band_sum = jnp.sum(weighted, axis=(0, 2))
-    counts = jnp.stack([jnp.sum(rows_ok), jnp.sum(flags)])
-    band_sq = jnp.sum(weighted * bands, axis=(0, 2))
-    stats = jnp.concatenate([band_sum, band_sq, counts])
-
-    pick, n_seen, n_hid = arrange(valid, masked, scene_ids)
-    picked_pixels = exact_pick(pick, pixels)
-    small = matmul(
-        pick, jnp.concatenate([(scene_ids % 2)[:, None], coords], 1).astype(BF)
-    )
-    odd, coord = small[:, 0], small[:, 1:]
-    level = jnp.where(odd == 0, gsd_index[0], gsd_index[1]).astype(jnp.float32)
-    scale = jnp.exp2(0.5 * level - 1.0)
-    index = jnp.arange(slots, dtype=jnp.int32)
-    kept = index[:VIS] < n_seen
-    hidden_ok = index[:HID] < n_hid
-    live = jnp.concatenate([kept, hidden_ok])
-    keptf = kept.astype(jnp.float32)[:, None]
-    allow = live[:, None] & (odd[:, None] == odd[None, :]) | (index[:, None] == index[None, :])
-    bias = jnp.where(allow, 0.0, NEGATIVE)
-    bias_enc, bias_dec = bias[:VIS, :VIS], bias[:, VIS:]
-
+    levels = jnp.exp2(0.5 * gsd_index.astype(jnp.float32) - 1.0)
     gains_enc = (vectors[:D], vectors[D : 2 * D])
     gain_enc_out = vectors[2 * D : 3 * D]
-    pos_enc = positions(coord[:VIS], scale[:VIS], D)
-    low_enc = [w.astype(BF) for w in (embed, wide_enc, enc_down)]
     if fast:
+        facts = jnp.stack([valid, masked, scene_ids % 2, coords[:, 0], coords[:, 1]])
+        facts = jnp.pad(facts, ((0, 3), (0, 0))).astype(F32)
+        scale = jnp.pad(jnp.broadcast_to(levels[:, None], (2, LANES)), ((0, 6), (0, 0)))
         gains = jnp.pad(vectors[: 3 * D].reshape(3, D), ((0, 5), (0, 0)))
-        stats = jnp.broadcast_to(stats[:, None], (8, LANES))
-        w_enc, w_enc_down, stats, *factors, h_start, qkv, middle, slope, h_end, seen_out = (
-            encoder_forward(picked_pixels[:VIS], stats, pos_enc, bias_enc.T, gains, *low_enc)
+        w_enc, w_enc_down, stats, by_row, by_column, picked_hidden, pos_dec, bias_enc, *saved = (
+            encoder_forward(pixels, facts, scale, gains, embed, wide_enc, enc_down)
         )
+        *factors, h_start, qkv, middle, slope, h_end, seen_out = saved
     else:
+        rows_ok = valid.astype(jnp.float32)
+        flags = rows_ok * masked.astype(jnp.float32)
+        bands = pixels.reshape(slots, BANDS, PATCH * PATCH)
+        weighted = bands * rows_ok[:, None, None]
+        band_sum = jnp.sum(weighted, axis=(0, 2))
+        counts = jnp.stack([jnp.sum(rows_ok), jnp.sum(flags)])
+        band_sq = jnp.sum(weighted * bands, axis=(0, 2))
+        stats = jnp.concatenate([band_sum, band_sq, counts])
         stats = jnp.broadcast_to(lax.psum(stats, ("dp", "fsdp"))[:, None], (8, LANES))
+        pick, n_seen, n_hid = arrange(valid, masked, scene_ids)
+        picked_pixels = exact_pick(pick, pixels)
+        picked_hidden = picked_pixels[VIS:]
+        small = matmul(pick, jnp.concatenate([(scene_ids % 2)[:, None], coords], 1).astype(BF))
+        odd, coord = small[:, 0], small[:, 1:]
+        scale = jnp.where(odd == 0, levels[0], levels[1])
+        index = jnp.arange(slots, dtype=jnp.int32)
+        live = jnp.concatenate([index[:VIS] < n_seen, index[:HID] < n_hid])
+        allow = live[:, None] & (odd[:, None] == odd[None, :]) | (index[:, None] == index[None, :])
+        bias_enc = jnp.where(allow, 0.0, NEGATIVE)[:VIS, :VIS]
+        by_row = jnp.pad(jnp.stack([live.astype(F32), odd, odd]), ((0, 5), (0, 0)))
+        by_column = by_row.T
+        pos_dec = positions(coord, scale, DD)
     count = stats[7, 0]
     if not fast:
         w_embed, w_enc, w_enc_down = [
-            lax.all_gather(w, "fsdp", axis=0, tiled=True) for w in low_enc
+            lax.all_gather(w.astype(BF), "fsdp", axis=0, tiled=True)
+            for w in (embed, wide_enc, enc_down)
         ]
         enc_weights, w_link = enc_split(w_enc, w_enc_down)
         mean = jnp.repeat(stats[:3, 0] / (stats[6, 0] * (PATCH * PATCH)), PATCH * PATCH)
         square = jnp.repeat(stats[3:6, 0] / (stats[6, 0] * (PATCH * PATCH)), PATCH * PATCH)
         rate = lax.rsqrt(square - mean * mean + EPS)
         inputs = ((picked_pixels[:VIS] - mean) * rate).astype(BF)
-        h_start = matmul(inputs, w_embed) + pos_enc
+        h_start = matmul(inputs, w_embed) + positions(coord[:VIS], scale[:VIS], D)
         h_end, enc_saved = block_forward(h_start, enc_weights, gains_enc, bias_enc, HEADS, 0)
         encoded = layer_norm(h_end, gain_enc_out).astype(BF)
         seen_out = matmul(encoded, w_link)
-    pos_dec = positions(coord, scale, DD)
     dec_grads, dy_seen, dec_vec, local_loss = decoder_step(
         pos_dec,
         seen_out,
-        kept,
-        hidden_ok.astype(F32),
-        picked_pixels[VIS:],
+        by_row,
+        by_column,
+        picked_hidden,
         stats,
-        bias_dec,
         vectors[3 * D :],
         w_dec,
         w_dec_down,
     )
-    wide = wide_dec.shape[1]
+    keptf = by_column[:VIS, 0:1]
     if fast:
         vec = jnp.concatenate([jnp.zeros((3 * D,), F32), dec_vec, local_loss[None]])
         vec = jnp.pad(vec, (0, 8 * D - vec.shape[0])).reshape(8, D)
@@ -1785,7 +1929,7 @@
             w_enc_down,
             (z_t, hidden_t, b_t, mixed_t, a_t, inputs_t),
         )
-        dec_parts = (dec_wide[:, :wide], dec_tall)
+        dec_parts = (dec_wide, dec_tall)
         vector_grad, loss_sum = vec[:5].reshape(-1), vec[5, 0]
     else:
         dseen = (dy_seen * keptf).astype(BF)
@@ -1808,22 +1952,17 @@
         dec_sum = lax.psum(reduce_rows(dec_grads), "dp")[0]
         rows, parts = dec_sum.shape[1], DFF // DD
         dec_parts = (
-            dec_sum[parts:].transpose(1, 0, 2).reshape(rows, -1)[:, :wide],
+            dec_sum[parts:].transpose(1, 0, 2).reshape(rows, -1),
             dec_sum[:parts].reshape(-1, DD),
         )
         vector_grad = jnp.concatenate([*dgains_enc, dgain_enc_out, dec_vec])
         vector_grad, loss_sum = lax.psum((vector_grad, local_loss), ("dp", "fsdp"))
-    shard_grads = [g.astype(F32) for g in (*enc_parts, *dec_parts)]
+    grads = (*enc_parts, *dec_parts)
     rate = STEP_UNIT * (PD * TOK_DEV * lax.axis_size("dp") * lax.axis_size("fsdp")) ** 0.5
     weights = (embed, wide_enc, enc_down, wide_dec, dec_down)
     moms = (embed_mom, wide_enc_mom, enc_down_mom, wide_dec_mom, dec_down_mom)
     avgs = (embed_avg, wide_enc_avg, enc_down_avg, wide_dec_avg, dec_down_avg)
-    outs = []
-    for number in range(5):
-        buf, new, avg = advance(
-            weights[number], moms[number], avgs[number], shard_grads[number], rate
-        )
-        outs += [buf, new, avg, new.astype(jnp.bfloat16)]
+    outs = advance_all(rate, grads, weights, moms, avgs)
     return (*outs, *advance(vectors, vector_mom, vector_avg, vector_grad, rate), loss_sum, count)
 
 

time: 480 us -> 444 us (0.925)
  other arithmetic: 56 us -> 9.2 us
  Pallas kernels: 377 us -> 402 us
  local copies, waits for them, and re-layouts: 16.8 us -> 9.62 us
    convert_element_type x8 -> x0, other arithmetic: 20.3 us -> none  [the longest x5 14.4 us: body(): outs += [buf, new, avg, new.astype(jnp.bfloat16)]]
    pallas_call x0 -> x1, Pallas kernels: none -> 19.5 us  [advance_all(): pl.pallas_call(partial(advance_kernel, rate), grid=(steps,), out_shape=[o...]
    add x6 -> x1, other arithmetic: 12.2 us -> 0.63 us  [advance(): return (buf, new, AVERAGE * avg + (1.0 - AVERAGE) * new)]
    pallas_call x1, Pallas kernels: 124 us -> 134 us  [encoder_forward(): pl.pallas_call(encoder_kernel, out_shape=(*full, *local), in_specs=[vmem]...]
  transfers between devices with their start and end apart: 2 -> 2, of which waited for: 0 -> 0; matrix products, arithmetic and copies ran while one was open for 9% -> 3% of each run, Pallas kernels for 26% -> 31%
where the time goes in v7:
time: 444 us; the launch traced here: 436 us
  Pallas kernels  402 us (91%)
  between operations  14.7 us (3%)
  local copies, waits for them, and re-layouts  9.62 us (2%)
  other arithmetic  9.2 us (2%)
    pallas_call x1, Pallas kernels, encoder_back(): pl.pallas_call(partial(back_kernel, dec_units, tuple(blocks), tuple(units...  177 us
    pallas_call x1, Pallas kernels, encoder_forward(): pl.pallas_call(encoder_kernel, out_shape=(*full, *local), in_specs=[vmem]...  134 us
    pallas_call x1, Pallas kernels, decoder_step(): pl.pallas_call(partial(decoder_kernel, owners), out_shape=(jax.ShapeDtype...  72.2 us
    pallas_call x1, Pallas kernels, advance_all(): pl.pallas_call(partial(advance_kernel, rate), grid=(steps,), out_shape=[o...  19.5 us
  transfers between devices with their start and end apart: 2, of which 0 were waited for; matrix products, arithmetic and copies ran while one was open for 3% of the time, Pallas kernels for 31%

profile of v7, /device:TPU:0, one launch (start us, length us, event | category | flops | bytes accessed | tf_op | source)
XLA Modules:
  0.0 436.2 jit_solution(9151808709105480044)
XLA Ops:
  7.3 1.8 convert_element_type.34
  9.2 2.2 convert_element_type.33
  11.6 0.2 copy.56
  11.8 0.8 fusion.23
  12.6 0.7 copy.57.row_ref
  13.3 0.6 pad.30.gains_ref
  14.0 0.6 pad.31.gains_ref
  14.6 0.6 stack.30.omega_ref
  15.3 0.7 pad.28.scale_ref
  15.9 133.5 %shard_map.423 = (bf16[8,128,8704]{2,1,0:T(8,128)(2,1)}, bf16[8,512,1024]{2,1,0:T(8,128)(2,1)}, f32[8,128]{1,0:T(8,128)}, f32[8,768]{1,0:T(8,128)}, f32[768,8]{1...) custom-call(f32[768,768]{1,0:T(8,128)} %pixels_ref.1, ...), custom_call_target="tpu_custom_call" | custom-call | flops 5637144576 | bytes 209715200 | tf_op jit(solution)/shard_map/pallas_call | solution.py:1353
  149.5 1.5 slice.56.kept_ref
  151.0 1.2 slice.61
  152.2 0.8 fusion.spread_ref
  153.0 0.9 select_convert_fusion.pool_ref
  153.9 72.2 %shard_map.424 = (bf16[8,14,64,512]{3,2,1,0:T(8,128)(2,1)}, f32[192,512]{1,0:T(8,128)}, f32[8,512]{1,0:T(8,128)}) custom-call(f32[768,512]{1,0:T(8,128)} %get-tuple-element.74.pos_ref, f32[192,512]{1,0:T(8,128)} %get-tuple-element.75.seen_ref, f32[8,768]{1,0:T(8,128)} %get-tuple-element.76.row_ref, f32[768,8]{1,0:T(8,128)} %get-tuple-element.77.column_ref, ...), custom_call_target="tpu_custom_call" | custom-call | flops 40000000000 | bytes 41943040 | tf_op jit(solution)/shard_map/pallas_call | solution.py:1673
  226.1 0.7 slice_bitcast_fusion
  226.8 1.3 slice_reduce_fusion
  228.2 0.6 select_maximum_fusion
  228.8 0.6 reshape.192.vec_ref
  229.4 177.3 %shard_map.425 = (bf16[96,1024]{1,0:T(8,128)(2,1)}, bf16[128,8704]{1,0:T(8,128)(2,1)}, bf16[512,1024]{1,0:T(8,128)(2,1)}, bf16[64,5120]{1,0:T(8,128)(2,1)}, bf16[256,512]{1,0:T(8,128)(2,1)}, /*index=5*/f32[8,1024]{1,0:T(8,128)}) custom-call(f32[192,512]{1,0:T(8,128)} %get-tuple-element.80.dy_ref, f32[192,1]{1,0:T(8,128)} %slice.56.kept_ref, ...), custom_call_target="tpu_custom_call" | custom-call | flops 30000001024 | bytes 314572800 | tf_op jit(solution)/shard_map/pallas_call | solution.py:813
  406.7 1.2 slice.60
  407.9 0.8 reshape.202
  408.7 0.6 multiply_add_fusion
  409.3 19.5 %shard_map.426 = (f32[96,1024]{1,0:T(8,128)}, f32[96,1024]{1,0:T(8,128)}, f32[96,1024]{1,0:T(8,128)}, bf16[96,1024]{1,0:T(8,128)(2,1)}, f32[128,8704]{1,0:T(8,12...) custom-call(bf16[96,1024]{1,0:T(8,128)(2,1)} %get-tuple-element.97.r, ...), custom_call_target="tpu_custom_call" | custom-call | flops 26296320 | bytes 61358080 | tf_op jit(solution)/shard_map/pallas_call | solution.py:1786
  (42 shorter events, 0.3 us)
Async XLA Ops:
  7.2 4.2 copy-start.6
  7.2 4.2 copy-start.4
  7.2 4.3 copy-start.5
  7.2 4.3 copy-start.3
  7.2 146.7 %all-gather.5.cloned.1.call-start = ((), (), s32[]{:S(2)}) async-start(), calls=%async_computation.1 | async-start | bytes 2359296 | tf_op jit(solution)/shard_map/all_gather | solution.py:1851
  9.1 4.2 slice-start
  9.1 4.9 %copy-start.7 = (s32[2]{0:T(128)S(1)}, s32[2]{0:T(128)}, u32[]{:S(2)}) copy-start(s32[2]{0:T(128)} %param.28) | copy-start | bytes 28
  9.1 4.9 %slice-start.1 = ((f32[5120]{0:T(1024)}), f32[2048]{0:T(1024)S(1)}, s32[]{:S(2)}) async-start(f32[5120]{0:T(1024)} %param.35), calls=%async_computation.3 | async-start | bytes 16384 | tf_op jit(solution)/shard_map/slice | solution.py:1910
  9.1 144.8 %all-gather.3.cloned.1.call-start = ((), (), s32[]{:S(2)}) async-start(), calls=%async_computation | async-start | bytes 5898240 | tf_op jit(solution)/shard_map/all_gather | solution.py:1851
  229.4 179.2 %copy-start = (f32[5120]{0:T(1024)S(1)}, f32[5120]{0:T(1024)}, u32[]{:S(2)}) copy-start(f32[5120]{0:T(1024)} %param.35) | copy-start | bytes 61444
  229.4 179.2 %copy-start.1 = (f32[5120]{0:T(1024)S(1)}, f32[5120]{0:T(1024)}, u32[]{:S(2)}) copy-start(f32[5120]{0:T(1024)} %param.47) | copy-start | bytes 61444
  229.4 179.2 %copy-start.2 = (f32[5120]{0:T(1024)S(1)}, f32[5120]{0:T(1024)}, u32[]{:S(2)}) copy-start(f32[5120]{0:T(1024)} %param.41) | copy-start | bytes 61444
Sparse Core Ops, SparseCore 0:
  10.5 39.1 all-gather.4
  52.2 62.3 all-gather.2

commit v8 on v7

--- a/solution.py
+++ b/solution.py
@@ -210,7 +210,7 @@
 HALF = UNIT // 2
 ROWS = 128
 HALF_ROWS = ROWS // 2
-LAGS = (2, 4, 6, 8, 11)
+LAGS = (1, 2, 3, 4, 6)
 
 
 def put(source, target, send, recv, device):
@@ -230,9 +230,9 @@
     units,
     spots,
     dy_ref,
-    kept_ref,
+    column_ref,
     vec_ref,
-    gains_ref,
+    vectors_ref,
     bias_ref,
     qkv_ref,
     dec_ref,
@@ -437,7 +437,7 @@
     def copy_v(step, device):
         return put(v_out.at[step], v_in.at[step], v_send.at[step], v_recv.at[step], device)
 
-    gain_one, gain_two, gain_out = [gains_ref[n : n + 1, :] for n in range(3)]
+    gain_one, gain_two, gain_out = [vectors_ref[:, n * D : (n + 1) * D] for n in range(3)]
 
     def give(r, value):
         yo[r] = value
@@ -447,7 +447,7 @@
         return slice(n * UNIT, (n + 1) * UNIT)
 
     def back_link():
-        dseen = jnp.where(kept_ref[...] > 0, dy_ref[...], 0.0).astype(BF)
+        dseen = jnp.where(column_ref[:VIS, 0:1] > 0, dy_ref[...], 0.0).astype(BF)
         give(0, dseen)
         wide_copy(0).wait()
         h_copy(end_ref).wait()
@@ -774,7 +774,7 @@
         lax.fori_loop(0, count, drain, 0)
 
 
-def encoder_back(dy, kept, vec, gains, bias, qkv, dec, states, wide, down, lefts):
+def encoder_back(dy, by_column, vec, vectors, bias, qkv, dec, states, wide, down, lefts):
     owners = lax.axis_size("fsdp")
     own = PD // owners
     dec_units = dec.shape[1] * dec.shape[2] // ROWS
@@ -867,17 +867,20 @@
         cost_estimate=pl.CostEstimate(
             flops=30 * 10**9, bytes_accessed=300 * 2**20, transcendentals=0
         ),
-    )(dy, kept, vec, gains, bias, qkv, dec, *states, wide, down, *lefts)
+    )(dy, by_column, vec, vectors, bias, qkv, dec, *states, wide, down, *lefts)
 
 
 def encoder_pieces(shapes):
-    (own, width), (rows, _), (tall, _) = shapes
-    pieces = [(0, 0, own, 0, width, 0)]
+    (own, width), (rows, _), (tall, _), (dec_rows, dec_width), (dec_tall, _) = shapes
+    half = dec_rows // 2
+    pieces = [(3, n * half, half, 0, dec_width, n + 1) for n in range(2)]
+    pieces += [(0, 0, own, 0, width, 0)]
     pieces += [(1, 0, rows, n * D, D, (1, 2, 0)[n]) for n in range(3)]
     pieces += [(1, 0, rows, 3 * D, D, 1)]
     pieces += [(1, 0, rows, 4 * D + n * D, D, (2, 0, 1, 2)[n]) for n in range(FF // D)]
     pieces += [(2, n * rows, rows, 0, D, (0, 1, 2, 0)[n]) for n in range(tall // rows)]
     pieces += [(1, 0, rows, 4 * D + FF, DD, 0)]
+    pieces += [(4, 0, dec_tall, 0, DD, 0)]
     return pieces
 
 
@@ -894,16 +897,21 @@
     column_ref,
     scale_ref,
     omega_ref,
-    gains_ref,
+    vectors_ref,
     embed_ref,
     wide_ref,
     down_ref,
+    dec_wide_ref,
+    dec_down_ref,
     wide_out,
     down_out,
+    dec_wide_out,
+    dec_down_out,
+    picked_out,
+    slope_out,
     stats_out,
     by_row,
     by_column,
-    picked_out,
     pos_out,
     bias_out,
     inputs_t,
@@ -915,7 +923,6 @@
     start_ref,
     qkv_ref,
     middle_ref,
-    slope_ref,
     end_ref,
     seen_ref,
     inputs_ref,
@@ -935,6 +942,12 @@
     picked_ref,
     pos_ref,
     bias_ref,
+    dec_stage,
+    dec_stage_down,
+    dec_own,
+    dec_own_down,
+    slope_ref,
+    hidden_pixels,
     v_in,
     v_out,
     load_sem,
@@ -943,10 +956,14 @@
     recv_sem,
     v_send,
     v_recv,
+    side_sem,
 ):
-    shards, gathered = (embed_ref, wide_ref, down_ref), (w_embed, w_wide, w_down)
+    shards = (embed_ref, wide_ref, down_ref, dec_wide_ref, dec_down_ref)
+    gathered = (w_embed, w_wide, w_down, dec_wide_out, dec_down_out)
+    gain_one, gain_two, gain_out = [vectors_ref[:, n * D : (n + 1) * D] for n in range(3)]
     pieces = encoder_pieces([ref.shape for ref in shards])
-    count = len(pieces)
+    count, base = len(pieces), 2
+    stores = []
     z, f = lax.axis_index("dp"), lax.axis_index("fsdp")
     core, place = f % 2, f // 2
     x, y = place % 2, place // 2
@@ -976,23 +993,40 @@
         array, row, rows, column, columns, _ = pieces[t]
         return pltpu.make_async_copy(
             shards[array].at[pl.ds(row, rows), pl.ds(column, columns)],
-            stage_ref.at[t % stages, pl.ds(0, rows), pl.ds(0, columns)],
-            load_sem.at[t % stages],
+            stage_ref.at[staged[t], pl.ds(0, rows), pl.ds(0, columns)],
+            load_sem.at[staged[t]],
         )
 
-    for t in range(stages):
+    encoder = [t for t, piece in enumerate(pieces) if piece[0] < 3]
+    staged = {t: n % stages for n, t in enumerate(encoder)}
+    after = dict(zip(encoder, encoder[stages:]))
+    dec_loads = [
+        pltpu.make_async_copy(dec_wide_ref, dec_stage, side_sem.at[0]),
+        pltpu.make_async_copy(dec_down_ref, dec_stage_down, side_sem.at[1]),
+    ]
+    for copy in dec_loads:
+        copy.start()
+    for t in encoder[:stages]:
         load(t).start()
 
     def spot(t, owner, half=None):
         array, row, rows, column, columns, _ = pieces[t]
+        if array > 2:
+            if half is not None:
+                rows //= 2
+                row += half * rows
+            return gathered[array].at[owner, pl.ds(row, rows)]
         if half is not None:
             columns //= 2
             column += half * columns
         return gathered[array].at[owner, pl.ds(row, rows), pl.ds(column, columns)]
 
     def move(t, owner, send, recv, device, half=None):
-        target = spot(t, owner, half)
-        return put(target, target, send_sem.at[t, send], recv_sem.at[t, recv], device)
+        target = source = spot(t, owner, half)
+        array, row, rows = pieces[t][:3]
+        if send < 3 and array > 2:
+            source = (dec_own, dec_own_down)[array - 3].at[pl.ds(row, rows)]
+        return put(source, target, send_sem.at[t, send], recv_sem.at[t, recv], device)
 
     def own_x(t):
         return move(t, f, 0, 0, x_side)
@@ -1025,11 +1059,22 @@
             pl.when(z % 2 != kind - 1)(other)
 
     def first(t):
-        load(t).wait()
         array, row, rows, column, columns, _ = pieces[t]
-        spot(t, f)[...] = stage_ref[t % stages, :rows, :columns].astype(BF)
-        if t + stages < count:
-            load(t + stages).start()
+        if array < 3:
+            load(t).wait()
+            spot(t, f)[...] = stage_ref[staged[t], :rows, :columns].astype(BF)
+            if t in after:
+                load(after[t]).start()
+        else:
+            if row == 0:
+                dec_loads[array - 3].wait()
+            own = (dec_own, dec_own_down)[array - 3]
+            own[row : row + rows, :] = (dec_stage, dec_stage_down)[array - 3][
+                row : row + rows, :
+            ].astype(BF)
+            store = pltpu.make_async_copy(own.at[pl.ds(row, rows)], spot(t, f), store_sem.at[t])
+            store.start()
+            stores.append(store)
         own_core(t).start()
 
         def then():
@@ -1190,10 +1235,18 @@
             target[rows, 2 * n * quarter : (2 * n + 1) * quarter] = jnp.sin(angle)
             target[rows, (2 * n + 1) * quarter : (2 * n + 2) * quarter] = jnp.cos(angle)
 
+    def pixel_store(n):
+        return pltpu.make_async_copy(
+            hidden_pixels, picked_out.at[pl.ds((n - 1) * VIS, VIS)], side_sem.at[4]
+        )
+
     def hidden_step(n):
         rows = slice(n * VIS, (n + 1) * VIS)
         if n > 0:
-            picked_out[(n - 1) * VIS : n * VIS, :] = pick_rows(rows)
+            if n > 1:
+                pixel_store(n - 1).wait()
+            hidden_pixels[...] = pick_rows(rows)
+            pixel_store(n).start()
         position_rows(pos_out, rows, DD, 1)
 
     def embed_step():
@@ -1205,8 +1258,8 @@
             for part in range(PATCH * PATCH // LANES):
                 lanes = pl.ds(band * PATCH * PATCH + part * LANES, LANES)
                 inputs_ref[:, lanes] = ((picked_ref[:, lanes] - mean) * rate).astype(BF)
-        start_ref[...] = matmul(inputs_ref[...], columns_of(0)) + pos_ref[...]
-        a_ref[...] = norm_rows(start_ref[...], gains_ref[0:1, :])
+        start_ref[...] = matmul(inputs_ref[...], columns_of(base)) + pos_ref[...]
+        a_ref[...] = norm_rows(start_ref[...], gain_one)
         own = w_embed.shape[1]
         flipped = jnp.concatenate(
             [inputs_ref[:, lane : lane + LANES].T for lane in range(0, PD, LANES)], 0
@@ -1217,7 +1270,7 @@
         turn(a_ref, a_t)
 
     def qkv_step(n):
-        qkv_ref[:, n * D : (n + 1) * D] = matmul(a_ref[...], columns_of(1 + n)).astype(BF)
+        qkv_ref[:, n * D : (n + 1) * D] = matmul(a_ref[...], columns_of(base + 1 + n)).astype(BF)
 
     def attention_step():
         size = D // HEADS
@@ -1241,43 +1294,51 @@
 
     def out_step():
         turn(mixed_ref, mixed_t)
-        middle_ref[...] = start_ref[...] + matmul(mixed_ref[...], columns_of(4))
-        b_ref[...] = norm_rows(middle_ref[...], gains_ref[1:2, :])
+        middle_ref[...] = start_ref[...] + matmul(mixed_ref[...], columns_of(base + 4))
+        b_ref[...] = norm_rows(middle_ref[...], gain_two)
         turn(b_ref, b_t)
+
+    def slope_store(n):
+        return pltpu.make_async_copy(
+            slope_ref.at[n % 2], slope_out.at[:, pl.ds(n * D, D)], side_sem.at[2 + n % 2]
+        )
 
     def up_step(n):
         columns = slice(n * D, (n + 1) * D)
-        after, slope = gelu_parts(matmul(b_ref[...], columns_of(5 + n)))
+        after, slope = gelu_parts(matmul(b_ref[...], columns_of(base + 5 + n)))
         hidden_ref[:, columns] = after.astype(BF)
-        slope_ref[:, columns] = slope
+        if n > 1:
+            slope_store(n - 2).wait()
+        slope_ref[n % 2] = slope
+        slope_store(n).start()
         turn(hidden_ref, hidden_t, n * D)
 
     def down_step(n):
         rows, owners = w_wide.shape[1], w_down.shape[0]
         tall = w_down.shape[1]
         parts = [hidden_ref[:, o * tall + n * rows : o * tall + (n + 1) * rows] for o in range(owners)]
-        total = matmul(jnp.concatenate(parts, 1), columns_of(9 + n))
+        total = matmul(jnp.concatenate(parts, 1), columns_of(base + 9 + n))
         end_ref[...] = (middle_ref[...] if n == 0 else end_ref[...]) + total
 
     def link_step():
-        z_ref[...] = norm_rows(end_ref[...], gains_ref[2:3, :])
+        z_ref[...] = norm_rows(end_ref[...], gain_out)
         turn(z_ref, z_t)
-        seen_ref[...] = matmul(z_ref[...], columns_of(count - 1))
+        seen_ref[...] = matmul(z_ref[...], columns_of(base + 13))
 
     work = [(0, None, arrange_step), (1, None, pick_step)]
     work += [(2, None, partial(position_rows, pos_ref, slice(0, VIS), D, 0))]
     work += [(at, None, partial(hidden_step, n)) for n, at in enumerate((3, 4, 11, 14))]
-    work += [(6, 0, embed_step), (6, 1, partial(qkv_step, 0)), (7, 2, partial(qkv_step, 1))]
-    work += [(8, 3, partial(qkv_step, 2)), (8, None, attention_step), (9, 4, out_step)]
-    work += [(at, 5 + n, partial(up_step, n)) for n, at in enumerate((10, 10, 12, 13))]
-    work += [(at, 9 + n, partial(down_step, n)) for n, at in enumerate((13, 15, 16, 16))]
-    work += [(17, count - 1, link_step)]
-    stores = []
+    work += [(6, base, embed_step), (8, base + 1, partial(qkv_step, 0))]
+    work += [(9, base + 2, partial(qkv_step, 1)), (9, base + 3, partial(qkv_step, 2))]
+    work += [(9, None, attention_step), (11, base + 4, out_step)]
+    work += [(at, base + 5 + n, partial(up_step, n)) for n, at in enumerate((12, 12, 14, 15))]
+    work += [(at, base + 9 + n, partial(down_step, n)) for n, at in enumerate((15, 17, 18, 18))]
+    work += [(19, base + 13, link_step)]
 
     first(0)
     local_statistics()
     first(1)
-    for i in range(18):
+    for i in range(20):
         if i + 2 < count:
             first(i + 2)
         statistics(i)
@@ -1306,6 +1367,12 @@
                     store.start()
                     stores.append(store)
             run()
+    for t, piece in enumerate(pieces):
+        if piece[0] > 2:
+            whole(t)
+    for n in range(2):
+        slope_store(FF // D - 2 + n).wait()
+    pixel_store(HID // VIS).wait()
     for store in stores:
         store.wait()
     for t in range(count):
@@ -1323,20 +1390,20 @@
         copy_v(5, z_side).wait_send()
 
 
-def encoder_forward(pixels, facts, scale, gains, embed, wide, down):
+def encoder_forward(pixels, facts, scale, vectors, *shards):
     owners = lax.axis_size("fsdp")
-    shapes = [w.shape for w in (embed, wide, down)]
+    shapes = [w.shape for w in shards]
     count = len(encoder_pieces(shapes))
     omega = [
         10000.0 ** (-jnp.arange(width // 4, dtype=jnp.float32) / (width // 4)) for width in (D, DD)
     ]
     omega = jnp.stack([omega[0], jnp.pad(omega[1], (0, D // 4 - DD // 4))] + [omega[0]] * 6)
     full = [jax.ShapeDtypeStruct((owners, *shape), BF) for shape in shapes[1:]]
+    full += [jax.ShapeDtypeStruct((HID, PD), F32), jax.ShapeDtypeStruct((VIS, FF), F32)]
     local = [
         jax.ShapeDtypeStruct((8, LANES), F32),
         jax.ShapeDtypeStruct((8, TOK_DEV), F32),
         jax.ShapeDtypeStruct((TOK_DEV, 8), F32),
-        jax.ShapeDtypeStruct((HID, PD), F32),
         jax.ShapeDtypeStruct((TOK_DEV, DD), F32),
         jax.ShapeDtypeStruct((VIS, VIS), F32),
         jax.ShapeDtypeStruct((owners, ROWS, VIS), BF),
@@ -1344,25 +1411,28 @@
         jax.ShapeDtypeStruct((VIS, D), F32),
         jax.ShapeDtypeStruct((VIS, 3 * D), BF),
         jax.ShapeDtypeStruct((VIS, D), F32),
-        jax.ShapeDtypeStruct((VIS, FF), F32),
         jax.ShapeDtypeStruct((VIS, D), F32),
         jax.ShapeDtypeStruct((VIS, DD), F32),
     ]
     vmem, anywhere = pl.BlockSpec(memory_space=pltpu.VMEM), pl.BlockSpec(memory_space=pl.ANY)
     dma = pltpu.SemaphoreType.DMA
-    wide_full, down_full, *rest = pl.pallas_call(
+    wide_full, down_full, dec_wide, dec_down, *rest = pl.pallas_call(
         encoder_kernel,
         out_shape=(*full, *local),
-        in_specs=[vmem] * 6 + [anywhere] * 3,
-        out_specs=(anywhere,) * 2 + (vmem,) * len(local),
+        in_specs=[vmem] * 6 + [anywhere] * len(shards),
+        out_specs=(anywhere,) * len(full) + (vmem,) * len(local),
         scratch_shapes=[pltpu.VMEM((VIS, width), BF) for width in (PD, D, D, D, FF, D)]
-        + [pltpu.VMEM((owners, *shape), BF) for shape in shapes]
+        + [pltpu.VMEM((owners, *shape), BF) for shape in shapes[:3]]
         + [
             pltpu.VMEM((4, ROWS, D), F32),
             *[pltpu.VMEM((TOK_DEV, PD), BF)] * 4,
             pltpu.VMEM((VIS, PD), F32),
             pltpu.VMEM((VIS, D), F32),
             pltpu.VMEM((VIS, VIS), F32),
+            *[pltpu.VMEM(shape, F32) for shape in shapes[3:]],
+            *[pltpu.VMEM(shape, BF) for shape in shapes[3:]],
+            pltpu.VMEM((2, VIS, D), F32),
+            pltpu.VMEM((VIS, PD), F32),
             pltpu.VMEM((6, 8, LANES), F32),
             pltpu.VMEM((6, 8, LANES), F32),
             dma((4,)),
@@ -1371,6 +1441,7 @@
             dma((count, 11)),
             dma((6,)),
             dma((6,)),
+            dma((5,)),
         ],
         compiler_params=pltpu.CompilerParams(
             collective_id=1, has_side_effects=True, vmem_limit_bytes=60 * 2**20
@@ -1378,8 +1449,14 @@
         cost_estimate=pl.CostEstimate(
             flops=2 * VIS * 14 * 2**20, bytes_accessed=200 * 2**20, transcendentals=0
         ),
-    )(pixels, facts, facts.T, scale, omega, gains, embed, wide, down)
-    return (wide_full.reshape(D, -1), down_full.reshape(FF, D), *rest)
+    )(pixels, facts, facts.T, scale, omega, vectors, *shards)
+    return (
+        wide_full.reshape(D, -1),
+        down_full.reshape(FF, D),
+        dec_wide.reshape(DD, -1),
+        dec_down.reshape(DFF, DD),
+        *rest,
+    )
 
 
 LOWP = 256
@@ -1421,14 +1498,12 @@
     column_ref,
     picked_ref,
     stats_ref,
-    gains_ref,
-    pool_ref,
-    spread_ref,
+    vectors_ref,
     wide_ref,
     down_ref,
     grads_ref,
     dy_ref,
-    vec_ref,
+    vec_out,
     y_ref,
     a_ref,
     q_ref,
@@ -1452,12 +1527,24 @@
     dv_ref,
     loss_ref,
     bias_ref,
+    pool_ref,
+    spread_ref,
+    vec_ref,
 ):
     size = DD // DHEADS
     per = LANES // size
     factor = size ** (-0.5)
-    gain_one, gain_two, gain_out = [gains_ref[n : n + 1, :] for n in range(3)]
-    token = gains_ref[3:4, :]
+    gain_one, gain_two, gain_out, token = [
+        vectors_ref[:, 3 * D + n * DD : 3 * D + (n + 1) * DD] for n in range(4)
+    ]
+
+    def pooled(shape, pixels):
+        pixel, low = [lax.broadcasted_iota(jnp.int32, shape, (pixels + n) % 2) for n in range(2)]
+        row, column = (pixel >> 4) & 15, pixel & 15
+        return ((pixel >> 8) << 6) + ((row >> 1) << 3) + (column >> 1) == low
+
+    pool_ref[...] = jnp.where(pooled((PD, LOWP), 0), 0.25, 0.0).astype(BF)
+    spread_ref[...] = jnp.where(pooled((LOWP, PD), 1), 1.0, 0.0).astype(BF)
     lane_head = lax.broadcasted_iota(jnp.int32, (HID, LANES), 1) // size
     key_head = lax.broadcasted_iota(jnp.int32, (TOK_DEV, LANES), 1) // size
     kept = column_ref[:VIS, 0:1] > 0
@@ -1634,15 +1721,13 @@
         return 0
 
     lax.fori_loop(0, 2, start_hidden, 0)
-    vec_ref[4:5, :] = loss_ref[:, :DD] + loss_ref[:, DD:]
+    vec_out[...] = jnp.zeros_like(vec_out)
+    for n in range(4):
+        vec_out[3 + n // 2 : 4 + n // 2, n % 2 * DD : (n % 2 + 1) * DD] = vec_ref[n : n + 1, :]
+    vec_out[5:6, :] = jnp.broadcast_to(jnp.sum(loss_ref[...], 1, keepdims=True), (1, D))
 
 
 def decoder_step(pos, seen, by_row, by_column, picked, stats, vectors, wide, down):
-    index = jnp.arange(PD)
-    band, row, column = index // PATCH**2, index // PATCH % PATCH, index % PATCH
-    low = band * (PATCH // 2) ** 2 + row // 2 * (PATCH // 2) + column // 2
-    spread = low[None, :] == jnp.arange(LOWP)[:, None]
-    gains = jnp.pad(vectors.reshape(4, DD), ((0, 4), (0, 0)))
     owners = lax.axis_size("fsdp")
     scratch = [
         ((TOK_DEV, DD), F32),
@@ -1668,6 +1753,9 @@
         ((TOK_DEV, DD), BF),
         ((1, HEADP), F32),
         ((TOK_DEV, HID), F32),
+        ((PD, LOWP), BF),
+        ((LOWP, PD), BF),
+        ((8, DD), F32),
     ]
     vmem = pl.BlockSpec(memory_space=pltpu.VMEM)
     grads, dy, vec = pl.pallas_call(
@@ -1675,9 +1763,9 @@
         out_shape=(
             jax.ShapeDtypeStruct((owners, DFF // DD + 10, DD // owners, UNIT), BF),
             jax.ShapeDtypeStruct((VIS, DD), F32),
-            jax.ShapeDtypeStruct((8, DD), F32),
+            jax.ShapeDtypeStruct((8, D), F32),
         ),
-        in_specs=[vmem] * 11,
+        in_specs=[vmem] * 9,
         out_specs=(vmem,) * 3,
         scratch_shapes=[pltpu.VMEM(*entry) for entry in scratch],
         compiler_params=pltpu.CompilerParams(vmem_limit_bytes=60 * 2**20),
@@ -1691,13 +1779,11 @@
         by_column,
         picked,
         stats,
-        gains,
-        (spread.T * 0.25).astype(BF),
-        spread.astype(BF),
+        vectors,
         wide,
         down,
     )
-    return grads, dy, vec[:4].reshape(-1), jnp.sum(vec[4])
+    return grads, dy, vec
 
 
 def block_forward(h, weights, gains, bias, heads, skip):
@@ -1847,9 +1933,7 @@
 ):
     slots = pixels.shape[0]
     fast = (lax.axis_size("dp"), lax.axis_size("fsdp")) == (4, 8)
-    w_dec, w_dec_down = [
-        lax.all_gather(w.astype(BF), "fsdp", axis=0, tiled=True) for w in (wide_dec, dec_down)
-    ]
+    vector_row = vectors.reshape(1, -1)
     levels = jnp.exp2(0.5 * gsd_index.astype(jnp.float32) - 1.0)
     gains_enc = (vectors[:D], vectors[D : 2 * D])
     gain_enc_out = vectors[2 * D : 3 * D]
@@ -1857,11 +1941,11 @@
         facts = jnp.stack([valid, masked, scene_ids % 2, coords[:, 0], coords[:, 1]])
         facts = jnp.pad(facts, ((0, 3), (0, 0))).astype(F32)
         scale = jnp.pad(jnp.broadcast_to(levels[:, None], (2, LANES)), ((0, 6), (0, 0)))
-        gains = jnp.pad(vectors[: 3 * D].reshape(3, D), ((0, 5), (0, 0)))
-        w_enc, w_enc_down, stats, by_row, by_column, picked_hidden, pos_dec, bias_enc, *saved = (
-            encoder_forward(pixels, facts, scale, gains, embed, wide_enc, enc_down)
+        w_enc, w_enc_down, w_dec, w_dec_down, picked_hidden, slope, *saved = encoder_forward(
+            pixels, facts, scale, vector_row, embed, wide_enc, enc_down, wide_dec, dec_down
         )
-        *factors, h_start, qkv, middle, slope, h_end, seen_out = saved
+        stats, by_row, by_column, pos_dec, bias_enc, *saved = saved
+        *factors, h_start, qkv, middle, h_end, seen_out = saved
     else:
         rows_ok = valid.astype(jnp.float32)
         flags = rows_ok * masked.astype(jnp.float32)
@@ -1887,9 +1971,9 @@
         pos_dec = positions(coord, scale, DD)
     count = stats[7, 0]
     if not fast:
-        w_embed, w_enc, w_enc_down = [
+        w_embed, w_enc, w_enc_down, w_dec, w_dec_down = [
             lax.all_gather(w.astype(BF), "fsdp", axis=0, tiled=True)
-            for w in (embed, wide_enc, enc_down)
+            for w in (embed, wide_enc, enc_down, wide_dec, dec_down)
         ]
         enc_weights, w_link = enc_split(w_enc, w_enc_down)
         mean = jnp.repeat(stats[:3, 0] / (stats[6, 0] * (PATCH * PATCH)), PATCH * PATCH)
@@ -1900,27 +1984,24 @@
         h_end, enc_saved = block_forward(h_start, enc_weights, gains_enc, bias_enc, HEADS, 0)
         encoded = layer_norm(h_end, gain_enc_out).astype(BF)
         seen_out = matmul(encoded, w_link)
-    dec_grads, dy_seen, dec_vec, local_loss = decoder_step(
+    dec_grads, dy_seen, vec = decoder_step(
         pos_dec,
         seen_out,
         by_row,
         by_column,
         picked_hidden,
         stats,
-        vectors[3 * D :],
+        vector_row,
         w_dec,
         w_dec_down,
     )
-    keptf = by_column[:VIS, 0:1]
     if fast:
-        vec = jnp.concatenate([jnp.zeros((3 * D,), F32), dec_vec, local_loss[None]])
-        vec = jnp.pad(vec, (0, 8 * D - vec.shape[0])).reshape(8, D)
         inputs_t, a_t, mixed_t, b_t, hidden_t, z_t = factors
         *enc_parts, dec_wide, dec_tall, vec = encoder_back(
             dy_seen,
-            keptf,
+            by_column,
             vec,
-            gains,
+            vector_row,
             bias_enc,
             qkv,
             dec_grads,
@@ -1932,7 +2013,8 @@
         dec_parts = (dec_wide, dec_tall)
         vector_grad, loss_sum = vec[:5].reshape(-1), vec[5, 0]
     else:
-        dseen = (dy_seen * keptf).astype(BF)
+        dseen = (dy_seen * by_column[:VIS, 0:1]).astype(BF)
+        dec_vec, local_loss = vec[3:5].reshape(-1), vec[5, 0]
         dh_end, dgain_enc_out = norm_back(h_end, gain_enc_out, right_t(dseen, w_link))
         dh_start, enc_factors, dgains_enc = block_backward(
             enc_saved, dh_end, enc_weights, gains_enc, bias_enc, HEADS, 0

time: 444 us -> 416 us (0.937)
  between operations: 14.7 us -> 1.23 us
  other arithmetic: 9.2 us -> 2.16 us
    pallas_call x1, Pallas kernels: 134 us -> 127 us  [encoder_forward(): pl.pallas_call(encoder_kernel, out_shape=(*full, *local), in_specs=[vmem]...]
    convert_element_type x4 -> x0, other arithmetic: 5.74 us -> none  [the longest x2 4 us: body(): w.astype(BF)]
  transfers between devices with their start and end apart: 2 -> 0, of which waited for: 0 -> 0; matrix products, arithmetic and copies ran while one was open for 3% -> 0% of each run, Pallas kernels for 31% -> 0%
where the time goes in v8:
time: 416 us; the launch traced here: 408 us
  Pallas kernels  399 us (96%)
  local copies, waits for them, and re-layouts  6.17 us (1%)
    pallas_call x1, Pallas kernels, encoder_back(): pl.pallas_call(partial(back_kernel, dec_units, tuple(blocks), tuple(units...  179 us
    pallas_call x1, Pallas kernels, encoder_forward(): pl.pallas_call(encoder_kernel, out_shape=(*full, *local), in_specs=[vmem]...  127 us
    pallas_call x1, Pallas kernels, decoder_step(): pl.pallas_call(partial(decoder_kernel, owners), out_shape=(jax.ShapeDtype...  72.6 us
    pallas_call x1, Pallas kernels, advance_all(): pl.pallas_call(partial(advance_kernel, rate), grid=(steps,), out_shape=[o...  19.6 us

profile of v8, /device:TPU:0, one launch (start us, length us, event | category | flops | bytes accessed | tf_op | source)
XLA Modules:
  0.0 408.1 jit_solution(9509086240432681775)
XLA Ops:
  0.7 0.0 copy-start.4
  0.7 0.8 slice_bitcast_fusion
  1.5 0.7 add_select_fusion
  2.2 0.7 stack.12
  2.8 0.7 stack.26
  3.6 0.2 copy.56
  3.8 0.8 fusion.1
  4.6 0.7 copy.57.row_ref
  5.3 0.6 stack.30.omega_ref
  6.0 0.0 copy-done.4
  6.0 0.7 pad.16.scale_ref
  6.7 127.1 %shard_map.423 = (bf16[8,128,8704]{2,1,0:T(8,128)(2,1)}, bf16[8,512,1024]{2,1,0:T(8,128)(2,1)}, bf16[8,64,5056]{2,1,0:T(8,128)(2,1)}, bf16[8,256,512]{2,1,0:T(8,...) custom-call(f32[768,768]{1,0:T(8,128)} %pixels_ref.1, ...), custom_call_target="tpu_custom_call" | custom-call | flops 5637144576 | bytes 209715200 | tf_op jit(solution)/shard_map/pallas_call | solution.py:1419
  133.8 72.6 %shard_map.424 = (bf16[8,14,64,512]{3,2,1,0:T(8,128)(2,1)}, f32[192,512]{1,0:T(8,128)}, f32[8,1024]{1,0:T(8,128)}) custom-call(f32[768,512]{1,0:T(8,128)} %get-tuple-element.76.pos_ref, f32[192,512]{1,0:T(8,128)} %get-tuple-element.77.seen_ref, f32[8,768]{1,0:T(8,128)} %get-tuple-element.78.row_ref, f32[768,8]{1,0:T(8,128)} %get-tuple-element.79.column_ref, ...), custom_call_target="tpu_custom_call" | custom-call | flops 40000000000 | bytes 41943040 | tf_op jit(solution)/shard_map/pallas_call | solution.py:1761
  206.4 179.2 %shard_map.425 = (bf16[96,1024]{1,0:T(8,128)(2,1)}, bf16[128,8704]{1,0:T(8,128)(2,1)}, bf16[512,1024]{1,0:T(8,128)(2,1)}, bf16[64,5120]{1,0:T(8,128)(2,1)}, bf16[256,512]{1,0:T(8,128)(2,1)}, /*index=5*/f32[8,1024]{1,0:T(8,128)}) custom-call(f32[192,512]{1,0:T(8,128)} %get-tuple-element.84.dy_ref, f32[768,8]{1,0:T(8,128)} %get-tuple-element.79.column_ref, ...), custom_call_target="tpu_custom_call" | custom-call | flops 30000001024 | bytes 314572800 | tf_op jit(solution)/shard_map/pallas_call | solution.py:813
  385.6 0.0 copy-start
  385.6 0.0 copy-start.1
  385.6 0.0 copy-start.2
  385.7 0.0 copy-start.3
  385.7 19.6 %shard_map.426 = (f32[96,1024]{1,0:T(8,128)}, f32[96,1024]{1,0:T(8,128)}, f32[96,1024]{1,0:T(8,128)}, bf16[96,1024]{1,0:T(8,128)(2,1)}, f32[128,8704]{1,0:T(8,12...) custom-call(bf16[96,1024]{1,0:T(8,128)(2,1)} %get-tuple-element.101., ...), custom_call_target="tpu_custom_call" | custom-call | flops 26296320 | bytes 61358080 | tf_op jit(solution)/shard_map/pallas_call | solution.py:1872
  405.3 0.0 copy-done
  405.3 0.0 copy-done.1
  405.4 0.6 multiply_add_fusion
  406.0 0.5 slice.18
  406.5 1.2 slice.19
  (10 shorter events, 0.1 us)
Async XLA Ops:
  0.7 5.3 %copy-start.4 = (s32[2]{0:T(128)S(1)}, s32[2]{0:T(128)}, u32[]{:S(2)}) copy-start(s32[2]{0:T(128)} %param.28) | copy-start | bytes 28
  385.6 19.7 %copy-start = (f32[8,1024]{1,0:T(8,128)S(1)}, f32[8,1024]{1,0:T(8,128)}, u32[]{:S(2)}) copy-start(f32[8,1024]{1,0:T(8,128)} %get-tuple-element.126) | copy-start | bytes 98308
  385.6 19.7 %copy-start.1 = (f32[5120]{0:T(1024)S(1)}, f32[5120]{0:T(1024)}, u32[]{:S(2)}) copy-start(f32[5120]{0:T(1024)} %param.35) | copy-start | bytes 61444
  385.6 19.7 %copy-start.2 = (f32[5120]{0:T(1024)S(1)}, f32[5120]{0:T(1024)}, u32[]{:S(2)}) copy-start(f32[5120]{0:T(1024)} %param.47) | copy-start | bytes 61444
  385.7 19.7 %copy-start.3 = (f32[5120]{0:T(1024)S(1)}, f32[5120]{0:T(1024)}, u32[]{:S(2)}) copy-start(f32[5120]{0:T(1024)} %param.41) | copy-start | bytes 61444

commit v9 on v8

--- a/solution.py
+++ b/solution.py
@@ -210,7 +210,7 @@
 HALF = UNIT // 2
 ROWS = 128
 HALF_ROWS = ROWS // 2
-LAGS = (1, 2, 3, 4, 6)
+LAGS = (1, 3, 4, 6, 9)
 
 
 def put(source, target, send, recv, device):
@@ -235,6 +235,7 @@
     vectors_ref,
     bias_ref,
     qkv_ref,
+    ready_ref,
     dec_ref,
     end_ref,
     middle_ref,
@@ -255,7 +256,6 @@
         yp,
         do,
         dp,
-        products,
         a_out,
         a_in,
         b_out,
@@ -264,6 +264,7 @@
         z_out,
         z_one,
         z_two,
+        z_ready,
         v_in,
         v_out,
         wide_buf,
@@ -293,7 +294,7 @@
         v_recv,
         store_sem,
     ) = refs
-    count = dec_units + len(units)
+    count, extra = dec_units + len(units), z_ready.shape[0]
     z, f = lax.axis_index("dp"), lax.axis_index("fsdp")
     core, place = f % 2, f // 2
     x, y = place % 2, place // 2
@@ -388,20 +389,23 @@
 
     first, second = pl.ds(0, HALF), pl.ds(HALF, HALF)
 
-    def part(u, owner, columns, k):
+    def ready_part(n, owners, columns):
+        parts = [do[n, o, :, columns].astype(F32) + dp[n, o, :, columns].astype(F32) for o in owners]
+        return parts[0] if len(parts) == 1 else jnp.concatenate(parts, 0)
+
+    def formed_part(e, owners, columns):
+        b, r = block_of(e), right_of(e)
+        mine, other = [jnp.concatenate([ref[b, o] for o in owners], 0) for ref in (xo, xp)]
+        return matmul(mine, yo[r, :, columns]) + matmul(other, yp[r, :, columns])
+
+    def on_unit(u, stage):
         @pl.when(u < dec_units)
         def _():
-            n = jnp.minimum(u, dec_units - 1)
-            products[k] = do[n, owner, :, columns].astype(F32) + dp[n, owner, :, columns].astype(F32)
+            stage(partial(ready_part, jnp.minimum(u, dec_units - 1)))
 
         @pl.when(u >= dec_units)
         def _():
-            e = jnp.maximum(u - dec_units, 0)
-            b, r = block_of(e), right_of(e)
-            total = matmul(xo[b, owner], yo[r, :, columns])
-            products[k] = total + matmul(xp[b, owner], yp[r, :, columns])
-
-        return products[k]
+            stage(partial(formed_part, jnp.maximum(u - dec_units, 0)))
 
     def copy_a(u, side):
         slot = u % a_out.shape[0]
@@ -433,6 +437,14 @@
 
     def copy_out(u):
         return put(z_one.at[u], z_one.at[u], z_send.at[u, 1], z_recv.at[u, 0], outward)
+
+    def ready_in(n):
+        u = count + n
+        return put(z_ready.at[n], z_one.at[u], z_send.at[u, 0], z_recv.at[u, 0], inward)
+
+    def ready_across(n):
+        u = count + n
+        return put(z_ready.at[n], z_two.at[u], z_send.at[u, 0], z_recv.at[u, 1], across)
 
     def copy_v(step, device):
         return put(v_out.at[step], v_in.at[step], v_send.at[step], v_recv.at[step], device)
@@ -595,12 +607,15 @@
                     copy_a(u - a_out.shape[0], side).wait_send()
 
             slot = u % a_out.shape[0]
-            a_out[slot, 0, 0] = part(u, at_x, first, 0).astype(BF)
-            a_out[slot, 0, 1] = part(u, at_far, first, 1).astype(BF)
-            copy_a(u, 0).start()
-            a_out[slot, 1, 0] = part(u, at_y, second, 2).astype(BF)
-            a_out[slot, 1, 1] = part(u, at_far, second, 3).astype(BF)
-            copy_a(u, 1).start()
+
+            def send(part):
+                for side, (near, columns) in enumerate(((at_x, first), (at_y, second))):
+                    both = part((near, at_far), columns).astype(BF)
+                    a_out[slot, side] = both.reshape(2, ROWS, HALF)
+
+            on_unit(u, send)
+            for side in range(2):
+                copy_a(u, side).start()
 
         u1, when = stage(LAGS[0])
 
@@ -614,12 +629,17 @@
                 for side in range(2):
                     copy_b(u - b_out.shape[0], side).wait_send()
 
-            copy_a(u, 0).wait_recv()
-            b_out[slot, 0] = (part(u, at_y, first, 0) + a_in[u, 0, 1].astype(F32)).astype(BF)
-            copy_b(u, 0).start()
-            copy_a(u, 1).wait_recv()
-            b_out[slot, 1] = (part(u, at_x, second, 1) + a_in[u, 1, 1].astype(F32)).astype(BF)
-            copy_b(u, 1).start()
+            for side in range(2):
+                copy_a(u, side).wait_recv()
+
+            def send(part):
+                for side, (near, columns) in enumerate(((at_y, first), (at_x, second))):
+                    total = part((near,), columns) + a_in[u, side, 1].astype(F32)
+                    b_out[slot, side] = total.astype(BF)
+
+            on_unit(u, send)
+            for side in range(2):
+                copy_b(u, side).start()
 
         u2, when = stage(LAGS[1])
 
@@ -628,9 +648,14 @@
             u = u2
             copy_b(u, 0).wait_recv()
             copy_b(u, 1).wait_recv()
-            for side, columns in enumerate((first, second)):
-                total = part(u, place, columns, side) + a_in[u, side, 0].astype(F32)
-                sums[u % 4, :, columns] = total + b_in[u, side].astype(F32)
+
+            def keep(part):
+                whole = part((place,), slice(None))
+                for side, columns in enumerate((slice(0, HALF), slice(HALF, UNIT))):
+                    total = whole[:, columns] + a_in[u, side, 0].astype(F32)
+                    sums[u % 4, :, columns] = total + b_in[u, side].astype(F32)
+
+            on_unit(u, keep)
 
             @pl.when(outer)
             def _():
@@ -669,6 +694,32 @@
         @when
         def _():
             copy_out(u5).wait_recv()
+
+        ends = [lag - LAGS[1] for lag in LAGS[2:]]
+
+        @pl.when((i < extra) & outer)
+        def _():
+            z_ready[i] = ready_ref[i].astype(BF)
+            ready_in(i).start()
+
+        @pl.when((i >= ends[0]) & (i < extra + ends[0]) & inner)
+        def _():
+            n = i - ends[0]
+            ready_in(n).wait_recv()
+            z_ready[n] = (ready_ref[n] + z_one[count + n].astype(F32)).astype(BF)
+            ready_across(n).start()
+
+        @pl.when((i >= ends[1]) & (i < extra + ends[1]) & inner)
+        def _():
+            n = i - ends[1]
+            ready_across(n).wait_recv()
+            total = z_ready[n].astype(F32) + z_two[count + n].astype(F32)
+            z_one[count + n] = total.astype(BF)
+            copy_out(count + n).start()
+
+        @pl.when((i >= ends[2]) & (i < extra + ends[2]) & outer)
+        def _():
+            copy_out(count + i - ends[2]).wait_recv()
 
         pl.when(i == 0)(back_link)
 
@@ -759,6 +810,8 @@
         copy_v(3, inward).wait_send()
         for u in range(count - z_slots, count):
             copy_in(u).wait_send()
+        for n in range(extra):
+            ready_in(n).wait_send()
 
     @pl.when(inner)
     def _():
@@ -766,25 +819,23 @@
         copy_v(5, outward).wait_send()
         for u in range(count - z_slots, count):
             copy_across(u).wait_send()
+        for n in range(extra):
+            ready_across(n).wait_send()
 
         def drain(u, _):
             copy_out(u).wait_send()
             return 0
 
-        lax.fori_loop(0, count, drain, 0)
-
-
-def encoder_back(dy, by_column, vec, vectors, bias, qkv, dec, states, wide, down, lefts):
+        lax.fori_loop(0, count + extra, drain, 0)
+
+
+def encoder_back(dy, by_column, vec, vectors, bias, qkv, ready, dec, states, wide, down, lefts):
     owners = lax.axis_size("fsdp")
     own = PD // owners
-    dec_units = dec.shape[1] * dec.shape[2] // ROWS
+    dec_units = LATE // 2
     dec = dec.reshape(4, 2, dec_units, ROWS, UNIT)
     half = ROWS // 2
     blocks, units, spots = [], [], []
-    for n in range(2 * dec_units):
-        place = (4, n * half, half, 0) if n < DFF // DD else (3, 0, half, (n - DFF // DD) * UNIT)
-        spots.append((n // 2, n % 2 * half, *place))
-
     def add(left, sub, right, out, row, rows, column, columns):
         blocks.append((left, sub))
         for n in range(columns // UNIT):
@@ -805,6 +856,15 @@
     add(5, 0, right, 0, 0, own, 0, D)
     right += D // UNIT
     count = dec_units + len(units)
+    tall = DFF // DD
+    for n in range(EARLY + LATE):
+        if tall <= n < tall + LATE:
+            unit = (n - tall) // 2
+        else:
+            unit = count + (n if n < tall else n - LATE) // 2
+        place = (4, n * half, half, 0) if n < tall else (3, 0, half, (n - tall) * UNIT)
+        spots.append((unit, n % 2 * half, *place))
+    full = count + ready.shape[0]
     shapes = ((own, D), (ROWS, 4 * D + FF + DD), (FF // owners, D), (half, 10 * UNIT), (DFF // owners, DD))
     lefts = [a.reshape(4, 2, -1, VIS) for a in lefts]
     slots = 3
@@ -814,7 +874,7 @@
         partial(back_kernel, dec_units, tuple(blocks), tuple(units), tuple(spots)),
         out_shape=tuple(jax.ShapeDtypeStruct(shape, BF) for shape in shapes)
         + (jax.ShapeDtypeStruct(vec.shape, F32),),
-        in_specs=[vmem] * 6 + [anywhere] * (7 + len(lefts)),
+        in_specs=[vmem] * 7 + [anywhere] * (7 + len(lefts)),
         out_specs=(anywhere,) * len(shapes) + (vmem,),
         scratch_shapes=[
             pltpu.VMEM((len(blocks), 4, ROWS, VIS), BF),
@@ -823,15 +883,15 @@
             pltpu.VMEM((right, VIS, UNIT), BF),
             pltpu.VMEM((dec_units, 4, ROWS, UNIT), BF),
             pltpu.VMEM((dec_units, 4, ROWS, UNIT), BF),
-            pltpu.VMEM((4, ROWS, HALF), F32),
             pltpu.VMEM((slots, 2, 2, ROWS, HALF), BF),
             pltpu.VMEM((count, 2, 2, ROWS, HALF), BF),
             pltpu.VMEM((slots, 2, ROWS, HALF), BF),
             pltpu.VMEM((count, 2, ROWS, HALF), BF),
             pltpu.VMEM((4, ROWS, UNIT), F32),
             pltpu.VMEM((6, ROWS, UNIT), BF),
-            pltpu.VMEM((count, ROWS, UNIT), BF),
-            pltpu.VMEM((count, ROWS, UNIT), BF),
+            pltpu.VMEM((full, ROWS, UNIT), BF),
+            pltpu.VMEM((full, ROWS, UNIT), BF),
+            pltpu.VMEM(ready.shape, BF),
             pltpu.VMEM((6, *vec.shape), F32),
             pltpu.VMEM((6, *vec.shape), F32),
             pltpu.VMEM((3, D, UNIT), BF),
@@ -855,11 +915,11 @@
             dma((count, 2)),
             dma((slots, 2)),
             dma((count, 2)),
-            dma((count, 2)),
-            dma((count, 2)),
+            dma((full, 2)),
+            dma((full, 2)),
             dma((6,)),
             dma((6,)),
-            dma((count + dec_units,)),
+            dma((len(spots),)),
         ],
         compiler_params=pltpu.CompilerParams(
             collective_id=0, has_side_effects=True, vmem_limit_bytes=61 * 2**20
@@ -867,7 +927,7 @@
         cost_estimate=pl.CostEstimate(
             flops=30 * 10**9, bytes_accessed=300 * 2**20, transcendentals=0
         ),
-    )(dy, by_column, vec, vectors, bias, qkv, dec, *states, wide, down, *lefts)
+    )(dy, by_column, vec, vectors, bias, qkv, ready, dec, *states, wide, down, *lefts)
 
 
 def encoder_pieces(shapes):
@@ -1490,8 +1550,13 @@
     return matmul(high, weight) + matmul(mid, weight) + matmul(low, weight)
 
 
+EARLY = DFF // DD + DFF // UNIT + HEADP // UNIT
+LATE = 4
+
+
 def decoder_kernel(
     owners,
+    fast,
     pos_ref,
     seen_ref,
     row_ref,
@@ -1501,9 +1566,11 @@
     vectors_ref,
     wide_ref,
     down_ref,
-    grads_ref,
+    late_ref,
     dy_ref,
     vec_out,
+    sums_ref,
+    early_ref,
     y_ref,
     a_ref,
     q_ref,
@@ -1530,7 +1597,83 @@
     pool_ref,
     spread_ref,
     vec_ref,
+    *links,
 ):
+    if fast:
+        (dp, a_out, a_in, b_out, b_in, swap_sem, a_send, a_recv, b_send, b_recv) = links
+        ready = EARLY // 2
+        z, f = lax.axis_index("dp"), lax.axis_index("fsdp")
+        core, place = f % 2, f // 2
+        x, y = place % 2, place // 2
+        partner = (z, f + 1 - 2 * core)
+        x_side, y_side = (z, f + 2 - 4 * x), (z, f + 4 - 8 * y)
+        at_x, at_y, at_far = place + 1 - 2 * x, place + 2 - 4 * y, 3 - place
+        first, second = pl.ds(0, HALF), pl.ds(HALF, HALF)
+        barrier = pltpu.get_barrier_semaphore()
+        for device in (partner, x_side, y_side):
+            pl.semaphore_signal(barrier, inc=1, device_id=device, device_id_type=MESH)
+
+        def swap(u):
+            return put(
+                early_ref.at[:, 1 - core, pl.ds(2 * u, 2)],
+                dp.at[u],
+                swap_sem.at[u, 0],
+                swap_sem.at[u, 1],
+                partner,
+            )
+
+        def share(u, owner, columns):
+            own = early_ref[owner, core, pl.ds(2 * u, 2), :, columns].astype(F32)
+            both = own + dp[u, owner, :, :, columns].astype(F32)
+            return both.reshape(ROWS, HALF)
+
+        def copy_a(u, side):
+            return put(
+                a_out.at[u, side],
+                a_in.at[u, side],
+                a_send.at[u, side],
+                a_recv.at[u, side],
+                (x_side, y_side)[side],
+            )
+
+        def copy_b(u, side):
+            return put(
+                b_out.at[u, side],
+                b_in.at[u, side],
+                b_send.at[u, side],
+                b_recv.at[u, side],
+                (y_side, x_side)[side],
+            )
+
+        def exchange(c):
+            @pl.when(c < ready)
+            def _():
+                swap(c).wait()
+                a_out[c, 0, 0] = share(c, at_x, first).astype(BF)
+                a_out[c, 0, 1] = share(c, at_far, first).astype(BF)
+                copy_a(c, 0).start()
+                a_out[c, 1, 0] = share(c, at_y, second).astype(BF)
+                a_out[c, 1, 1] = share(c, at_far, second).astype(BF)
+                copy_a(c, 1).start()
+
+            @pl.when((c >= 2) & (c < ready + 2))
+            def _():
+                u = c - 2
+                copy_a(u, 0).wait_recv()
+                b_out[u, 0] = (share(u, at_y, first) + a_in[u, 0, 1].astype(F32)).astype(BF)
+                copy_b(u, 0).start()
+                copy_a(u, 1).wait_recv()
+                b_out[u, 1] = (share(u, at_x, second) + a_in[u, 1, 1].astype(F32)).astype(BF)
+                copy_b(u, 1).start()
+
+            @pl.when((c >= 4) & (c < ready + 4))
+            def _():
+                u = c - 4
+                for side, columns in enumerate((first, second)):
+                    copy_b(u, side).wait_recv()
+                    total = share(u, place, columns) + a_in[u, side, 0].astype(F32)
+                    sums_ref[u, :, columns] = total + b_in[u, side].astype(F32)
+
     size = DD // DHEADS
     per = LANES // size
     factor = size ** (-0.5)
@@ -1556,6 +1699,8 @@
             (VIS, HID),
             start - VIS,
         )
+    if not fast:
+        sums_ref[...] = jnp.zeros_like(sums_ref)
     vec_ref[...] = jnp.zeros_like(vec_ref)
     loss_ref[...] = jnp.zeros_like(loss_ref)
     head_ref[...] = jnp.zeros_like(head_ref)
@@ -1658,22 +1803,29 @@
 
     rows = DD // owners
 
-    def store(block, grad):
-        grads_ref[:, block] = grad.astype(BF).reshape(owners, rows, UNIT)
+    def store(ref, block, grad):
+        ref[:, :, block] = grad.astype(BF).reshape(owners // 2, 2, rows, UNIT)
 
     parts = DFF // DD
     down_grad = left_t(hidden_ref[...], dbranch_ref[...]).astype(BF)
-    down_grad = down_grad.reshape(owners, parts, rows, UNIT)
+    down_grad = down_grad.reshape(owners // 2, 2, parts, rows, UNIT)
     for part in range(parts):
-        grads_ref[:, part] = down_grad[:, part]
+        early_ref[:, :, part] = down_grad[:, :, part]
+    for n in range(DFF // UNIT):
+        columns = slice(n * UNIT, (n + 1) * UNIT)
+        store(early_ref, parts + n, left_t(b_ref[...], dbefore_ref[:, columns]))
+    for n in range(HEADP // UNIT):
+        columns = slice(n * UNIT, (n + 1) * UNIT)
+        store(early_ref, parts + DFF // UNIT + n, left_t(z_ref[...], dpred_ref[:, columns]))
+    if fast:
+        pl.semaphore_wait(barrier, 3)
+        for u in range(ready):
+            swap(u).start()
     store(
-        parts + 3,
+        late_ref,
+        3,
         jnp.concatenate([matmul(mixed_t[g], dattn_ref[...]) for g in range(DD // LANES)], 0),
     )
-    for n in range(DFF // UNIT):
-        store(parts + 4 + n, left_t(b_ref[...], dbefore_ref[:, n * UNIT : (n + 1) * UNIT]))
-    for n in range(HEADP // UNIT):
-        store(parts + 8 + n, left_t(z_ref[...], dpred_ref[:, n * UNIT : (n + 1) * UNIT]))
 
     def attend_back_group(g, _):
         lanes = pl.ds(pl.multiple_of(g * LANES, LANES), LANES)
@@ -1683,6 +1835,8 @@
         dvalues = jnp.zeros((TOK_DEV, LANES), F32)
         dquery = []
         for j in range(per):
+            if fast and j % 2 == 0:
+                exchange(2 * g + j // 2)
             scores = right_t(keys, only(query, lane_head, j)) * factor + bias_ref[...]
             probs = jnp.exp(scores - lse_ref[g, j : j + 1, :])
             dvalues = jnp.where(key_head == j, matmul(probs.astype(BF), dout), dvalues)
@@ -1698,9 +1852,11 @@
 
     lax.fori_loop(0, DD // LANES, attend_back_group, 0)
 
-    store(parts, left_t(a_ref[VIS:, :], dq_ref[...]))
-    store(parts + 1, left_t(a_ref[...], dk_ref[...]))
-    store(parts + 2, left_t(a_ref[...], dv_ref[...]))
+    store(late_ref, 0, left_t(a_ref[VIS:, :], dq_ref[...]))
+    if fast:
+        exchange(2 * (DD // LANES))
+    store(late_ref, 1, left_t(a_ref[...], dk_ref[...]))
+    store(late_ref, 2, left_t(a_ref[...], dv_ref[...]))
 
     def start_rows(rows, da):
         unit, rate = normalize(y_ref[rows, :])
@@ -1725,9 +1881,14 @@
     for n in range(4):
         vec_out[3 + n // 2 : 4 + n // 2, n % 2 * DD : (n % 2 + 1) * DD] = vec_ref[n : n + 1, :]
     vec_out[5:6, :] = jnp.broadcast_to(jnp.sum(loss_ref[...], 1, keepdims=True), (1, D))
-
-
-def decoder_step(pos, seen, by_row, by_column, picked, stats, vectors, wide, down):
+    if fast:
+        for u in range(ready):
+            for side in range(2):
+                copy_a(u, side).wait_send()
+                copy_b(u, side).wait_send()
+
+
+def decoder_step(fast, pos, seen, by_row, by_column, picked, stats, vectors, wide, down):
     owners = lax.axis_size("fsdp")
     scratch = [
         ((TOK_DEV, DD), F32),
@@ -1758,17 +1919,42 @@
         ((8, DD), F32),
     ]
     vmem = pl.BlockSpec(memory_space=pltpu.VMEM)
-    grads, dy, vec = pl.pallas_call(
-        partial(decoder_kernel, owners),
-        out_shape=(
-            jax.ShapeDtypeStruct((owners, DFF // DD + 10, DD // owners, UNIT), BF),
-            jax.ShapeDtypeStruct((VIS, DD), F32),
-            jax.ShapeDtypeStruct((8, D), F32),
-        ),
+    early, late = [
+        jax.ShapeDtypeStruct((owners // 2, 2, blocks, DD // owners, UNIT), BF)
+        for blocks in (EARLY, LATE)
+    ]
+    ready = EARLY // 2
+    dma = pltpu.SemaphoreType.DMA
+    scratch = [pltpu.VMEM(*entry) for entry in scratch]
+    params = {}
+    if fast:
+        sums = jax.ShapeDtypeStruct((ready, ROWS, UNIT), F32)
+        scratch = [pltpu.VMEM(early.shape, BF)] + scratch
+        scratch += [
+            pltpu.VMEM((ready, owners // 2, 2, DD // owners, UNIT), BF),
+            pltpu.VMEM((ready, 2, 2, ROWS, HALF), BF),
+            pltpu.VMEM((ready, 2, 2, ROWS, HALF), BF),
+            pltpu.VMEM((ready, 2, ROWS, HALF), BF),
+            pltpu.VMEM((ready, 2, ROWS, HALF), BF),
+            *[dma((ready, 2))] * 5,
+        ]
+        params = {"collective_id": 2, "has_side_effects": True}
+    else:
+        sums = jax.ShapeDtypeStruct((8, LANES), F32)
+    outs = (
+        late,
+        jax.ShapeDtypeStruct((VIS, DD), F32),
+        jax.ShapeDtypeStruct((8, D), F32),
+        sums,
+        *([] if fast else [early]),
+    )
+    return pl.pallas_call(
+        partial(decoder_kernel, owners, fast),
+        out_shape=outs,
         in_specs=[vmem] * 9,
-        out_specs=(vmem,) * 3,
-        scratch_shapes=[pltpu.VMEM(*entry) for entry in scratch],
-        compiler_params=pltpu.CompilerParams(vmem_limit_bytes=60 * 2**20),
+        out_specs=(vmem,) * len(outs),
+        scratch_shapes=scratch,
+        compiler_params=pltpu.CompilerParams(vmem_limit_bytes=60 * 2**20, **params),
         cost_estimate=pl.CostEstimate(
             flops=40 * 10**9, bytes_accessed=40 * 2**20, transcendentals=2 * 10**7
         ),
@@ -1783,7 +1969,6 @@
         wide,
         down,
     )
-    return grads, dy, vec
 
 
 def block_forward(h, weights, gains, bias, heads, skip):
@@ -1984,7 +2169,8 @@
         h_end, enc_saved = block_forward(h_start, enc_weights, gains_enc, bias_enc, HEADS, 0)
         encoded = layer_norm(h_end, gain_enc_out).astype(BF)
         seen_out = matmul(encoded, w_link)
-    dec_grads, dy_seen, vec = decoder_step(
+    late, dy_seen, vec, ready, *early = decoder_step(
+        fast,
         pos_dec,
         seen_out,
         by_row,
@@ -2004,7 +2190,8 @@
             vector_row,
             bias_enc,
             qkv,
-            dec_grads,
+            ready,
+            late,
             (h_end, middle, h_start, slope),
             w_enc,
             w_enc_down,
@@ -2031,6 +2218,10 @@
             ),
             "dp",
         )
+        parts = DFF // DD
+        early = early[0]
+        dec_grads = jnp.concatenate([early[:, :, :parts], late, early[:, :, parts:]], 2)
+        dec_grads = dec_grads.reshape(-1, *dec_grads.shape[2:])
         dec_sum = lax.psum(reduce_rows(dec_grads), "dp")[0]
         rows, parts = dec_sum.shape[1], DFF // DD
         dec_parts = (

time: 416 us -> 400 us (0.962)
  Pallas kernels: 399 us -> 383 us
    pallas_call x1, Pallas kernels: 179 us -> 158 us  [encoder_back(): pl.pallas_call(partial(back_kernel, dec_units, tuple(blocks), tuple(units...]
    pallas_call x1, Pallas kernels: 72.6 us -> 78.4 us  [decoder_step(): pl.pallas_call(partial(decoder_kernel, owners, fast), out_shape=outs, in_...]
where the time goes in v9:
time: 400 us; the launch traced here: 393 us
  Pallas kernels  383 us (96%)
  local copies, waits for them, and re-layouts  6.17 us (2%)
    pallas_call x1, Pallas kernels, encoder_back(): pl.pallas_call(partial(back_kernel, dec_units, tuple(blocks), tuple(units...  158 us
    pallas_call x1, Pallas kernels, encoder_forward(): pl.pallas_call(encoder_kernel, out_shape=(*full, *local), in_specs=[vmem]...  127 us
    pallas_call x1, Pallas kernels, decoder_step(): pl.pallas_call(partial(decoder_kernel, owners, fast), out_shape=outs, in_...  78.4 us
    pallas_call x1, Pallas kernels, advance_all(): pl.pallas_call(partial(advance_kernel, rate), grid=(steps,), out_shape=[o...  19.7 us

profile of v9, /device:TPU:0, one launch (start us, length us, event | category | flops | bytes accessed | tf_op | source)
XLA Modules:
  0.0 392.6 jit_solution(4243564651341341540)
XLA Ops:
  0.7 0.0 copy-start.4
  0.7 0.8 slice_bitcast_fusion
  1.5 0.7 add_select_fusion
  2.2 0.7 stack.12
  2.8 0.7 stack.26
  3.6 0.2 copy.56
  3.8 0.8 fusion.1
  4.6 0.7 copy.57.row_ref
  5.3 0.6 stack.30.omega_ref
  6.0 0.0 copy-done.4
  6.0 0.7 pad.16.scale_ref
  6.7 127.2 %shard_map.423 = (bf16[8,128,8704]{2,1,0:T(8,128)(2,1)}, bf16[8,512,1024]{2,1,0:T(8,128)(2,1)}, bf16[8,64,5056]{2,1,0:T(8,128)(2,1)}, bf16[8,256,512]{2,1,0:T(8,...) custom-call(f32[768,768]{1,0:T(8,128)} %pixels_ref.1, ...), custom_call_target="tpu_custom_call" | custom-call | flops 5637144576 | bytes 209715200 | tf_op jit(solution)/shard_map/pallas_call | solution.py:1479
  133.9 78.4 %shard_map.424 = (bf16[4,2,4,64,512]{4,3,2,1,0:T(8,128)(2,1)}, f32[192,512]{1,0:T(8,128)}, f32[8,1024]{1,0:T(8,128)}, f32[5,128,512]{2,1,0:T(8,128)}) custom-call(f32[768,512]{1,0:T(8,128)} %get-tuple-element.77.pos_ref, f32[192,512]{1,0:T(8,128)} %get-tuple-element.78.seen_ref, f32[8,768]{1,0:T(8,128)} %get-tuple-element.79.row_ref, ...), custom_call_target="tpu_custom_call" | custom-call | flops 40000000000 | bytes 41943040 | tf_op jit(solution)/shard_map/pallas_call | solution.py:1951
  212.2 157.9 %shard_map.425 = (bf16[96,1024]{1,0:T(8,128)(2,1)}, bf16[128,8704]{1,0:T(8,128)(2,1)}, bf16[512,1024]{1,0:T(8,128)(2,1)}, bf16[64,5120]{1,0:T(8,128)(2,1)}, bf16[256,512]{1,0:T(8,128)(2,1)}, /*index=5*/f32[8,1024]{1,0:T(8,128)}) custom-call(f32[192,512]{1,0:T(8,128)} %get-tuple-element.85.dy_ref, f32[768,8]{1,0:T(8,128)} %get-tuple-element.80.column_ref, ...), custom_call_target="tpu_custom_call" | custom-call | flops 30000001024 | bytes 314572800 | tf_op jit(solution)/shard_map/pallas_call | solution.py:873
  370.1 0.0 copy-start
  370.1 0.0 copy-start.1
  370.1 0.0 copy-start.2
  370.1 0.0 copy-start.3
  370.2 19.7 %shard_map.426 = (f32[96,1024]{1,0:T(8,128)}, f32[96,1024]{1,0:T(8,128)}, f32[96,1024]{1,0:T(8,128)}, bf16[96,1024]{1,0:T(8,128)(2,1)}, f32[128,8704]{1,0:T(8,12...) custom-call(bf16[96,1024]{1,0:T(8,128)(2,1)} %get-tuple-element.103., ...), custom_call_target="tpu_custom_call" | custom-call | flops 26296320 | bytes 61358080 | tf_op jit(solution)/shard_map/pallas_call | solution.py:2057
  389.8 0.0 copy-done
  389.8 0.0 copy-done.1
  389.9 0.6 multiply_add_fusion
  390.5 0.5 slice.18
  391.0 1.2 slice.19
  (10 shorter events, 0.1 us)
Async XLA Ops:
  0.7 5.3 %copy-start.4 = (s32[2]{0:T(128)S(1)}, s32[2]{0:T(128)}, u32[]{:S(2)}) copy-start(s32[2]{0:T(128)} %param.28) | copy-start | bytes 28
  370.1 19.7 %copy-start = (f32[8,1024]{1,0:T(8,128)S(1)}, f32[8,1024]{1,0:T(8,128)}, u32[]{:S(2)}) copy-start(f32[8,1024]{1,0:T(8,128)} %get-tuple-element.128) | copy-start | bytes 98308
  370.1 19.7 %copy-start.1 = (f32[5120]{0:T(1024)S(1)}, f32[5120]{0:T(1024)}, u32[]{:S(2)}) copy-start(f32[5120]{0:T(1024)} %param.35) | copy-start | bytes 61444
  370.1 19.7 %copy-start.2 = (f32[5120]{0:T(1024)S(1)}, f32[5120]{0:T(1024)}, u32[]{:S(2)}) copy-start(f32[5120]{0:T(1024)} %param.47) | copy-start | bytes 61444
  370.1 19.7 %copy-start.3 = (f32[5120]{0:T(1024)S(1)}, f32[5120]{0:T(1024)}, u32[]{:S(2)}) copy-start(f32[5120]{0:T(1024)} %param.41) | copy-start | bytes 61444
